TPU v7x, 32 devices: a whole 2x2x4 slice. The times are simulated.
32 devices in a mesh: fsdp: 8 (over y, x, core), rep: 4 (over z).
Axes of the slice: x: 2, y: 2, z: 4, core: 2. Of those that a mesh axis runs over, the one named last changes fastest.
Arguments:
- history: bfloat16 [9, 4096, 2048], P(None, ('fsdp', 'rep')), may hold values from -6 to 6
- mix_in: float32 [4096, 36], P(('fsdp', 'rep')), may hold values from -3 to 3
- doc_ids: int32 [32, 128], P(('fsdp', 'rep')), may hold values from 0 to 3, never falling along the last dimension, each value on 1 to 64 neighbouring positions
- doc_group: int32 [32, 4], P(('fsdp', 'rep')), may hold values from 0 to 21
- group_weight: float32 [22], replicated, may hold values from 0.3 to 3
- norm_gain: float32 [3, 2048], P(None, ('fsdp', 'rep')), may hold values from 0.1 to 1.9
- norm_bias: float32 [2, 2048], P(None, ('fsdp', 'rep')), may hold values from -1.75 to 1.75
- w_qkv: float32 [2048, 6144], P(('fsdp', 'rep')), may hold values from -0.125 to 0.125
- b_qkv: float32 [6144], P(('fsdp', 'rep')), may hold values from -1.75 to 1.75
- w_out: float32 [2048, 2048], P(('fsdp', 'rep')), may hold values from -0.75 to 0.75
- b_out: float32 [2048], P(('fsdp', 'rep')), may hold values from -1.75 to 1.75
- w_fc1: float32 [2048, 8192], P(('fsdp', 'rep')), may hold values from -0.125 to 0.125
- b_fc1: float32 [8192], P(('fsdp', 'rep')), may hold values from -1.75 to 1.75
- w_fc2: float32 [2048, 8192], P(('fsdp', 'rep')), may hold values from -0.0625 to 0.0625
- b_fc2: float32 [2048], P(('fsdp', 'rep')), may hold values from -1.75 to 1.75
- w_mix1: float32 [2048, 100], P(('fsdp', 'rep')), may hold values from -0.125 to 0.125
- b_mix1: float32 [100], replicated, may hold values from -3 to 3
- w_mix2: float32 [100, 40], replicated, may hold values from -0.625 to 0.625
- b_mix2: float32 [40], replicated, may hold values from -3 to 3
- cotangent: bfloat16 [4, 4096, 2048], P(None, ('fsdp', 'rep')), may hold values from -6 to 6
Outputs:
- next_streams: bfloat16 [4, 4096, 2048], P(None, ('fsdp', 'rep'))
- grad_history: float32 [9, 4096, 2048], P(None, ('fsdp', 'rep'))
- grad_mix_in: float32 [4096, 36], P(('fsdp', 'rep'))
- grad_norm_gain: float32 [3, 2048], P(None, ('fsdp', 'rep'))
- grad_norm_bias: float32 [2, 2048], P(None, ('fsdp', 'rep'))
- grad_w_qkv: float32 [2048, 6144], P(('fsdp', 'rep'))
- grad_b_qkv: float32 [6144], P(('fsdp', 'rep'))
- grad_w_out: float32 [2048, 2048], P(('fsdp', 'rep'))
- grad_b_out: float32 [2048], P(('fsdp', 'rep'))
- grad_w_fc1: float32 [2048, 8192], P(('fsdp', 'rep'))
- grad_b_fc1: float32 [8192], P(('fsdp', 'rep'))
- grad_w_fc2: float32 [2048, 8192], P(('fsdp', 'rep'))
- grad_b_fc2: float32 [2048], P(('fsdp', 'rep'))
- grad_w_mix1: float32 [2048, 100], P(('fsdp', 'rep'))
- grad_b_mix1: float32 [100], replicated
- grad_w_mix2: float32 [100, 40], replicated
- grad_b_mix2: float32 [40], replicated
Inputs may be any that keep to these rules, and one draw needn't show every extreme that they name: `doc_ids`: within a sequence document numbers never fall; each of the 4 documents has 1 to 64 tokens, and one has exactly that many.
All inputs are finite; a program needn't handle non-finite values.
Results may differ from a plain program's by a relative error of at most 0.015.
The roundings to bfloat16 on the way count: a program that leaves them out, or rounds other values in their place, can miss the bound.
Values may be sent and summed in bfloat16 or wider, within the bound.
No kernel may reach another device: no remote copies, remote signals or barrier semaphores. Data moves between devices by JAX's collectives and lax.ppermute only.
A program may use at most 384 MiB of HBM per device.

v0:
```python
import jax
import jax.numpy as jnp
from jax import lax
from jax.sharding import PartitionSpec as P

HEAD_DIM = 128
ROT = 32


NARROW = jnp.bfloat16
SINGLE = jnp.float32
NORM_EPSILON = 1e-05
RMS_EPSILON = 1e-06


def layer_norm(values, gain_row, shift_row):
    center = values - jnp.mean(values, -1, keepdims=True)
    spread = jnp.mean(center * center, -1, keepdims=True)
    return center * lax.rsqrt(spread + NORM_EPSILON) * gain_row + shift_row


def norm_streams(query_in, key_in, value_in, resid_in, gains, shifts):
    return (
        layer_norm(query_in, gains[0], shifts[0]),
        layer_norm(key_in, gains[0], shifts[0]),
        layer_norm(value_in, gains[0], shifts[0]),
        layer_norm(resid_in, gains[1], shifts[1]),
    )


def rms_norm(entry, gain_row):
    return entry * lax.rsqrt(jnp.mean(entry * entry, -1, keepdims=True) + RMS_EPSILON) * gain_row


def gelu_exact(values):
    return jax.nn.gelu(values, approximate=False)


def rotate(values, cosine, sine):
    halfway = ROT // 2
    former = values[..., :halfway]
    latter = values[..., halfway:ROT]
    return jnp.concatenate(
        [former * cosine - latter * sine, latter * cosine + former * sine, values[..., ROT:]], -1
    )


def times_transposed(left, right):
    return lax.dot_general(left, right, (((1,), (1,)), ((), ())), preferred_element_type=SINGLE)


def transposed_times(left, right):
    return lax.dot_general(left, right, (((0,), (0,)), ((), ())), preferred_element_type=SINGLE)


def blend(weights, sources):
    result = weights[:, 0:1] * sources[0]
    for index in range(1, len(sources)):
        result = result + weights[:, index : index + 1] * sources[index]
    return result


def on_device(
    history,
    mix_in,
    doc_ids,
    doc_group,
    group_weight,
    norm_gain,
    norm_bias,
    w_qkv,
    b_qkv,
    w_out,
    b_out,
    w_fc1,
    b_fc1,
    w_fc2,
    b_fc2,
    w_mix1,
    b_mix1,
    w_mix2,
    b_mix2,
    cotangent,
):
    entries = history.shape[0]
    length = history.shape[1]
    width = history.shape[2]
    stream_count = cotangent.shape[0]
    heads = width // HEAD_DIM
    attn_set = (
        lax.all_gather(w_qkv.astype(NARROW), ("fsdp", "rep"), axis=0, tiled=True),
        lax.all_gather(b_qkv.astype(NARROW), ("fsdp", "rep"), axis=0, tiled=True),
        lax.all_gather(w_out.astype(NARROW), ("fsdp", "rep"), axis=0, tiled=True),
        lax.all_gather(b_out.astype(NARROW), ("fsdp", "rep"), axis=0, tiled=True),
        lax.all_gather(norm_gain.astype(NARROW), ("fsdp", "rep"), axis=1, tiled=True),
        lax.all_gather(norm_bias.astype(NARROW), ("fsdp", "rep"), axis=1, tiled=True),
        lax.all_gather(w_mix1.astype(NARROW), ("fsdp", "rep"), axis=0, tiled=True),
    )
    mlp_set = (
        lax.all_gather(w_fc1.astype(NARROW), ("fsdp", "rep"), axis=0, tiled=True),
        lax.all_gather(b_fc1.astype(NARROW), ("fsdp", "rep"), axis=0, tiled=True),
        lax.all_gather(w_fc2.astype(NARROW), ("fsdp", "rep"), axis=0, tiled=True),
        lax.all_gather(b_fc2.astype(NARROW), ("fsdp", "rep"), axis=0, tiled=True),
    )
    qkv_full, qkv_bias, out_full, out_bias, gains_full, shifts_full, mix_first = attn_set
    first_full, first_bias, second_full, second_bias = mlp_set
    sources = [history[index].astype(SINGLE) for index in range(entries)]
    alpha = mix_in.reshape(length, stream_count, entries)
    stream_in = [blend(alpha[:, stream], sources) for stream in range(stream_count)]
    normed, norm_back = jax.vjp(
        norm_streams,
        stream_in[0],
        stream_in[1],
        stream_in[2],
        stream_in[3],
        gains_full[:2].astype(SINGLE),
        shifts_full.astype(SINGLE),
    )
    query_norm = normed[0].astype(NARROW)
    key_norm = normed[1].astype(NARROW)
    value_norm = normed[2].astype(NARROW)
    resid_norm = normed[3].astype(NARROW)
    query_lin = jnp.dot(query_norm, qkv_full[:, :width], preferred_element_type=SINGLE) + qkv_bias[
        :width
    ].astype(SINGLE)
    key_lin = jnp.dot(
        key_norm, qkv_full[:, width : 2 * width], preferred_element_type=SINGLE
    ) + qkv_bias[width : 2 * width].astype(SINGLE)
    value_lin = jnp.dot(
        value_norm, qkv_full[:, 2 * width :], preferred_element_type=SINGLE
    ) + qkv_bias[2 * width :].astype(SINGLE)
    position = jnp.arange(length).astype(SINGLE)
    frequency = 10000.0 ** (-jnp.arange(0, ROT, 2).astype(SINGLE) / ROT)
    angle = position[:, None] * frequency[None, :]
    cosine = jnp.cos(angle)[:, None, :]
    sine = jnp.sin(angle)[:, None, :]
    query_rot = rotate(query_lin.reshape(length, heads, HEAD_DIM), cosine, sine).astype(NARROW)
    key_rot = rotate(key_lin.reshape(length, heads, HEAD_DIM), cosine, sine).astype(NARROW)
    value_low = value_lin.reshape(length, heads, HEAD_DIM).astype(NARROW)
    scale = HEAD_DIM ** (-0.5)
    documents = doc_ids[0]
    place = jnp.arange(length)
    allowed = (place[None, :] <= place[:, None]) & (documents[None, :] == documents[:, None])

    def attention_scores():
        raw = jnp.einsum("qhd,khd->hqk", query_rot, key_rot, preferred_element_type=SINGLE) * scale
        return jnp.where(allowed[None], raw, -1e30)

    scores = attention_scores()
    largest = jnp.max(scores, -1, keepdims=True)
    summed = jnp.sum(jnp.exp(scores - largest), -1, keepdims=True)
    log_total = largest + jnp.log(summed)
    probs = jnp.exp(scores - log_total)
    mixed = jnp.einsum(
        "hqk,khd->qhd", probs.astype(NARROW), value_low, preferred_element_type=SINGLE
    )
    mixed_low = mixed.reshape(length, width).astype(NARROW)
    attn_branch = times_transposed(mixed_low, out_full) + out_bias.astype(SINGLE)
    hidden_pre = jnp.dot(resid_norm, first_full, preferred_element_type=SINGLE) + first_bias.astype(
        SINGLE
    )
    hidden_act, gelu_back = jax.vjp(gelu_exact, hidden_pre)
    hidden_low = hidden_act.astype(NARROW)
    mlp_branch = times_transposed(hidden_low, second_full) + second_bias.astype(SINGLE)
    new_entry = stream_in[3] + attn_branch + mlp_branch
    scaled, rms_back = jax.vjp(rms_norm, new_entry, gains_full[2].astype(SINGLE))
    scaled_low = scaled.astype(NARROW)
    mix_pre = jnp.dot(scaled_low, mix_first, preferred_element_type=SINGLE) + b_mix1
    mix_hidden, mix_back = jax.vjp(gelu_exact, mix_pre)
    mix_weights = (
        jnp.dot(mix_hidden, w_mix2, precision=lax.Precision.HIGHEST, preferred_element_type=SINGLE)
        + b_mix2
    )
    all_sources = sources + [new_entry]
    coef = mix_weights.reshape(length, stream_count, entries + 1)
    next_streams = jnp.stack(
        [blend(coef[:, stream], all_sources) for stream in range(stream_count)]
    ).astype(NARROW)
    attn_again = (
        lax.all_gather(w_qkv.astype(NARROW), ("fsdp", "rep"), axis=0, tiled=True),
        lax.all_gather(b_qkv.astype(NARROW), ("fsdp", "rep"), axis=0, tiled=True),
        lax.all_gather(w_out.astype(NARROW), ("fsdp", "rep"), axis=0, tiled=True),
        lax.all_gather(b_out.astype(NARROW), ("fsdp", "rep"), axis=0, tiled=True),
        lax.all_gather(norm_gain.astype(NARROW), ("fsdp", "rep"), axis=1, tiled=True),
        lax.all_gather(norm_bias.astype(NARROW), ("fsdp", "rep"), axis=1, tiled=True),
        lax.all_gather(w_mix1.astype(NARROW), ("fsdp", "rep"), axis=0, tiled=True),
    )
    mlp_again = (
        lax.all_gather(w_fc1.astype(NARROW), ("fsdp", "rep"), axis=0, tiled=True),
        lax.all_gather(b_fc1.astype(NARROW), ("fsdp", "rep"), axis=0, tiled=True),
        lax.all_gather(w_fc2.astype(NARROW), ("fsdp", "rep"), axis=0, tiled=True),
        lax.all_gather(b_fc2.astype(NARROW), ("fsdp", "rep"), axis=0, tiled=True),
    )
    qkv_back = attn_again[0]
    out_back = attn_again[2]
    mix_first_back = attn_again[6]
    first_back = mlp_again[0]
    second_back = mlp_again[2]
    doc_match = documents[:, None] == jnp.arange(doc_group.shape[1], dtype=jnp.int32)[None, :]
    token_group = jnp.sum(jnp.where(doc_match, doc_group[0][None, :], 0), axis=1)
    group_match = (
        token_group[:, None] == jnp.arange(group_weight.shape[0], dtype=jnp.int32)[None, :]
    )
    token_weight = jnp.sum(jnp.where(group_match, group_weight[None, :], 0.0), axis=1)
    grad_out = cotangent.astype(SINGLE) * token_weight[None, :, None]
    grad_list = [grad_out[stream] for stream in range(stream_count)]
    grad_sources = [blend(coef[:, :, index], grad_list) for index in range(entries + 1)]
    grad_coef = jnp.stack(
        [
            jnp.stack(
                [
                    jnp.sum(grad_list[stream] * all_sources[index], -1)
                    for index in range(entries + 1)
                ],
                -1,
            )
            for stream in range(stream_count)
        ],
        1,
    )
    grad_mix_weights = grad_coef.reshape(length, stream_count * (entries + 1))
    grad_w_mix2 = jnp.dot(
        mix_hidden.T,
        grad_mix_weights,
        precision=lax.Precision.HIGHEST,
        preferred_element_type=SINGLE,
    )
    grad_b_mix2 = jnp.sum(grad_mix_weights, 0)
    grad_mix_hidden = jnp.dot(
        grad_mix_weights, w_mix2.T, precision=lax.Precision.HIGHEST, preferred_element_type=SINGLE
    )
    (grad_mix_pre,) = mix_back(grad_mix_hidden)
    grad_b_mix1 = jnp.sum(grad_mix_pre, 0)
    grad_mix_low = grad_mix_pre.astype(NARROW)
    grad_w_mix1 = transposed_times(scaled_low, grad_mix_low)
    grad_scaled = times_transposed(grad_mix_low, mix_first_back)
    grad_entry_rms, grad_rms_gain = rms_back(grad_scaled)
    grad_entry = grad_sources[entries] + grad_entry_rms
    grad_branch_bias = jnp.sum(grad_entry, 0)
    grad_branch = grad_entry.astype(NARROW)
    grad_hidden = jnp.dot(grad_branch, second_back, preferred_element_type=SINGLE)
    (grad_hidden_pre,) = gelu_back(grad_hidden)
    grad_first_bias = jnp.sum(grad_hidden_pre, 0)
    grad_hidden_low = grad_hidden_pre.astype(NARROW)
    grad_resid_norm = times_transposed(grad_hidden_low, first_back)
    grad_mixed = jnp.dot(grad_branch, out_back, preferred_element_type=SINGLE)
    grad_mixed_low = grad_mixed.reshape(length, heads, HEAD_DIM).astype(NARROW)
    grad_w_fc2 = lax.psum_scatter(
        transposed_times(grad_branch, hidden_low), ("fsdp", "rep"), scatter_dimension=0, tiled=True
    )
    grad_w_fc1 = lax.psum_scatter(
        transposed_times(resid_norm, grad_hidden_low),
        ("fsdp", "rep"),
        scatter_dimension=0,
        tiled=True,
    )
    grad_w_out = lax.psum_scatter(
        transposed_times(grad_branch, mixed_low), ("fsdp", "rep"), scatter_dimension=0, tiled=True
    )
    again_probs = jnp.exp(attention_scores() - log_total)
    grad_value = jnp.einsum(
        "hqk,qhd->khd", again_probs.astype(NARROW), grad_mixed_low, preferred_element_type=SINGLE
    ).reshape(length, width)
    grad_probs = jnp.einsum(
        "qhd,khd->hqk", grad_mixed_low, value_low, preferred_element_type=SINGLE
    )
    inner = jnp.sum(again_probs * grad_probs, -1, keepdims=True)
    grad_scores = (again_probs * (grad_probs - inner)).astype(NARROW)
    grad_query_rot = (
        jnp.einsum("hqk,khd->qhd", grad_scores, key_rot, preferred_element_type=SINGLE) * scale
    )
    grad_key_rot = (
        jnp.einsum("hqk,qhd->khd", grad_scores, query_rot, preferred_element_type=SINGLE) * scale
    )
    grad_query = rotate(grad_query_rot, cosine, -sine).reshape(length, width)
    grad_key = rotate(grad_key_rot, cosine, -sine).reshape(length, width)
    grad_qkv_bias = jnp.concatenate(
        [jnp.sum(grad_query, 0), jnp.sum(grad_key, 0), jnp.sum(grad_value, 0)]
    )
    grad_query_low = grad_query.astype(NARROW)
    grad_key_low = grad_key.astype(NARROW)
    grad_value_low = grad_value.astype(NARROW)
    grad_query_norm = times_transposed(grad_query_low, qkv_back[:, :width])
    grad_key_norm = times_transposed(grad_key_low, qkv_back[:, width : 2 * width])
    grad_value_norm = times_transposed(grad_value_low, qkv_back[:, 2 * width :])
    grad_w_qkv = lax.psum_scatter(
        jnp.concatenate(
            [
                transposed_times(query_norm, grad_query_low),
                transposed_times(key_norm, grad_key_low),
                transposed_times(value_norm, grad_value_low),
            ],
            1,
        ),
        ("fsdp", "rep"),
        scatter_dimension=0,
        tiled=True,
    )
    grad_normed = norm_back((grad_query_norm, grad_key_norm, grad_value_norm, grad_resid_norm))
    stream_grads = [grad_normed[0], grad_normed[1], grad_normed[2], grad_normed[3] + grad_entry]
    grad_history = jnp.stack(
        [grad_sources[index] + blend(alpha[:, :, index], stream_grads) for index in range(entries)]
    )
    grad_mix_in = jnp.stack(
        [
            jnp.stack(
                [jnp.sum(stream_grads[stream] * sources[index], -1) for index in range(entries)], -1
            )
            for stream in range(stream_count)
        ],
        1,
    ).reshape(length, stream_count * entries)
    grad_gain_all = jnp.concatenate([grad_normed[4], grad_rms_gain[None]], 0)
    small = (
        lax.psum_scatter(grad_qkv_bias, ("fsdp", "rep"), scatter_dimension=0, tiled=True),
        lax.psum_scatter(grad_branch_bias, ("fsdp", "rep"), scatter_dimension=0, tiled=True),
        lax.psum_scatter(grad_first_bias, ("fsdp", "rep"), scatter_dimension=0, tiled=True),
        lax.psum_scatter(grad_branch_bias, ("fsdp", "rep"), scatter_dimension=0, tiled=True),
        lax.psum_scatter(grad_gain_all, ("fsdp", "rep"), scatter_dimension=1, tiled=True),
        lax.psum_scatter(grad_normed[5], ("fsdp", "rep"), scatter_dimension=1, tiled=True),
        lax.psum_scatter(grad_w_mix1, ("fsdp", "rep"), scatter_dimension=0, tiled=True),
    )
    tail = lax.psum((grad_b_mix1, grad_w_mix2, grad_b_mix2), ("fsdp", "rep"))
    return (
        next_streams,
        grad_history,
        grad_mix_in,
        small[4],
        small[5],
        grad_w_qkv,
        small[0],
        grad_w_out,
        small[1],
        grad_w_fc1,
        small[2],
        grad_w_fc2,
        small[3],
        small[6],
        tail[0],
        tail[1],
        tail[2],
    )


def solution(mesh):
    in_specs = (
        P(None, ("fsdp", "rep"), None),
        P(("fsdp", "rep"), None),
        P(("fsdp", "rep"), None),
        P(("fsdp", "rep"), None),
        P(),
        P(None, ("fsdp", "rep")),
        P(None, ("fsdp", "rep")),
        P(("fsdp", "rep"), None),
        P(("fsdp", "rep")),
        P(("fsdp", "rep"), None),
        P(("fsdp", "rep")),
        P(("fsdp", "rep"), None),
        P(("fsdp", "rep")),
        P(("fsdp", "rep"), None),
        P(("fsdp", "rep")),
        P(("fsdp", "rep"), None),
        P(),
        P(),
        P(),
        P(None, ("fsdp", "rep"), None),
    )
    out_specs = (
        P(None, ("fsdp", "rep"), None),
        P(None, ("fsdp", "rep"), None),
        P(("fsdp", "rep"), None),
        P(None, ("fsdp", "rep")),
        P(None, ("fsdp", "rep")),
        P(("fsdp", "rep"), None),
        P(("fsdp", "rep")),
        P(("fsdp", "rep"), None),
        P(("fsdp", "rep")),
        P(("fsdp", "rep"), None),
        P(("fsdp", "rep")),
        P(("fsdp", "rep"), None),
        P(("fsdp", "rep")),
        P(("fsdp", "rep"), None),
        P(),
        P(),
        P(),
    )
    return jax.shard_map(
        on_device, mesh=mesh, in_specs=in_specs, out_specs=out_specs, check_vma=False
    )
```

profile of v0, /device:TPU:0, one launch (start us, length us, event | category | flops | bytes accessed | tf_op | source)
XLA Modules:
  0.0 4928.6 jit_solution(11905802671768574912)
XLA Ops:
  15.6 43.0 all-reduce.15
  58.6 66.4 %all-gather.1 = bf16[32,64,2]{1,2,0:T(2,128)(2,1)S(1)} all-gather(bf16[1,64,2]{1,2,0:T(2,128)(2,1)S(1)} %convert_bitcast_fusion.10), channel_id=1, replica_groups=mesh['fsdp'=8,'rep'=4] {'fsdp','rep'}, dimensions={0}, use_global_device_ids=true | all-gather | bytes 8448 | tf_op jit(solution)/shard_map/all_gather | solution.py:96
  125.1 64.3 %all-gather = bf16[32,64,3]{1,2,0:T(4,128)(2,1)S(1)} all-gather(bf16[1,64,3]{1,2,0:T(4,128)(2,1)S(1)} %convert_bitcast_fusion.9), channel_id=1, replica_groups=mesh['fsdp'=8,'rep'=4] {'fsdp','rep'}, dimensions={0}, use_global_device_ids=true | all-gather | bytes 12672 | tf_op jit(solution)/shard_map/all_gather | solution.py:95
  189.5 66.7 %all-gather.2 = bf16[32,1,256]{2,1,0:T(2,128)(2,1)S(1)} all-gather(bf16[1,1,256]{2,1,0:T(2,128)(2,1)S(1)} %reshape.710), channel_id=1, replica_groups=mesh['fsdp'=8,'rep'=4] {'fsdp','rep'}, dimensions={0}, use_global_device_ids=true | all-gather | bytes 16896 | tf_op jit(solution)/shard_map/all_gather | solution.py:101
  267.7 83.5 %all_gather.48 = bf16[2048,100]{1,0:T(8,128)(2,1)} all-gather(bf16[64,100]{1,0:T(8,128)(2,1)S(1)} %convert_element_type.396), channel_id=1, replica_groups=mesh['fsdp'=8,'rep'=4] {'fsdp','rep'}, dimensions={0}, use_global_device_ids=true | all-gather | bytes 422400 | tf_op jit(solution)/shard_map/all_gather | solution.py:97
  356.0 5.3 fusion.176
  372.4 5.3 fusion.185
  379.7 22.4 multiply_convert_fusion
  402.1 171.0 %all-gather.14.cloned.1.call-done = bf16[2048,8192]{1,0:T(8,128)(2,1)} async-done(((bf16[64,8192]{1,0:T(8,128)(2,1)}), bf16[2048,8192]{1,0:T(8,128)(2,1)}) %all-gather.14.cloned.1.call-update) | async-done | bytes 33554448 | tf_op jit(solution)/shard_map/all_gather | solution.py:102
  573.1 17.7 convolution_add_fusion.1
  590.8 60.7 %all-gather.10.cloned.1.call-done = bf16[2048,2048]{1,0:T(8,128)(2,1)} async-done(((bf16[64,2048]{1,0:T(8,128)(2,1)}), bf16[2048,2048]{1,0:T(8,128)(2,1)}) %all-gather.10.cloned.1.call-update) | async-done | bytes 8388624 | tf_op jit(solution)/shard_map/all_gather | solution.py:93
  651.5 10.4 fusion.345
  691.6 18.5 fusion.497
  710.1 20.0 multiply_reduce_fusion.4
  730.1 6.4 fusion.4
  736.6 6.7 fusion
  743.4 8.3 multiply_reduce_fusion.3
  757.5 9.1 fusion.522
  767.7 11.0 fusion.382
  778.9 11.1 fusion.384
  790.1 11.1 fusion.380
  801.2 34.3 pad_maximum_fusion
  835.5 48.9 copy.182
  885.1 24.9 fusion.369
  910.1 25.1 fusion.523
  984.4 31.2 all-reduce.18.cloned.1.call-done
  1018.9 135.4 %reduce-scatter.22.cloned.1.call-done = f32[64,3]{1,0:T(8,128)} async-done(((f32[2048,3]{1,0:T(8,128)}), f32[64,3]{1,0:T(8,128)}) %reduce-scatter.22.cloned.1.call-update) | async-done | bytes 784
  1155.8 133.6 %reduce-scatter.20.cloned.1.call-done = f32[64,100]{1,0:T(8,128)} async-done(((f32[2048,100]{1,0:T(8,128)}), f32[64,100]{1,0:T(8,128)}) %reduce-scatter.20.cloned.1.call-update) | async-done | bytes 25616 | tf_op jit(solution)/shard_map/reduce_scatter | solution.py:321
  1289.4 364.1 %reduce-scatter.14.cloned.1.call-done = f32[64,2048]{1,0:T(8,128)} async-done(((f32[2048,2048]{1,0:T(8,128)}), f32[64,2048]{1,0:T(8,128)}) %reduce-scatter.14.cloned.1.call-update) | async-done | bytes 524304 | tf_op jit(solution)/shard_map/reduce_scatter | solution.py:257
  1653.5 437.5 %reduce-scatter.26.cloned.1.call-done = f32[64,6144]{1,0:T(8,128)} async-done(((f32[2048,6144]{1,0:T(8,128)}), f32[64,6144]{1,0:T(8,128)}) %reduce-scatter.26.cloned.1.call-update) | async-done | bytes 1572880
  2091.0 1412.7 %reduce-scatter.16.cloned.1.call-done = f32[64,8192]{1,0:T(8,128)} async-done(((f32[2048,8192]{1,0:T(8,128)}), f32[64,8192]{1,0:T(8,128)}) %reduce-scatter.16.cloned.1.call-update) | async-done | bytes 2097168 | tf_op jit(solution)/shard_map/reduce_scatter | solution.py:251
  3503.6 1413.6 %reduce-scatter.18.cloned.1.call-done = f32[64,8192]{1,0:T(8,128)} async-done(((f32[2048,8192]{1,0:T(8,128)}), f32[64,8192]{1,0:T(8,128)}) %reduce-scatter.18.cloned.1.call-update) | async-done | bytes 2097168 | tf_op jit(solution)/shard_map/reduce_scatter | solution.py:248
  (544 shorter events, 131.0 us)
Async XLA Ops:
  7.2 657.9 %copy-start = (f32[100,40]{0,1:T(8,128)S(1)}, f32[100,40]{0,1:T(8,128)}, u32[]{:S(2)}) copy-start(f32[100,40]{0,1:T(8,128)} %param.37) | copy-start | bytes 48004
  7.2 348.8 %all-gather.8.cloned.1.call-start = ((), (), s32[]{:S(2)}) async-start(), calls=%async_computation.7 | async-start | bytes 25952256 | tf_op jit(solution)/shard_map/all_gather | solution.py:91
  9.9 115.2 %copy-start.53 = (f32[64,100]{1,0:T(8,128)S(1)}, f32[64,100]{1,0:T(8,128)}, u32[]{:S(2)}) copy-start(f32[64,100]{1,0:T(8,128)} %param.35) | copy-start | bytes 76804
  9.9 246.4 %copy-start.54 = (f32[128,36]{0,1:T(8,128)S(1)}, f32[128,36]{0,1:T(8,128)}, u32[]{:S(2)}) copy-start(f32[128,36]{0,1:T(8,128)} %param.21) | copy-start | bytes 55300
  9.9 369.8 %all-gather.12.cloned.1.call-start = ((), (), s32[]{:S(2)}) async-start(), calls=%async_computation.9 | async-start | bytes 34603008 | tf_op jit(solution)/shard_map/all_gather | solution.py:100
  11.1 562.0 %all-gather.14.cloned.1.call-start = ((), (), s32[]{:S(2)}) async-start(), calls=%async_computation.10 | async-start | bytes 34603008 | tf_op jit(solution)/shard_map/all_gather | solution.py:102
  13.8 637.7 %all-gather.10.cloned.1.call-start = ((), (), s32[]{:S(2)}) async-start(), calls=%async_computation.8 | async-start | bytes 8650752 | tf_op jit(solution)/shard_map/all_gather | solution.py:93
  14.6 968.3 %reduce-scatter.24.cloned.1.call-start = ((), (), s32[]{:S(2)}) async-start(), calls=%async_computation.16 | async-start | bytes 1081344
  264.0 526.0 %copy-start.64 = (f32[128]{0:T(128)}, f32[128]{0:T(128)S(1)}, u32[]{:S(2)}) copy-start(f32[128]{0:T(128)S(1)} %broadcast_multiply_fusion.3) | copy-start | bytes 1540
  265.2 501.8 %copy-start.66 = (f32[128]{0:T(128)}, f32[128]{0:T(128)S(1)}, u32[]{:S(2)}) copy-start(f32[128]{0:T(128)S(1)} %broadcast_multiply_fusion.1) | copy-start | bytes 1540
  265.6 85.6 %copy-start.142 = (f32[128]{0:T(128)}, f32[128]{0:T(128)S(1)}, u32[]{:S(2)}) copy-start(f32[128]{0:T(128)S(1)} %multiply_reduce_fusion.16) | copy-start | bytes 1540
  266.0 85.5 %copy-start.39 = (bf16[4,128,2048]{2,1,0:T(8,128)(2,1)S(1)}, bf16[4,128,2048]{2,1,0:T(8,128)(2,1)}, u32[]{:S(2)}) copy-start(bf16[4,128,2048]{2,1,0:T(8,128)(2,1)} %param.39) | copy-start | bytes 6291460
  266.3 85.8 %copy-start.106 = (f32[128]{0:T(128)}, f32[128]{0:T(128)S(1)}, u32[]{:S(2)}) copy-start(f32[128]{0:T(128)S(1)} %get-tuple-element.334) | copy-start | bytes 1540
  266.3 85.8 %copy-start.108 = (f32[128]{0:T(128)}, f32[128]{0:T(128)S(1)}, u32[]{:S(2)}) copy-start(f32[128]{0:T(128)S(1)} %get-tuple-element.335) | copy-start | bytes 1540
  266.3 85.8 %copy-start.110 = (f32[128]{0:T(128)}, f32[128]{0:T(128)S(1)}, u32[]{:S(2)}) copy-start(f32[128]{0:T(128)S(1)} %get-tuple-element.336) | copy-start | bytes 1540
  266.3 85.8 %copy-start.112 = (f32[128]{0:T(128)}, f32[128]{0:T(128)S(1)}, u32[]{:S(2)}) copy-start(f32[128]{0:T(128)S(1)} %get-tuple-element.337) | copy-start | bytes 1540
  267.4 85.8 %copy-start.18 = (f32[128,2048]{1,0:T(8,128)}, f32[128,2048]{1,0:T(8,128)S(1)}, u32[]{:S(2)}) copy-start(f32[128,2048]{1,0:T(8,128)S(1)} %get-tuple-element.216) | copy-start | bytes 3145732
  267.4 511.2 %copy-start.68 = (f32[128]{0:T(128)}, f32[128]{0:T(128)S(1)}, u32[]{:S(2)}) copy-start(f32[128]{0:T(128)S(1)} %broadcast_multiply_fusion.2) | copy-start | bytes 1540
  351.2 438.8 %copy-start.124 = (f32[128]{0:T(128)}, f32[128]{0:T(128)S(1)}, u32[]{:S(2)}) copy-start(f32[128]{0:T(128)S(1)} %fusion.458) | copy-start | bytes 1540
  351.3 415.7 %copy-start.126 = (f32[128]{0:T(128)}, f32[128]{0:T(128)S(1)}, u32[]{:S(2)}) copy-start(f32[128]{0:T(128)S(1)} %fusion.460) | copy-start | bytes 1540
  351.3 427.4 %copy-start.128 = (f32[128]{0:T(128)}, f32[128]{0:T(128)S(1)}, u32[]{:S(2)}) copy-start(f32[128]{0:T(128)S(1)} %fusion.459) | copy-start | bytes 1540
  356.0 434.0 %copy-start.51 = (f32[1,2048]{1,0:T(1,128)}, f32[1,2048]{1,0:T(1,128)S(1)}, u32[]{:S(2)}) copy-start(f32[1,2048]{1,0:T(1,128)S(1)} %get-tuple-element.277) | copy-start | bytes 24580
  662.0 94.0 %copy-start.7 = (f32[128,2048]{1,0:T(8,128)}, f32[128,2048]{1,0:T(8,128)S(1)}, u32[]{:S(2)}) copy-start(f32[128,2048]{1,0:T(8,128)S(1)} %get-tuple-element.452) | copy-start | bytes 3145732
  753.1 262.4 %all-reduce.18.cloned.1.call-start = ((), (), s32[]{:S(2)}) async-start(), calls=%async_computation.18 | async-start | bytes 174080
  754.4 399.9 %reduce-scatter.22.cloned.1.call-start = ((), (), s32[]{:S(2)}) async-start(), calls=%async_computation.15 | async-start | bytes 1081344
  755.9 533.5 %reduce-scatter.20.cloned.1.call-start = ((), (), s32[]{:S(2)}) async-start(), calls=%async_computation.14 | async-start | bytes 1081344 | tf_op jit(solution)/shard_map/reduce_scatter | solution.py:321
  757.4 896.1 %reduce-scatter.14.cloned.1.call-start = ((), (), s32[]{:S(2)}) async-start(), calls=%async_computation.11 | async-start | bytes 17301504 | tf_op jit(solution)/shard_map/reduce_scatter | solution.py:257
  766.8 1324.2 %reduce-scatter.26.cloned.1.call-start = ((), (), s32[]{:S(2)}) async-start(), calls=%async_computation.17 | async-start | bytes 51904512
  884.4 2619.2 %reduce-scatter.16.cloned.1.call-start = ((), (), s32[]{:S(2)}) async-start(), calls=%async_computation.12 | async-start | bytes 69206016 | tf_op jit(solution)/shard_map/reduce_scatter | solution.py:251
  910.0 4007.2 %reduce-scatter.18.cloned.1.call-start = ((), (), s32[]{:S(2)}) async-start(), calls=%async_computation.13 | async-start | bytes 69206016 | tf_op jit(solution)/shard_map/reduce_scatter | solution.py:248
  981.2 3940.1 %copy-start.1 = (f32[100,40]{0,1:T(8,128)S(1)}, f32[100,40]{0,1:T(8,128)}, u32[]{:S(2)}) copy-start(f32[100,40]{0,1:T(8,128)} %param.37) | copy-start | bytes 48004
  1016.3 3905.1 %copy-start.157 = (f32[64]{0:T(128)}, f32[64]{0:T(128)S(1)}, u32[]{:S(2)}) copy-start(f32[64]{0:T(128)S(1)} %dynamic-slice.1) | copy-start | bytes 772
  (144 other events, 1360.4 us)
Sparse Core Ops, SparseCore 0:
  11.5 159.0 all-gather.7
  174.1 201.1 all-gather.11
  378.8 194.2 all-gather.13
  575.9 75.5 all-gather.9
  753.2 133.9 reduce-scatter.23
  895.7 119.7 all-reduce.17
  1017.8 136.4 reduce-scatter.21
  1157.2 132.1 reduce-scatter.19
  1292.3 361.0 reduce-scatter.13
  1661.5 429.4 reduce-scatter.25
  2094.0 1409.5 reduce-scatter.15
  3506.6 1410.6 reduce-scatter.17
where the time goes:
time: 4940 us; the launch traced here: 4930 us
  waiting for transfers between devices  4160 us (84%)
  blocking collectives  324 us (7%)
  matrix products  235 us (5%)
  other arithmetic  111 us (2%)
  local copies, waits for them, and re-layouts  80.7 us (2%)
    reduce_scatter x1, waiting for transfers between devices, on_device(): lax.psum_scatter(transposed_times(grad_branch, hidden_low), ('fsdp', 'rep...  1410 us
    reduce_scatter x1, waiting for transfers between devices, on_device(): lax.psum_scatter(transposed_times(resid_norm, grad_hidden_low), ('fsdp',...  1410 us
    unnamed x16, waiting for transfers between devices  604 us
    reduce_scatter x1, waiting for transfers between devices, on_device(): lax.psum_scatter(transposed_times(grad_branch, mixed_low), ('fsdp', 'rep'...  364 us
    all_gather x1, waiting for transfers between devices, on_device(): lax.all_gather(w_fc2.astype(NARROW), ('fsdp', 'rep'), axis=0, tiled=True)  171 us
    reduce_scatter x1, waiting for transfers between devices, on_device(): lax.psum_scatter(grad_w_mix1, ('fsdp', 'rep'), scatter_dimension=0, tiled...  134 us
  transfers between devices with their start and end apart: 12, of which 9 were waited for; matrix products, arithmetic and copies ran while one was open for 6% of the time, Pallas kernels for 0%

commit v1 on v0

v1 whole, which is shorter than its diff:
```python
import jax
import jax.numpy as jnp
from jax import lax
from jax.sharding import PartitionSpec as P

HEAD_DIM = 128
ROT = 32
NARROW = jnp.bfloat16
SINGLE = jnp.float32
NORM_EPSILON = 1e-05
RMS_EPSILON = 1e-06
AXES = ("fsdp", "rep")


def layer_norm(values, gain_row, shift_row):
    center = values - jnp.mean(values, -1, keepdims=True)
    spread = jnp.mean(center * center, -1, keepdims=True)
    return center * lax.rsqrt(spread + NORM_EPSILON) * gain_row + shift_row


def norm_streams(query_in, key_in, value_in, resid_in, gains, shifts):
    return (
        layer_norm(query_in, gains[0], shifts[0]),
        layer_norm(key_in, gains[0], shifts[0]),
        layer_norm(value_in, gains[0], shifts[0]),
        layer_norm(resid_in, gains[1], shifts[1]),
    )


def rms_norm(entry, gain_row):
    return entry * lax.rsqrt(jnp.mean(entry * entry, -1, keepdims=True) + RMS_EPSILON) * gain_row


def gelu_exact(values):
    return jax.nn.gelu(values, approximate=False)


def rotate(values, cosine, sine):
    halfway = ROT // 2
    former = values[..., :halfway]
    latter = values[..., halfway:ROT]
    return jnp.concatenate(
        [former * cosine - latter * sine, latter * cosine + former * sine, values[..., ROT:]], -1
    )


def times(left, right):
    return jnp.dot(left, right, preferred_element_type=SINGLE)


def times_transposed(left, right):
    return lax.dot_general(left, right, (((1,), (1,)), ((), ())), preferred_element_type=SINGLE)


def transposed_times(left, right):
    return lax.dot_general(left, right, (((0,), (0,)), ((), ())), preferred_element_type=SINGLE)


def blend(weights, sources):
    result = weights[:, 0:1] * sources[0]
    for index in range(1, len(sources)):
        result = result + weights[:, index : index + 1] * sources[index]
    return result


def pick(values, index, axis=0):
    return lax.dynamic_index_in_dim(values, index, axis, keepdims=False)


def ordered(parts, own, axis=0):
    shape = parts[0].shape[:axis] + (len(parts),) + parts[0].shape[axis:]
    result = jnp.zeros(shape, parts[0].dtype)
    for k, part in enumerate(parts):
        result = lax.dynamic_update_index_in_dim(result, part, own ^ k, axis)
    return result


def on_device(
    fsdp,
    rep,
    history,
    mix_in,
    doc_ids,
    doc_group,
    group_weight,
    norm_gain,
    norm_bias,
    w_qkv,
    b_qkv,
    w_out,
    b_out,
    w_fc1,
    b_fc1,
    w_fc2,
    b_fc2,
    w_mix1,
    b_mix1,
    w_mix2,
    b_mix2,
    cotangent,
):
    entries, length, width = history.shape
    stream_count = cotangent.shape[0]
    rows = w_qkv.shape[0]
    hidden = w_fc1.shape[1]
    chips = fsdp // 2
    devices = fsdp * rep
    head_cols = width // fsdp
    heads = head_cols // HEAD_DIM
    hid_cols = hidden // (2 * rep)
    place = lax.axis_index("fsdp")
    line = lax.axis_index("rep")
    core = place & 1
    chip = place >> 1

    def swap_core(values):
        return lax.ppermute(values, "fsdp", [(i, i ^ 1) for i in range(fsdp)])

    def hop_chip(values, m):
        return lax.ppermute(values, "fsdp", [(i, i ^ (2 * m)) for i in range(fsdp)])

    def hop_rep(values, k):
        return lax.ppermute(values, "rep", [(i, i ^ k) for i in range(rep)])

    def both_cores(mine, theirs):
        other = swap_core(theirs)
        return jnp.stack([jnp.where(core == 0, mine, other), jnp.where(core == 0, other, mine)])

    small = [
        norm_gain.reshape(-1),
        norm_bias.reshape(-1),
        b_qkv,
        b_out,
        b_fc1,
        b_fc2,
        doc_ids.reshape(-1),
        w_mix1.reshape(-1),
    ]
    sizes = [part.shape[0] for part in small]
    packed = jnp.concatenate([part.astype(NARROW) for part in small])
    gathered = lax.all_to_all(
        jnp.broadcast_to(packed[None], (devices, packed.shape[0])), AXES, 0, 0, tiled=True
    )
    fields, start = [], 0
    for size in sizes:
        fields.append(gathered[:, start : start + size])
        start += size
    gains = fields[0].reshape(devices, 3, rows).transpose(1, 0, 2).reshape(3, width).astype(SINGLE)
    shifts = fields[1].reshape(devices, 2, rows).transpose(1, 0, 2).reshape(2, width).astype(SINGLE)
    qkv_bias = fields[2].reshape(3, fsdp, head_cols).astype(SINGLE)
    out_bias = fields[3].reshape(width).astype(SINGLE)
    first_bias = fields[4].reshape(2 * rep, hid_cols).astype(SINGLE)
    second_bias = fields[5].reshape(width).astype(SINGLE)
    docs_all = fields[6].reshape(fsdp, rep, length)
    mix_first = fields[7].reshape(width, -1)
    my_qkv_bias = pick(qkv_bias, place, 1).reshape(3 * head_cols)
    my_first_bias = pick(first_bias, core * rep + line)

    def spread_hidden(weight):
        split = weight.astype(NARROW).reshape(rows, 2, rep, hid_cols)
        pair = both_cores(pick(split, core, 1), pick(split, 1 - core, 1))
        parts = [pick(pair, line, 2)]
        for k in range(1, rep):
            parts.append(hop_rep(pick(pair, line ^ k, 2), k))
        block = ordered(parts, line, 1).reshape(2 * rep * rows, hid_cols)
        blocks = [block] + [hop_chip(block, m) for m in range(1, chips)]
        return ordered(blocks, chip, 0).reshape(width, hid_cols)

    def spread_heads():
        split = jnp.concatenate(
            [
                w_qkv.astype(NARROW).reshape(rows, 3, fsdp, head_cols),
                w_out.astype(NARROW).reshape(rows, 1, fsdp, head_cols),
            ],
            1,
        )
        split = split.transpose(2, 0, 1, 3).reshape(chips, 2, rows, 4 * head_cols)
        pair = both_cores(pick(split, core, 1), pick(split, 1 - core, 1))
        parts = [pick(pair, chip, 1)]
        for m in range(1, chips):
            parts.append(hop_chip(pick(pair, chip ^ m, 1), m))
        block = ordered(parts, chip, 0)
        blocks = [block] + [hop_rep(block, k) for k in range(1, rep)]
        return ordered(blocks, line, 2).reshape(width, 4 * head_cols)

    first_full = spread_hidden(w_fc1)
    second_full = spread_hidden(w_fc2)
    heads_full = spread_heads()
    qkv_full = heads_full[:, : 3 * head_cols]
    out_full = heads_full[:, 3 * head_cols :]

    def gather_rep(values):
        parts = [values] + [hop_rep(values, k) for k in range(1, rep)]
        mine = jnp.stack(parts)
        return jnp.stack([mine, swap_core(mine)])

    def scatter_rep(values):
        mine = values[0] + swap_core(values[1].astype(NARROW)).astype(SINGLE)
        total = mine[0]
        for k in range(1, rep):
            total = total + hop_rep(mine[k].astype(NARROW), k).astype(SINGLE)
        return total

    def gather_fsdp(values):
        parts = [values] + [hop_chip(values, m) for m in range(1, chips)]
        mine = jnp.stack(parts)
        return jnp.stack([mine, swap_core(mine)])

    def scatter_fsdp(values):
        mine = values[0] + swap_core(values[1].astype(NARROW)).astype(SINGLE)
        total = mine[0]
        for m in range(1, chips):
            total = total + hop_chip(mine[m].astype(NARROW), m).astype(SINGLE)
        return total

    sources = [history[index].astype(SINGLE) for index in range(entries)]
    alpha = mix_in.reshape(length, stream_count, entries)
    stream_in = [blend(alpha[:, stream], sources) for stream in range(stream_count)]
    normed, norm_back = jax.vjp(
        norm_streams,
        stream_in[0],
        stream_in[1],
        stream_in[2],
        stream_in[3],
        gains[:2],
        shifts,
    )
    resid_norm = gather_rep(normed[3].astype(NARROW)).reshape(2 * rep * length, width)
    qkv_norm = gather_fsdp(jnp.stack(normed[:3]).astype(NARROW))
    qkv_norm = qkv_norm.transpose(2, 0, 1, 3, 4).reshape(3, fsdp * length, width)

    seqs = fsdp
    position = jnp.arange(length).astype(SINGLE)
    frequency = 10000.0 ** (-jnp.arange(0, ROT, 2).astype(SINGLE) / ROT)
    angle = position[:, None] * frequency[None, :]
    cosine = jnp.cos(angle)[None, :, None, :]
    sine = jnp.sin(angle)[None, :, None, :]
    linear = [
        times(qkv_norm[i], qkv_full[:, i * head_cols : (i + 1) * head_cols])
        + my_qkv_bias[i * head_cols : (i + 1) * head_cols]
        for i in range(3)
    ]
    linear = [values.reshape(seqs, length, heads, HEAD_DIM) for values in linear]
    query_rot = rotate(linear[0], cosine, sine).astype(NARROW)
    key_rot = rotate(linear[1], cosine, sine).astype(NARROW)
    value_low = linear[2].astype(NARROW)
    scale = HEAD_DIM ** (-0.5)
    docs_line = pick(docs_all, line, 1)
    docs = jnp.stack(
        [pick(docs_line, place ^ (2 * m + other)) for other in range(2) for m in range(chips)]
    )
    spot = jnp.arange(length)
    allowed = (spot[None, None, :] <= spot[None, :, None]) & (docs[:, None, :] == docs[:, :, None])

    def attention_scores():
        raw = jnp.einsum("bqhd,bkhd->bhqk", query_rot, key_rot, preferred_element_type=SINGLE)
        return jnp.where(allowed[:, None], raw * scale, -1e30)

    scores = attention_scores()
    largest = jnp.max(scores, -1, keepdims=True)
    summed = jnp.sum(jnp.exp(scores - largest), -1, keepdims=True)
    log_total = largest + jnp.log(summed)
    probs = jnp.exp(scores - log_total)
    mixed = jnp.einsum(
        "bhqk,bkhd->bqhd", probs.astype(NARROW), value_low, preferred_element_type=SINGLE
    )
    mixed_low = mixed.reshape(seqs * length, head_cols).astype(NARROW)
    attn_branch = scatter_fsdp(
        times_transposed(mixed_low, out_full).reshape(2, chips, length, width)
    )

    hidden_pre = times(resid_norm, first_full) + my_first_bias
    hidden_act, gelu_back = jax.vjp(gelu_exact, hidden_pre)
    hidden_low = hidden_act.astype(NARROW)
    mlp_branch = scatter_rep(
        times_transposed(hidden_low, second_full).reshape(2, rep, length, width)
    )

    new_entry = stream_in[3] + attn_branch + mlp_branch + (out_bias + second_bias)
    scaled, rms_back = jax.vjp(rms_norm, new_entry, gains[2])
    scaled_low = scaled.astype(NARROW)
    mix_pre = times(scaled_low, mix_first) + b_mix1
    mix_hidden, mix_back = jax.vjp(gelu_exact, mix_pre)
    mix_weights = (
        jnp.dot(mix_hidden, w_mix2, precision=lax.Precision.HIGHEST, preferred_element_type=SINGLE)
        + b_mix2
    )
    all_sources = sources + [new_entry]
    coef = mix_weights.reshape(length, stream_count, entries + 1)
    next_streams = jnp.stack(
        [blend(coef[:, stream], all_sources) for stream in range(stream_count)]
    ).astype(NARROW)

    documents = doc_ids[0]
    doc_match = documents[:, None] == jnp.arange(doc_group.shape[1], dtype=jnp.int32)[None, :]
    token_group = jnp.sum(jnp.where(doc_match, doc_group[0][None, :], 0), axis=1)
    group_match = (
        token_group[:, None] == jnp.arange(group_weight.shape[0], dtype=jnp.int32)[None, :]
    )
    token_weight = jnp.sum(jnp.where(group_match, group_weight[None, :], 0.0), axis=1)
    grad_out = cotangent.astype(SINGLE) * token_weight[None, :, None]
    grad_list = [grad_out[stream] for stream in range(stream_count)]
    grad_sources = [blend(coef[:, :, index], grad_list) for index in range(entries + 1)]
    grad_coef = jnp.stack(
        [
            jnp.stack(
                [
                    jnp.sum(grad_list[stream] * all_sources[index], -1)
                    for index in range(entries + 1)
                ],
                -1,
            )
            for stream in range(stream_count)
        ],
        1,
    )
    grad_mix_weights = grad_coef.reshape(length, stream_count * (entries + 1))
    grad_w_mix2 = jnp.dot(
        mix_hidden.T,
        grad_mix_weights,
        precision=lax.Precision.HIGHEST,
        preferred_element_type=SINGLE,
    )
    grad_b_mix2 = jnp.sum(grad_mix_weights, 0)
    grad_mix_hidden = jnp.dot(
        grad_mix_weights, w_mix2.T, precision=lax.Precision.HIGHEST, preferred_element_type=SINGLE
    )
    (grad_mix_pre,) = mix_back(grad_mix_hidden)
    grad_b_mix1 = jnp.sum(grad_mix_pre, 0)
    grad_mix_low = grad_mix_pre.astype(NARROW)
    grad_w_mix1 = transposed_times(scaled_low, grad_mix_low)
    grad_scaled = times_transposed(grad_mix_low, mix_first)
    grad_entry_rms, grad_rms_gain = rms_back(grad_scaled)
    grad_entry = grad_sources[entries] + grad_entry_rms
    grad_branch_bias = jnp.sum(grad_entry, 0)
    grad_branch = grad_entry.astype(NARROW)
    grad_rep = gather_rep(grad_branch).reshape(2 * rep * length, width)
    grad_fsdp = gather_fsdp(grad_branch).reshape(fsdp * length, width)

    grad_hidden = times(grad_rep, second_full)
    (grad_hidden_pre,) = gelu_back(grad_hidden)
    grad_first_bias = jnp.sum(grad_hidden_pre, 0)
    grad_hidden_low = grad_hidden_pre.astype(NARROW)
    grad_resid_norm = scatter_rep(
        times_transposed(grad_hidden_low, first_full).reshape(2, rep, length, width)
    )

    def collect_hidden(grad):
        blocks = grad.reshape(chips, 2 * rep * rows, hid_cols)
        total = pick(blocks, chip)
        for m in range(1, chips):
            total = total + hop_chip(pick(blocks, chip ^ m).astype(NARROW), m).astype(SINGLE)
        split = total.astype(NARROW).reshape(2, rep, rows, hid_cols)
        parts = [pick(split, line, 1)]
        for k in range(1, rep):
            parts.append(hop_rep(pick(split, line ^ k, 1), k))
        across = ordered(parts, line, 1)
        pair = both_cores(pick(across, core), pick(across, 1 - core))
        return pair.transpose(2, 0, 1, 3).reshape(rows, hidden).astype(SINGLE)

    grad_w_fc2 = collect_hidden(transposed_times(grad_rep, hidden_low))
    grad_w_fc1 = collect_hidden(transposed_times(resid_norm, grad_hidden_low))

    grad_mixed_low = (
        times(grad_fsdp, out_full).astype(NARROW).reshape(seqs, length, heads, HEAD_DIM)
    )
    again_probs = probs
    grad_value = jnp.einsum(
        "bhqk,bqhd->bkhd", again_probs.astype(NARROW), grad_mixed_low, preferred_element_type=SINGLE
    )
    grad_probs = jnp.einsum(
        "bqhd,bkhd->bhqk", grad_mixed_low, value_low, preferred_element_type=SINGLE
    )
    inner = jnp.sum(again_probs * grad_probs, -1, keepdims=True)
    grad_scores = (again_probs * (grad_probs - inner)).astype(NARROW)
    grad_query_rot = (
        jnp.einsum("bhqk,bkhd->bqhd", grad_scores, key_rot, preferred_element_type=SINGLE) * scale
    )
    grad_key_rot = (
        jnp.einsum("bhqk,bqhd->bkhd", grad_scores, query_rot, preferred_element_type=SINGLE) * scale
    )
    grad_linear = [
        values.reshape(seqs * length, head_cols)
        for values in (
            rotate(grad_query_rot, cosine, -sine),
            rotate(grad_key_rot, cosine, -sine),
            grad_value,
        )
    ]
    grad_qkv_bias = jnp.stack([jnp.sum(values, 0) for values in grad_linear])
    grad_linear_low = [values.astype(NARROW) for values in grad_linear]
    grad_qkv_norm = jnp.stack(
        [
            times_transposed(grad_linear_low[i], qkv_full[:, i * head_cols : (i + 1) * head_cols])
            for i in range(3)
        ]
    )
    grad_qkv_norm = scatter_fsdp(
        grad_qkv_norm.reshape(3, 2, chips, length, width).transpose(1, 2, 0, 3, 4)
    )
    grad_heads = jnp.concatenate(
        [transposed_times(qkv_norm[i], grad_linear_low[i]) for i in range(3)]
        + [transposed_times(grad_fsdp, mixed_low)],
        1,
    )

    def collect_heads(grad):
        blocks = grad.reshape(chips, 2, rep, rows, 4 * head_cols)
        total = pick(blocks, line, 2)
        for k in range(1, rep):
            total = total + hop_rep(pick(blocks, line ^ k, 2).astype(NARROW), k).astype(SINGLE)
        split = total.astype(NARROW)
        parts = [pick(split, chip)]
        for m in range(1, chips):
            parts.append(hop_chip(pick(split, chip ^ m), m))
        across = ordered(parts, chip, 1)
        pair = both_cores(pick(across, core), pick(across, 1 - core))
        return pair.transpose(2, 1, 0, 3).reshape(rows, fsdp, 4, head_cols).transpose(0, 2, 1, 3)

    grad_heads = collect_heads(grad_heads)
    grad_w_qkv = grad_heads[:, :3].reshape(rows, 3 * width).astype(SINGLE)
    grad_w_out = grad_heads[:, 3].reshape(rows, width).astype(SINGLE)

    grad_normed = norm_back(
        (grad_qkv_norm[0], grad_qkv_norm[1], grad_qkv_norm[2], grad_resid_norm)
    )
    stream_grads = [grad_normed[0], grad_normed[1], grad_normed[2], grad_normed[3] + grad_entry]
    grad_history = jnp.stack(
        [grad_sources[index] + blend(alpha[:, :, index], stream_grads) for index in range(entries)]
    )
    grad_mix_in = jnp.stack(
        [
            jnp.stack(
                [jnp.sum(stream_grads[stream] * sources[index], -1) for index in range(entries)], -1
            )
            for stream in range(stream_count)
        ],
        1,
    ).reshape(length, stream_count * entries)

    grad_gain_all = jnp.concatenate([grad_normed[4], grad_rms_gain[None]], 0)
    qkv_bias_all = lax.dynamic_update_index_in_dim(
        jnp.zeros((3, fsdp, head_cols), SINGLE), grad_qkv_bias, place, 1
    )
    first_bias_all = lax.dynamic_update_index_in_dim(
        jnp.zeros((2 * rep, hid_cols), SINGLE), grad_first_bias, core * rep + line, 0
    )
    tail = jnp.concatenate([grad_b_mix1, grad_w_mix2.reshape(-1), grad_b_mix2])
    sums = [
        grad_gain_all.reshape(3, devices, rows).transpose(1, 0, 2).reshape(devices, -1),
        grad_normed[5].reshape(2, devices, rows).transpose(1, 0, 2).reshape(devices, -1),
        qkv_bias_all.reshape(devices, -1),
        grad_branch_bias.reshape(devices, -1),
        first_bias_all.reshape(devices, -1),
        grad_w_mix1.reshape(devices, -1),
        jnp.broadcast_to(tail[None], (devices, tail.shape[0])),
    ]
    widths = [part.shape[1] for part in sums]
    total = jnp.sum(lax.all_to_all(jnp.concatenate(sums, 1), AXES, 0, 0, tiled=True), 0)
    outs, start = [], 0
    for size in widths:
        outs.append(total[start : start + size])
        start += size
    hid = b_mix1.shape[0]
    mixes = b_mix2.shape[0]
    return (
        next_streams,
        grad_history,
        grad_mix_in,
        outs[0].reshape(3, rows),
        outs[1].reshape(2, rows),
        grad_w_qkv,
        outs[2],
        grad_w_out,
        outs[3],
        grad_w_fc1,
        outs[4],
        grad_w_fc2,
        outs[3],
        outs[5].reshape(rows, hid),
        outs[6][:hid],
        outs[6][hid : hid + hid * mixes].reshape(hid, mixes),
        outs[6][hid + hid * mixes :],
    )


def solution(mesh):
    fsdp, rep = mesh.shape["fsdp"], mesh.shape["rep"]
    rows = P(AXES, None)
    line = P(AXES)
    streams = P(None, AXES, None)
    columns = P(None, AXES)
    in_specs = (
        streams,
        rows,
        rows,
        rows,
        P(),
        columns,
        columns,
        rows,
        line,
        rows,
        line,
        rows,
        line,
        rows,
        line,
        rows,
        P(),
        P(),
        P(),
        streams,
    )
    out_specs = (
        streams,
        streams,
        rows,
        columns,
        columns,
        rows,
        line,
        rows,
        line,
        rows,
        line,
        rows,
        line,
        rows,
        P(),
        P(),
        P(),
    )

    def local(*args):
        return on_device(fsdp, rep, *args)

    return jax.shard_map(
        local, mesh=mesh, in_specs=in_specs, out_specs=out_specs, check_vma=False
    )
```

time: 4940 us -> 1050 us (0.21)
  waiting for transfers between devices: 4160 us -> 395 us
  blocking collectives: 324 us -> 0 us
  starting transfers between devices: 0.67 us -> 176 us
  matrix products: 235 us -> 90.6 us
  local copies, waits for them, and re-layouts: 80.7 us -> 182 us
  other arithmetic: 111 us -> 190 us
    reduce_scatter x4 -> x0, waiting for transfers between devices: 3320 us -> none  [the longest x1 1410 us: on_device(): lax.psum_scatter(transposed_times(grad_branch, hidden_low), ('fsdp', 'rep...]
    unnamed x16 -> x0, waiting for transfers between devices: 604 us -> none
    ppermute x0 -> x74, waiting for transfers between devices: none -> 390 us  [the longest x30 202 us: hop_rep(): return lax.ppermute(values, 'rep', [(i, i ^ k) for i in range(rep)])]
    all_gather x4 -> x0, blocking collectives: 281 us -> none  [the longest x1 83.5 us: on_device(): lax.all_gather(w_mix1.astype(NARROW), ('fsdp', 'rep'), axis=0, tiled=True)]
    all_gather x4 -> x0, waiting for transfers between devices: 232 us -> none  [the longest x1 171 us: on_device(): lax.all_gather(w_fc2.astype(NARROW), ('fsdp', 'rep'), axis=0, tiled=True)]
    ppermute x0 -> x74, starting transfers between devices: none -> 164 us  [the longest x30 122 us: hop_rep(): return lax.ppermute(values, 'rep', [(i, i ^ k) for i in range(rep)])]
    dot_general x7, matrix products: 93.7 us -> 20.8 us  [transposed_times(): lax.dot_general(left, right, (((0,), (0,)), ((), ())), preferred_element_...]
    another operation x1 -> x27, other arithmetic: 1.38 us -> 60.6 us
  transfers between devices with their start and end apart: 12 -> 76, of which waited for: 9 -> 26; matrix products, arithmetic and copies ran while one was open for 6% -> 35% of each run, Pallas kernels for 0% -> 0%
where the time goes in v1:
time: 1050 us; the launch traced here: 1040 us
  waiting for transfers between devices  395 us (38%)
  other arithmetic  190 us (18%)
  local copies, waits for them, and re-layouts  182 us (17%)
  starting transfers between devices  176 us (17%)
  matrix products  90.6 us (9%)
    ppermute x30, waiting for transfers between devices, hop_rep(): return lax.ppermute(values, 'rep', [(i, i ^ k) for i in range(rep)])  202 us
    ppermute x30, waiting for transfers between devices, hop_chip(): return lax.ppermute(values, 'fsdp', [(i, i ^ 2 * m) for i in range(fsdp)])  188 us
    ppermute x30, starting transfers between devices, hop_rep(): return lax.ppermute(values, 'rep', [(i, i ^ k) for i in range(rep)])  122 us
    ppermute x30, starting transfers between devices, hop_chip(): return lax.ppermute(values, 'fsdp', [(i, i ^ 2 * m) for i in range(fsdp)])  39.1 us
    unnamed x599, local copies, waits for them, and re-layouts  38 us
    dot_general x7, matrix products, times(): return jnp.dot(left, right, preferred_element_type=SINGLE)  37.5 us
    another operation x8, other arithmetic  33 us
    dot_general x7, matrix products, times_transposed(): lax.dot_general(left, right, (((1,), (1,)), ((), ())), preferred_element_...  23.5 us
  transfers between devices with their start and end apart: 76, of which 26 were waited for; matrix products, arithmetic and copies ran while one was open for 35% of the time, Pallas kernels for 0%

profile of v1, /device:TPU:0, one launch (start us, length us, event | category | flops | bytes accessed | tf_op | source)
XLA Modules:
  0.0 1039.1 jit_solution(10512708348496262610)
XLA Ops:
  12.2 7.4 all-to-all-start
  73.8 5.1 collective-permute-done.28
  78.9 18.3 %collective-permute-start.9 = (bf16[4,2,64,1024]{3,2,1,0:T(8,128)(2,1)}, bf16[4,2,64,1024]{3,2,1,0:T(8,128)(2,1)}, u32[]{:S(2)}, u32[]{:S(2)}) collective-permute-start(bf16[4,2,64,1024]{3,2,1,0:T(8,128)(2,1)} %bitcast_dynamic-update-slice_fusion.35), channel_id=1, source_target_pairs={{0,2},{1,3},{2,0},{3,1},{4,6},{5,7},{6,4},{7,5},{8,10},{9,11},{10,... | collective-permute-start | bytes 3145736 | tf_op jit(solution)/shard_map/ppermute | solution.py:123
  128.4 6.2 collective-permute-start.15
  138.2 38.3 %collective-permute-done.15 = bf16[128,2048]{1,0:T(8,128)(2,1)S(1)} collective-permute-done((bf16[128,2048]{1,0:T(8,128)(2,1)}, bf16[128,2048]{1,0:T(8,128)(2,1)S(1)}, u32[]{:S(2)}, u32[]{:S(2)}) %collective-permute-start.15) | collective-permute-done | bytes 524320 | tf_op jit(solution)/shard_map/ppermute | solution.py:123
  182.4 48.4 %collective-permute-done.16 = bf16[128,2048]{1,0:T(8,128)(2,1)} collective-permute-done((bf16[128,2048]{1,0:T(8,128)(2,1)}, bf16[128,2048]{1,0:T(8,128)(2,1)}, u32[]{:S(2)}, u32[]{:S(2)}) %collective-permute-start.16) | collective-permute-done | bytes 524320 | tf_op jit(solution)/shard_map/ppermute | solution.py:123
  245.9 11.0 %collective-permute-done.30 = bf16[512,1024]{1,0:T(8,128)(2,1)S(1)} collective-permute-done((bf16[512,1024]{1,0:T(8,128)(2,1)S(1)}, bf16[512,1024]{1,0:T(8,128)(2,1)S(1)}, u32[]{:S(2)}, u32[]{:S(2)}) %collective-permute-start.30) | collective-permute-done | bytes 1048608 | tf_op jit(solution)/shard_map/ppermute | solution.py:120
  259.4 85.7 %collective-permute-done.31 = bf16[512,1024]{1,0:T(8,128)(2,1)S(1)} collective-permute-done((bf16[512,1024]{1,0:T(8,128)(2,1)S(1)}, bf16[512,1024]{1,0:T(8,128)(2,1)S(1)}, u32[]{:S(2)}, u32[]{:S(2)}) %collective-permute-start.31) | collective-permute-done | bytes 1048608 | tf_op jit(solution)/shard_map/ppermute | solution.py:120
  352.0 19.6 %collective-permute-done.23 = bf16[512,1024]{1,0:T(8,128)(2,1)S(1)} collective-permute-done((bf16[512,1024]{1,0:T(8,128)(2,1)S(1)}, bf16[512,1024]{1,0:T(8,128)(2,1)S(1)}, u32[]{:S(2)}, u32[]{:S(2)}) %collective-permute-start.23) | collective-permute-done | bytes 1048608 | tf_op jit(solution)/shard_map/ppermute | solution.py:120
  371.7 16.9 %collective-permute-done.24 = bf16[512,1024]{1,0:T(8,128)(2,1)S(1)} collective-permute-done((bf16[512,1024]{1,0:T(8,128)(2,1)S(1)}, bf16[512,1024]{1,0:T(8,128)(2,1)S(1)}, u32[]{:S(2)}, u32[]{:S(2)}) %collective-permute-start.24) | collective-permute-done | bytes 1048608 | tf_op jit(solution)/shard_map/ppermute | solution.py:120
  394.5 15.0 %multiply_convert_fusion = (bf16[1024,1024]{1,0:T(8,128)(2,1)S(1)}, f32[1024,1024]{1,0:T(8,128)}, f32[1024,1024]{1,0:T(8,128)}) fusion(f32[1024]{0:T(1024)S(1)} %bitcast.2193, bf16[1024,2048]{1,0:T(8,128)(2,1)S(1)} %bitcast.2077, bf16[2048,1024]{1,0:T(8,128)(2,1)S(1)} %bitcast.2106), kind=kOutput, calls=%fused_computation.23 | convolution fusion | flops 4364173312 | bytes 18878464 | tf_op jit(solution)/shard_map/dot_general | solution.py:48
  468.0 11.8 %collective-permute-start.34 = (bf16[128,2048]{1,0:T(8,128)(2,1)S(1)}, bf16[128,2048]{1,0:T(8,128)(2,1)S(1)}, u32[]{:S(2)}, u32[]{:S(2)}) collective-permute-start(bf16[128,2048]{1,0:T(8,128)(2,1)S(1)} %get-tuple-element.285), channel_id=1, source_target_pairs={{0,1},{1,0},{2,3},{3,2},{4,5},{5,4},{6,7},{7,6},{8,9},{9,8},{10,11... | collective-permute-start | bytes 1572872 | tf_op jit(solution)/shard_map/ppermute | solution.py:123
  489.6 10.9 %collective-permute-done.34 = bf16[128,2048]{1,0:T(8,128)(2,1)S(1)} collective-permute-done((bf16[128,2048]{1,0:T(8,128)(2,1)S(1)}, bf16[128,2048]{1,0:T(8,128)(2,1)S(1)}, u32[]{:S(2)}, u32[]{:S(2)}) %collective-permute-start.34) | collective-permute-done | bytes 524320 | tf_op jit(solution)/shard_map/ppermute | solution.py:123
  506.8 6.6 copy.463
  535.5 9.3 collective-permute-start.45
  554.8 7.7 collective-permute-done.45
  562.5 20.5 %collective-permute-done.46 = bf16[128,2048]{1,0:T(8,128)(2,1)S(1)} collective-permute-done((bf16[128,2048]{1,0:T(8,128)(2,1)S(1)}, bf16[128,2048]{1,0:T(8,128)(2,1)S(1)}, u32[]{:S(2)}, u32[]{:S(2)}) %collective-permute-start.46) | collective-permute-done | bytes 524320 | tf_op jit(solution)/shard_map/ppermute | solution.py:123
  642.9 6.5 copy.465
  649.3 7.1 fusion.18
  661.7 8.1 fusion.507
  689.2 9.7 copy.459
  706.6 8.5 maximum_bitcast_fusion
  721.0 6.8 fusion.398
  729.9 7.3 collective-permute-start.53
  739.6 8.2 fusion.1
  762.9 19.1 %collective-permute-done.53 = bf16[4,2,64,1024]{3,2,1,0:T(8,128)(2,1)} collective-permute-done((bf16[4,2,64,1024]{3,2,1,0:T(8,128)(2,1)}, bf16[4,2,64,1024]{3,2,1,0:T(8,128)(2,1)}, u32[]{:S(2)}, u32[]{:S(2)}) %collective-permute-start.53) | collective-permute-done | bytes 1048608 | tf_op jit(solution)/shard_map/ppermute | solution.py:123
  782.0 27.4 %collective-permute-done.54 = bf16[4,2,64,1024]{3,2,1,0:T(8,128)(2,1)} collective-permute-done((bf16[4,2,64,1024]{3,2,1,0:T(8,128)(2,1)}, bf16[4,2,64,1024]{3,2,1,0:T(8,128)(2,1)}, u32[]{:S(2)}, u32[]{:S(2)}) %collective-permute-start.54) | collective-permute-done | bytes 1048608 | tf_op jit(solution)/shard_map/ppermute | solution.py:123
  815.7 33.4 %collective-permute-start.63 = (bf16[2,64,1024]{2,1,0:T(8,128)(2,1)S(1)}, bf16[2,64,1024]{2,1,0:T(8,128)(2,1)S(1)}, u32[]{:S(2)}, u32[]{:S(2)}) collective-permute-start(bf16[2,64,1024]{2,1,0:T(8,128)(2,1)S(1)} %get-tuple-element.308), channel_id=1, source_target_pairs={{0,1},{1,0},{2,3},{3,2},{4,5},{5,4},{6,7},{7,6},{8,9},{9,8},{10,11... | collective-permute-start | bytes 786440 | tf_op jit(solution)/shard_map/ppermute | solution.py:123
  888.7 5.3 collective-permute-start.50
  896.3 12.9 %fusion.513 = (bf16[4,3,128,2048]{3,2,1,0:T(8,128)(2,1)S(1)}, f32[4,3,128,2048]{3,2,1,0:T(8,128)}) fusion(bf16[4,3,128,2048]{3,2,1,0:T(8,128)(2,1)} %collective-permute-done.41, f32[2,4,3,128,2048]{4,3,2,1,0:T(8,128)} %maximum_bitcast_fusion), kind=kLoop, calls=%fused_computation.1023 | loop fusion | flops 9437184 | bytes 37748736 | tf_op jit(solution)/shard_map/convert.27
  937.3 11.7 %collective-permute-done.42 = bf16[3,128,2048]{2,1,0:T(8,128)(2,1)} collective-permute-done((bf16[3,128,2048]{2,1,0:T(8,128)(2,1)}, bf16[3,128,2048]{2,1,0:T(8,128)(2,1)}, u32[]{:S(2)}, u32[]{:S(2)}) %collective-permute-start.42) | collective-permute-done | bytes 1572896 | tf_op jit(solution)/shard_map/ppermute | solution.py:120
  949.1 31.8 %collective-permute-done.43 = bf16[3,128,2048]{2,1,0:T(8,128)(2,1)} collective-permute-done((bf16[3,128,2048]{2,1,0:T(8,128)(2,1)}, bf16[3,128,2048]{2,1,0:T(8,128)(2,1)}, u32[]{:S(2)}, u32[]{:S(2)}) %collective-permute-start.43) | collective-permute-done | bytes 1572896 | tf_op jit(solution)/shard_map/ppermute | solution.py:120
  (1089 shorter events, 490.2 us)
Async XLA Ops:
  12.2 96.9 %all-to-all-start = ((bf16[32,2,3712]{2,1,0:T(2,128)(2,1)}), bf16[32,2,3712]{2,1,0:T(2,128)(2,1)}, u32[]{:S(2)}, u32[]{:S(2)}) async-start(bf16[32,2,3712]{2,1,0:T(2,128)(2,1)} %reshape.1160), calls=%async_computation | async-start | bytes 950272 | tf_op jit(solution)/shard_map/all_to_all | solution.py:141
  78.9 153.9 %collective-permute-start.8 = (bf16[4,2,64,1024]{3,2,1,0:T(8,128)(2,1)}, bf16[4,2,64,1024]{3,2,1,0:T(8,128)(2,1)}, u32[]{:S(2)}, u32[]{:S(2)}) collective-permute-start(bf16[4,2,64,1024]{3,2,1,0:T(8,128)(2,1)} %bitcast_dynamic-update-slice_fusion.35), channel_id=1, source_target_pairs={{0,1},{1,0},{2,3},{3,2},{4,5},{5,4},{6,7},{7,6},{8,9},{9,8},{10,11... | collective-permute-start | bytes 3145736 | tf_op jit(solution)/shard_map/ppermute | solution.py:123
  78.9 155.4 %collective-permute-start.9 = (bf16[4,2,64,1024]{3,2,1,0:T(8,128)(2,1)}, bf16[4,2,64,1024]{3,2,1,0:T(8,128)(2,1)}, u32[]{:S(2)}, u32[]{:S(2)}) collective-permute-start(bf16[4,2,64,1024]{3,2,1,0:T(8,128)(2,1)} %bitcast_dynamic-update-slice_fusion.35), channel_id=1, source_target_pairs={{0,2},{1,3},{2,0},{3,1},{4,6},{5,7},{6,4},{7,5},{8,10},{9,11},{10,... | collective-permute-start | bytes 3145736 | tf_op jit(solution)/shard_map/ppermute | solution.py:123
  97.3 140.0 %collective-permute-start.10 = (bf16[4,2,64,1024]{3,2,1,0:T(8,128)(2,1)}, bf16[4,2,64,1024]{3,2,1,0:T(8,128)(2,1)}, u32[]{:S(2)}, u32[]{:S(2)}) collective-permute-start(bf16[4,2,64,1024]{3,2,1,0:T(8,128)(2,1)} %bitcast_dynamic-update-slice_fusion.35), channel_id=1, source_target_pairs={{0,3},{1,2},{2,1},{3,0},{4,7},{5,6},{6,5},{7,4},{8,11},{9,10},{10,... | collective-permute-start | bytes 3145736 | tf_op jit(solution)/shard_map/ppermute | solution.py:123
  128.4 48.0 %collective-permute-start.15 = (bf16[128,2048]{1,0:T(8,128)(2,1)}, bf16[128,2048]{1,0:T(8,128)(2,1)S(1)}, u32[]{:S(2)}, u32[]{:S(2)}) collective-permute-start(bf16[128,2048]{1,0:T(8,128)(2,1)} %add_convert_fusion), channel_id=1, source_target_pairs={{0,1},{1,0},{2,3},{3,2},{4,5},{5,4},{6,7},{7,6},{8,9},{9,8},{10,11... | collective-permute-start | bytes 1572872 | tf_op jit(solution)/shard_map/ppermute | solution.py:123
  134.6 96.2 %collective-permute-start.16 = (bf16[128,2048]{1,0:T(8,128)(2,1)}, bf16[128,2048]{1,0:T(8,128)(2,1)}, u32[]{:S(2)}, u32[]{:S(2)}) collective-permute-start(bf16[128,2048]{1,0:T(8,128)(2,1)} %add_convert_fusion), channel_id=1, source_target_pairs={{0,2},{1,3},{2,0},{3,1},{4,6},{5,7},{6,4},{7,5},{8,10},{9,11},{10,... | collective-permute-start | bytes 1572872 | tf_op jit(solution)/shard_map/ppermute | solution.py:123
  176.5 55.8 %collective-permute-start.17 = (bf16[128,2048]{1,0:T(8,128)(2,1)}, bf16[128,2048]{1,0:T(8,128)(2,1)S(1)}, u32[]{:S(2)}, u32[]{:S(2)}) collective-permute-start(bf16[128,2048]{1,0:T(8,128)(2,1)} %add_convert_fusion), channel_id=1, source_target_pairs={{0,3},{1,2},{2,1},{3,0},{4,7},{5,6},{6,5},{7,4},{8,11},{9,10},{10,... | collective-permute-start | bytes 1572872 | tf_op jit(solution)/shard_map/ppermute | solution.py:123
  232.3 115.3 %collective-permute-start = (bf16[3,128,2048]{2,1,0:T(8,128)(2,1)S(1)}, bf16[3,128,2048]{2,1,0:T(8,128)(2,1)S(1)}, u32[]{:S(2)}, u32[]{:S(2)}) collective-permute-start(bf16[3,128,2048]{2,1,0:T(8,128)(2,1)S(1)} %pad_maximum_fusion.9), channel_id=1, source_target_pairs={{0,8},{4,12},{8,0},{12,4},{16,24},{20,28},{24,16},{28,20},{1,9},{5... | collective-permute-start | bytes 4718600 | tf_op jit(solution)/shard_map/ppermute | solution.py:120
  232.8 117.5 %collective-permute-start.1 = (bf16[3,128,2048]{2,1,0:T(8,128)(2,1)S(1)}, bf16[3,128,2048]{2,1,0:T(8,128)(2,1)S(1)}, u32[]{:S(2)}, u32[]{:S(2)}) collective-permute-start(bf16[3,128,2048]{2,1,0:T(8,128)(2,1)S(1)} %pad_maximum_fusion.9), channel_id=1, source_target_pairs={{0,16},{4,20},{8,24},{12,28},{16,0},{20,4},{24,8},{28,12},{1,17},{... | collective-permute-start | bytes 4718600 | tf_op jit(solution)/shard_map/ppermute | solution.py:120
  234.3 116.0 %collective-permute-start.2 = (bf16[3,128,2048]{2,1,0:T(8,128)(2,1)S(1)}, bf16[3,128,2048]{2,1,0:T(8,128)(2,1)S(1)}, u32[]{:S(2)}, u32[]{:S(2)}) collective-permute-start(bf16[3,128,2048]{2,1,0:T(8,128)(2,1)S(1)} %pad_maximum_fusion.9), channel_id=1, source_target_pairs={{0,24},{4,28},{8,16},{12,20},{16,8},{20,12},{24,0},{28,4},{1,25},{... | collective-permute-start | bytes 4718600 | tf_op jit(solution)/shard_map/ppermute | solution.py:120
  237.4 107.7 %collective-permute-start.31 = (bf16[512,1024]{1,0:T(8,128)(2,1)S(1)}, bf16[512,1024]{1,0:T(8,128)(2,1)S(1)}, u32[]{:S(2)}, u32[]{:S(2)}) collective-permute-start(bf16[512,1024]{1,0:T(8,128)(2,1)S(1)} %bitcast.2094), channel_id=1, source_target_pairs={{0,16},{4,20},{8,24},{12,28},{16,0},{20,4},{24,8},{28,12},{1,17},{... | collective-permute-start | bytes 3145736 | tf_op jit(solution)/shard_map/ppermute | solution.py:120
  256.9 94.4 %collective-permute-start.32 = (bf16[512,1024]{1,0:T(8,128)(2,1)S(1)}, bf16[512,1024]{1,0:T(8,128)(2,1)S(1)}, u32[]{:S(2)}, u32[]{:S(2)}) collective-permute-start(bf16[512,1024]{1,0:T(8,128)(2,1)S(1)} %bitcast.2095), channel_id=1, source_target_pairs={{0,24},{4,28},{8,16},{12,20},{16,8},{20,12},{24,0},{28,4},{1,25},{... | collective-permute-start | bytes 3145736 | tf_op jit(solution)/shard_map/ppermute | solution.py:120
  347.6 41.0 %collective-permute-start.24 = (bf16[512,1024]{1,0:T(8,128)(2,1)S(1)}, bf16[512,1024]{1,0:T(8,128)(2,1)S(1)}, u32[]{:S(2)}, u32[]{:S(2)}) collective-permute-start(bf16[512,1024]{1,0:T(8,128)(2,1)S(1)} %bitcast.2098), channel_id=1, source_target_pairs={{0,16},{4,20},{8,24},{12,28},{16,0},{20,4},{24,8},{28,12},{1,17},{... | collective-permute-start | bytes 3145736 | tf_op jit(solution)/shard_map/ppermute | solution.py:120
  350.3 39.4 %collective-permute-start.18 = (bf16[4,128,2048]{2,1,0:T(8,128)(2,1)S(1)}, bf16[4,128,2048]{2,1,0:T(8,128)(2,1)S(1)}, u32[]{:S(2)}, u32[]{:S(2)}) collective-permute-start(bf16[4,128,2048]{2,1,0:T(8,128)(2,1)S(1)} %get-tuple-element.289), channel_id=1, source_target_pairs={{0,4},{4,0},{8,12},{12,8},{16,20},{20,16},{24,28},{28,24},{1,5},{5... | collective-permute-start | bytes 6291464 | tf_op jit(solution)/shard_map/ppermute | solution.py:117
  351.3 64.6 %collective-permute-start.3 = (bf16[4,3,128,2048]{3,2,1,0:T(8,128)(2,1)S(1)}, bf16[4,3,128,2048]{3,2,1,0:T(8,128)(2,1)}, u32[]{:S(2)}, u32[]{:S(2)}) collective-permute-start(bf16[4,3,128,2048]{3,2,1,0:T(8,128)(2,1)S(1)} %pad_maximum_fusion.1), channel_id=1, source_target_pairs={{0,4},{4,0},{8,12},{12,8},{16,20},{20,16},{24,28},{28,24},{1,5},{5... | collective-permute-start | bytes 18874376 | tf_op jit(solution)/shard_map/ppermute | solution.py:117
  416.0 44.3 %collective-permute-start.33 = (bf16[4,128,2048]{2,1,0:T(8,128)(2,1)}, bf16[4,128,2048]{2,1,0:T(8,128)(2,1)}, u32[]{:S(2)}, u32[]{:S(2)}) collective-permute-start(bf16[4,128,2048]{2,1,0:T(8,128)(2,1)} %bitcast.155), channel_id=1, source_target_pairs={{0,4},{4,0},{8,12},{12,8},{16,20},{20,16},{24,28},{28,24},{1,5},{5... | collective-permute-start | bytes 6291464 | tf_op jit(solution)/shard_map/ppermute | solution.py:117
  479.8 38.5 %collective-permute-start.35 = (bf16[128,2048]{1,0:T(8,128)(2,1)}, bf16[128,2048]{1,0:T(8,128)(2,1)}, u32[]{:S(2)}, u32[]{:S(2)}) collective-permute-start(bf16[128,2048]{1,0:T(8,128)(2,1)} %get-tuple-element.287), channel_id=1, source_target_pairs={{0,2},{1,3},{2,0},{3,1},{4,6},{5,7},{6,4},{7,5},{8,10},{9,11},{10,... | collective-permute-start | bytes 1572872 | tf_op jit(solution)/shard_map/ppermute | solution.py:123
  658.2 69.6 %collective-permute-start.67 = (bf16[512,1024]{1,0:T(8,128)(2,1)}, bf16[512,1024]{1,0:T(8,128)(2,1)}, u32[]{:S(2)}, u32[]{:S(2)}) collective-permute-start(bf16[512,1024]{1,0:T(8,128)(2,1)} %get-tuple-element.255), channel_id=1, source_target_pairs={{0,8},{4,12},{8,0},{12,4},{16,24},{20,28},{24,16},{28,20},{1,9},{5... | collective-permute-start | bytes 3145736 | tf_op jit(solution)/shard_map/ppermute | solution.py:120
  659.4 70.5 %collective-permute-start.68 = (bf16[512,1024]{1,0:T(8,128)(2,1)}, bf16[512,1024]{1,0:T(8,128)(2,1)}, u32[]{:S(2)}, u32[]{:S(2)}) collective-permute-start(bf16[512,1024]{1,0:T(8,128)(2,1)} %get-tuple-element.257), channel_id=1, source_target_pairs={{0,16},{4,20},{8,24},{12,28},{16,0},{20,4},{24,8},{28,12},{1,17},{... | collective-permute-start | bytes 3145736 | tf_op jit(solution)/shard_map/ppermute | solution.py:120
  660.9 76.3 %collective-permute-start.69 = (bf16[512,1024]{1,0:T(8,128)(2,1)}, bf16[512,1024]{1,0:T(8,128)(2,1)}, u32[]{:S(2)}, u32[]{:S(2)}) collective-permute-start(bf16[512,1024]{1,0:T(8,128)(2,1)} %get-tuple-element.256), channel_id=1, source_target_pairs={{0,24},{4,28},{8,16},{12,20},{16,8},{20,12},{24,0},{28,4},{1,25},{... | collective-permute-start | bytes 3145736 | tf_op jit(solution)/shard_map/ppermute | solution.py:120
  676.4 61.8 %collective-permute-start.60 = (bf16[512,1024]{1,0:T(8,128)(2,1)}, bf16[512,1024]{1,0:T(8,128)(2,1)}, u32[]{:S(2)}, u32[]{:S(2)}) collective-permute-start(bf16[512,1024]{1,0:T(8,128)(2,1)} %get-tuple-element.258), channel_id=1, source_target_pairs={{0,8},{4,12},{8,0},{12,4},{16,24},{20,28},{24,16},{28,20},{1,9},{5... | collective-permute-start | bytes 3145736 | tf_op jit(solution)/shard_map/ppermute | solution.py:120
  677.5 81.3 %collective-permute-start.61 = (bf16[512,1024]{1,0:T(8,128)(2,1)}, bf16[512,1024]{1,0:T(8,128)(2,1)}, u32[]{:S(2)}, u32[]{:S(2)}) collective-permute-start(bf16[512,1024]{1,0:T(8,128)(2,1)} %get-tuple-element.260), channel_id=1, source_target_pairs={{0,16},{4,20},{8,24},{12,28},{16,0},{20,4},{24,8},{28,12},{1,17},{... | collective-permute-start | bytes 3145736 | tf_op jit(solution)/shard_map/ppermute | solution.py:120
  729.9 52.1 %collective-permute-start.53 = (bf16[4,2,64,1024]{3,2,1,0:T(8,128)(2,1)}, bf16[4,2,64,1024]{3,2,1,0:T(8,128)(2,1)}, u32[]{:S(2)}, u32[]{:S(2)}) collective-permute-start(bf16[4,2,64,1024]{3,2,1,0:T(8,128)(2,1)} %get-tuple-element.261), channel_id=1, source_target_pairs={{0,1},{1,0},{2,3},{3,2},{4,5},{5,4},{6,7},{7,6},{8,9},{9,8},{10,11... | collective-permute-start | bytes 3145736 | tf_op jit(solution)/shard_map/ppermute | solution.py:123
  737.2 72.3 %collective-permute-start.54 = (bf16[4,2,64,1024]{3,2,1,0:T(8,128)(2,1)}, bf16[4,2,64,1024]{3,2,1,0:T(8,128)(2,1)}, u32[]{:S(2)}, u32[]{:S(2)}) collective-permute-start(bf16[4,2,64,1024]{3,2,1,0:T(8,128)(2,1)} %get-tuple-element.263), channel_id=1, source_target_pairs={{0,2},{1,3},{2,0},{3,1},{4,6},{5,7},{6,4},{7,5},{8,10},{9,11},{10,... | collective-permute-start | bytes 3145736 | tf_op jit(solution)/shard_map/ppermute | solution.py:123
  738.2 71.3 %collective-permute-start.55 = (bf16[4,2,64,1024]{3,2,1,0:T(8,128)(2,1)}, bf16[4,2,64,1024]{3,2,1,0:T(8,128)(2,1)}, u32[]{:S(2)}, u32[]{:S(2)}) collective-permute-start(bf16[4,2,64,1024]{3,2,1,0:T(8,128)(2,1)} %get-tuple-element.262), channel_id=1, source_target_pairs={{0,3},{1,2},{2,1},{3,0},{4,7},{5,6},{6,5},{7,4},{8,11},{9,10},{10,... | collective-permute-start | bytes 3145736 | tf_op jit(solution)/shard_map/ppermute | solution.py:123
  758.8 137.5 %collective-permute-start.41 = (bf16[4,3,128,2048]{3,2,1,0:T(8,128)(2,1)}, bf16[4,3,128,2048]{3,2,1,0:T(8,128)(2,1)}, u32[]{:S(2)}, u32[]{:S(2)}) collective-permute-start(bf16[4,3,128,2048]{3,2,1,0:T(8,128)(2,1)} %fusion.1), channel_id=1, source_target_pairs={{0,4},{4,0},{8,12},{12,8},{16,20},{20,16},{24,28},{28,24},{1,5},{5... | collective-permute-start | bytes 18874376 | tf_op jit(solution)/shard_map/ppermute | solution.py:117
  758.9 124.2 %collective-permute-start.49 = (bf16[4,128,2048]{2,1,0:T(8,128)(2,1)}, bf16[4,128,2048]{2,1,0:T(8,128)(2,1)}, u32[]{:S(2)}, u32[]{:S(2)}) collective-permute-start(bf16[4,128,2048]{2,1,0:T(8,128)(2,1)} %bitcast.311), channel_id=1, source_target_pairs={{0,4},{4,0},{8,12},{12,8},{16,20},{20,16},{24,28},{28,24},{1,5},{5... | collective-permute-start | bytes 6291464 | tf_op jit(solution)/shard_map/ppermute | solution.py:117
  809.5 39.7 %collective-permute-start.71 = (bf16[2,64,1024]{2,1,0:T(8,128)(2,1)S(1)}, bf16[2,64,1024]{2,1,0:T(8,128)(2,1)S(1)}, u32[]{:S(2)}, u32[]{:S(2)}) collective-permute-start(bf16[2,64,1024]{2,1,0:T(8,128)(2,1)S(1)} %get-tuple-element.303), channel_id=1, source_target_pairs={{0,2},{1,3},{2,0},{3,1},{4,6},{5,7},{6,4},{7,5},{8,10},{9,11},{10,... | collective-permute-start | bytes 786440 | tf_op jit(solution)/shard_map/ppermute | solution.py:123
  809.5 39.8 %collective-permute-start.72 = (bf16[2,64,1024]{2,1,0:T(8,128)(2,1)S(1)}, bf16[2,64,1024]{2,1,0:T(8,128)(2,1)S(1)}, u32[]{:S(2)}, u32[]{:S(2)}) collective-permute-start(bf16[2,64,1024]{2,1,0:T(8,128)(2,1)S(1)} %get-tuple-element.302), channel_id=1, source_target_pairs={{0,3},{1,2},{2,1},{3,0},{4,7},{5,6},{6,5},{7,4},{8,11},{9,10},{10,... | collective-permute-start | bytes 786440 | tf_op jit(solution)/shard_map/ppermute | solution.py:123
  815.7 38.6 %collective-permute-start.63 = (bf16[2,64,1024]{2,1,0:T(8,128)(2,1)S(1)}, bf16[2,64,1024]{2,1,0:T(8,128)(2,1)S(1)}, u32[]{:S(2)}, u32[]{:S(2)}) collective-permute-start(bf16[2,64,1024]{2,1,0:T(8,128)(2,1)S(1)} %get-tuple-element.308), channel_id=1, source_target_pairs={{0,1},{1,0},{2,3},{3,2},{4,5},{5,4},{6,7},{7,6},{8,9},{9,8},{10,11... | collective-permute-start | bytes 786440 | tf_op jit(solution)/shard_map/ppermute | solution.py:123
  912.3 68.5 %collective-permute-start.43 = (bf16[3,128,2048]{2,1,0:T(8,128)(2,1)}, bf16[3,128,2048]{2,1,0:T(8,128)(2,1)}, u32[]{:S(2)}, u32[]{:S(2)}) collective-permute-start(bf16[3,128,2048]{2,1,0:T(8,128)(2,1)} %get-tuple-element.266), channel_id=1, source_target_pairs={{0,16},{4,20},{8,24},{12,28},{16,0},{20,4},{24,8},{28,12},{1,17},{... | collective-permute-start | bytes 4718600 | tf_op jit(solution)/shard_map/ppermute | solution.py:120
  917.0 65.5 %collective-permute-start.44 = (bf16[3,128,2048]{2,1,0:T(8,128)(2,1)}, bf16[3,128,2048]{2,1,0:T(8,128)(2,1)}, u32[]{:S(2)}, u32[]{:S(2)}) collective-permute-start(bf16[3,128,2048]{2,1,0:T(8,128)(2,1)} %get-tuple-element.265), channel_id=1, source_target_pairs={{0,24},{4,28},{8,16},{12,20},{16,8},{20,12},{24,0},{28,4},{1,25},{... | collective-permute-start | bytes 4718600 | tf_op jit(solution)/shard_map/ppermute | solution.py:120
  (339 other events, 5131.2 us)

commit v2 on v0

v2 whole, which is shorter than its diff:
```python
import functools
import math

import jax
import jax.numpy as jnp
from jax import lax
from jax.experimental import pallas as pl
from jax.experimental.pallas import tpu as pltpu
from jax.sharding import Mesh
from jax.sharding import PartitionSpec as P

HEAD_DIM = 128
ROT = 32
LANES = 128
NARROW = jnp.bfloat16
SINGLE = jnp.float32
NORM_EPSILON = 1e-05
RMS_EPSILON = 1e-06
AXES = ("chip", "core", "rep")
GROUP = ("core", "rep")
RING = ("chip", "core")
ROWS = 16
MIX_ROWS = 32
CHUNK = 512
VMEM_BYTES = 56 * 1024 * 1024
EXACT = lax.Precision.HIGHEST


def times(left, right, precision=None):
    return lax.dot_general(
        left, right, (((1,), (0,)), ((), ())), precision=precision, preferred_element_type=SINGLE
    )


def times_transposed(left, right, precision=None):
    return lax.dot_general(
        left, right, (((1,), (1,)), ((), ())), precision=precision, preferred_element_type=SINGLE
    )


def transposed_times(left, right, precision=None):
    return lax.dot_general(
        left, right, (((0,), (0,)), ((), ())), precision=precision, preferred_element_type=SINGLE
    )


def gelu_parts(values):
    cumulative = 0.5 * (1.0 + lax.erf(values * math.sqrt(0.5)))
    density = jnp.exp(-0.5 * values * values) * (1.0 / math.sqrt(2.0 * math.pi))
    return values * cumulative, cumulative + values * density


def params(*semantics):
    return pltpu.CompilerParams(vmem_limit_bytes=VMEM_BYTES)


def spec(shape, index=None):
    if index is None:
        index = lambda *i: (0,) * len(shape)
    return pl.BlockSpec(shape, index)


def scalar_spec():
    return pl.BlockSpec(memory_space=pltpu.SMEM)


def cost(flops, moved):
    return pl.CostEstimate(flops=flops // 1000, bytes_accessed=moved // 1000, transcendentals=0)


def mean(values):
    return jnp.mean(values, -1, keepdims=True)


def same_token(shape):
    row = lax.broadcasted_iota(jnp.int32, shape, 0)
    col = lax.broadcasted_iota(jnp.int32, shape, 1)
    return row == col % ROWS


def places(first, count):
    row = lax.broadcasted_iota(jnp.int32, (LANES, count * ROWS), 0)
    col = lax.broadcasted_iota(jnp.int32, (LANES, count * ROWS), 1)
    return (row == first + col // ROWS).astype(SINGLE)


def spread_out(coef, count, entries, stride):
    mask = same_token((ROWS, entries * ROWS))
    highs, lows = [], []
    for s in range(count):
        full = jnp.where(mask, times(coef, places(s * stride, entries), EXACT), 0.0)
        high = full.astype(NARROW)
        highs.append(high)
        lows.append((full - high.astype(SINGLE)).astype(NARROW))
    return jnp.concatenate(highs, 0), jnp.concatenate(lows, 0)


def draw_in(products, count, entries, stride):
    mask = same_token((ROWS, entries * ROWS))
    total = None
    for s in range(count):
        own = jnp.where(mask, products[s * ROWS : (s + 1) * ROWS], 0.0)
        term = times_transposed(own, places(s * stride, entries), EXACT)
        total = term if s == 0 else total + term
    return total


def blend_streams(hist, mix, streams):
    entries, _, width = hist.shape
    count = streams.shape[0]
    both = jnp.concatenate(spread_out(mix[...], count, entries, entries), 0)
    for start in range(0, width, CHUNK):
        sources = hist[:, :, start : start + CHUNK].reshape(entries * ROWS, CHUNK)
        total = times(both, sources)
        total = total[: count * ROWS] + total[count * ROWS :]
        streams[:, :, start : start + CHUNK] = total.reshape(count, ROWS, CHUNK)


def streams_kernel(chips, chip, hist, mix, affine, qkv, resid, last, streams):
    width = hist.shape[2]
    blend_streams(hist, mix, streams)
    for s in range(4):
        values = streams[s]
        center = values - mean(values)
        row = 0 if s < 3 else 2
        normed = (
            center * lax.rsqrt(mean(center * center) + NORM_EPSILON) * affine[row : row + 1]
            + affine[row + 1 : row + 2]
        )
        if s < 3:
            qkv[s] = normed.astype(NARROW)
        else:
            last[...] = values
            streams[0] = normed
    part = width // chips
    for m in range(chips):
        start = pl.multiple_of((chip[0] ^ m) * part, part)
        resid[:, m * part : (m + 1) * part] = streams[0, :, pl.ds(start, part)].astype(NARROW)


def history_dots_kernel(hist, cot, weight, out):
    entries, rows, width = hist.shape
    count = cot.shape[0]
    products = times_transposed(
        cot[...].reshape(count * rows, width), hist[...].reshape(entries * rows, width)
    )
    out[...] = draw_in(products, count, entries, entries + 1) * weight[...]


def mix_kernel(
    chips,
    near,
    rep,
    entries,
    chip,
    last,
    attn_own,
    *refs,
):
    attn_rest, mlp_parts, refs = refs[:near], refs[near : near + rep], refs[near + rep :]
    mix_body(chips, entries, chip, last, attn_own, attn_rest, mlp_parts, *refs)


def mix_body(
    chips,
    entries,
    chip,
    last,
    attn_own,
    attn_rest,
    mlp_parts,
    branch_bias,
    gain,
    first,
    first_bias,
    second,
    second_bias,
    cot,
    weight,
    dots,
    entry_out,
    grad_out,
    grad_low,
    grad_turned,
    scaled_out,
    grad_pre_low,
    act_out,
    grad_coef_out,
    coef_out,
    grad_gain,
    grad_bias,
    grad_pre_sum,
    grad_coef_sum,
    turned,
):
    rows, width = last.shape
    count = cot.shape[0]
    entry = last[...] + attn_own[...] + branch_bias[...]
    for part in attn_rest:
        entry = entry + part[...].astype(SINGLE)
    total = mlp_parts[0][...].astype(SINGLE)
    for values in mlp_parts[1:]:
        total = total + values[...].astype(SINGLE)
    part = width // chips
    for m in range(chips):
        start = pl.multiple_of((chip[0] ^ m) * part, part)
        turned[:, pl.ds(start, part)] = total[:, m * part : (m + 1) * part]
    entry = entry + turned[...]
    entry_out[...] = entry
    scale = lax.rsqrt(mean(entry * entry) + RMS_EPSILON)
    scaled = (entry * scale * gain[...]).astype(NARROW)
    scaled_out[...] = scaled
    pre = times(scaled, first[...]) + first_bias[...]
    act, slope = gelu_parts(pre)
    act_out[...] = act
    coef = times(act, second[...], EXACT) + second_bias[...]
    coef_out[...] = coef
    lane = lax.broadcasted_iota(jnp.int32, (rows, LANES), 1)
    grad_coef = dots[...]
    grad = jnp.zeros((rows, width), SINGLE)
    for s in range(count):
        arriving = cot[s].astype(SINGLE)
        place = s * (entries + 1) + entries
        total = jnp.sum(arriving * entry, -1, keepdims=True) * weight[...]
        grad_coef = jnp.where(lane == place, total, grad_coef)
        grad = grad + (coef[:, place : place + 1] * weight[...]) * arriving
    grad_coef_out[...] = grad_coef
    grad_pre = slope * times_transposed(grad_coef, second[...], EXACT)
    grad_pre_narrow = grad_pre.astype(NARROW)
    grad_pre_low[...] = grad_pre_narrow
    grad_scaled = times_transposed(grad_pre_narrow, first[...])
    gained = grad_scaled * gain[...]
    grad = grad + scale * gained - entry * (scale * scale * scale * mean(gained * entry))
    grad_out[...] = grad
    grad_low[...] = grad.astype(NARROW)
    for m in range(chips):
        start = pl.multiple_of((chip[0] ^ m) * part, part)
        grad_turned[:, m * part : (m + 1) * part] = grad_out[:, pl.ds(start, part)].astype(NARROW)

    @pl.when(pl.program_id(0) == 0)
    def _():
        grad_gain[...] = jnp.zeros_like(grad_gain)
        grad_bias[...] = jnp.zeros_like(grad_bias)
        grad_pre_sum[...] = jnp.zeros_like(grad_pre_sum)
        grad_coef_sum[...] = jnp.zeros_like(grad_coef_sum)

    grad_gain[...] += jnp.sum(grad_scaled * entry * scale, 0, keepdims=True)
    grad_bias[...] += jnp.sum(grad, 0, keepdims=True)
    grad_pre_sum[...] += jnp.sum(grad_pre, 0, keepdims=True)
    grad_coef_sum[...] += jnp.sum(grad_coef, 0, keepdims=True)


def next_kernel(hist, entry, coef, out):
    entries, _, width = hist.shape
    count = out.shape[0]
    both = jnp.concatenate(spread_out(coef[...], count, entries, entries + 1), 0)
    for start in range(0, width, CHUNK):
        cols = slice(start, start + CHUNK)
        sources = hist[:, :, cols].reshape(entries * ROWS, CHUNK)
        total = times(both, sources)
        total = total[: count * ROWS] + total[count * ROWS :]
        for s in range(count):
            place = s * (entries + 1) + entries
            out[s, :, cols] = (
                total[s * ROWS : (s + 1) * ROWS] + coef[:, place : place + 1] * entry[:, cols]
            ).astype(NARROW)


def close_kernel(
    chips,
    near,
    rep,
    chip,
    hist,
    cot,
    coef,
    weight,
    mix,
    affine,
    grad_entry,
    qkv_own,
    *refs,
):
    qkv_rest, resid, refs = refs[:near], refs[near : near + rep], refs[near + rep :]
    close_body(
        chips, chip, hist, cot, coef, weight, mix, affine, grad_entry, resid, qkv_own, qkv_rest, *refs
    )


def close_body(
    chips,
    chip,
    hist,
    cot,
    coef,
    weight,
    mix,
    affine,
    grad_entry,
    resid,
    qkv_own,
    qkv_rest,
    grad_hist,
    grad_mix,
    grad_affine,
    streams,
    turned,
    stacked,
):
    entries, rows, width = hist.shape
    count = cot.shape[0]
    part = width // chips

    @pl.when(pl.program_id(0) == 0)
    def _():
        grad_affine[...] = jnp.zeros_like(grad_affine)

    blend_streams(hist, mix, streams)
    for s in range(count):
        values = streams[s]
        center = values - mean(values)
        scale = lax.rsqrt(mean(center * center) + NORM_EPSILON)
        unit = center * scale
        if s < 3:
            arriving = qkv_own[s]
            for rest in qkv_rest:
                arriving = arriving + rest[s].astype(SINGLE)
        else:
            total = resid[0][...].astype(SINGLE)
            for rest in resid[1:]:
                total = total + rest[...].astype(SINGLE)
            for m in range(chips):
                start = pl.multiple_of((chip[0] ^ m) * part, part)
                turned[:, pl.ds(start, part)] = total[:, m * part : (m + 1) * part]
            arriving = turned[...]
        row = 0 if s < 3 else 2
        grad_affine[row : row + 1] += jnp.sum(arriving * unit, 0, keepdims=True)
        grad_affine[row + 1 : row + 2] += jnp.sum(arriving, 0, keepdims=True)
        gained = arriving * affine[row : row + 1]
        grad = scale * (gained - mean(gained) - unit * mean(gained * unit))
        streams[s] = grad if s < 3 else grad + grad_entry[...]
    size = count * rows
    grads = streams[...].reshape(size, width)
    high = grads.astype(NARROW)
    stacked[0:size] = high
    stacked[size : 2 * size] = (grads - high.astype(SINGLE)).astype(NARROW)
    stacked[2 * size : 3 * size] = high
    arriving = cot[...].reshape(size, width)
    stacked[3 * size : 4 * size] = arriving
    stacked[4 * size : 5 * size] = arriving
    mix_high, mix_low = spread_out(mix[...], count, entries, entries)
    out_high, out_low = spread_out(coef[...] * weight[...], count, entries, entries + 1)
    spread = jnp.concatenate([mix_high, mix_high, mix_low, out_high, out_low], 0)
    products = jnp.zeros((2 * size, entries * rows), SINGLE)
    for start in range(0, width, CHUNK):
        cols = slice(start, start + CHUNK)
        grad_hist[:, :, cols] = transposed_times(spread, stacked[:, cols]).reshape(
            entries, rows, CHUNK
        )
        sources = hist[:, :, cols].reshape(entries * rows, CHUNK)
        products = products + times_transposed(stacked[0 : 2 * size, cols], sources)
    products = products[:size] + products[size:]
    grad_mix[...] = draw_in(products, count, entries, entries)[:, : grad_mix.shape[1]]


def turn(values, rope, sign):
    forward = pltpu.roll(values, HEAD_DIM - ROT // 2, 1)
    backward = pltpu.roll(values, ROT // 2, 1)
    return values * rope[0] + sign * (forward * rope[1] + backward * rope[2])


def allowed_pairs(row, column, length):
    query = lax.broadcasted_iota(jnp.int32, (length, length), 0)
    key = lax.broadcasted_iota(jnp.int32, (length, length), 1)
    return (key <= query) & (row == column)


def probabilities(query, key, allowed):
    scores = jnp.where(allowed, times_transposed(query, key) * HEAD_DIM ** (-0.5), -1e30)
    raised = jnp.exp(scores - jnp.max(scores, -1, keepdims=True))
    return raised / jnp.sum(raised, -1, keepdims=True)


def attend_kernel(own, other, weight, bias, rope, doc_row, doc_column, qkv, mixed, out_own, out_other):
    _, length, _ = own.shape
    cols = bias.shape[1] // 3
    for i in range(3):
        tokens = jnp.concatenate([own[i], other[i]], 0)
        linear = times(tokens, weight[:, i * cols : (i + 1) * cols]) + bias[:, i * cols : (i + 1) * cols]
        if i == 2:
            qkv[i] = linear.astype(NARROW)
            continue
        for s in range(2):
            for start in range(0, cols, HEAD_DIM):
                piece = linear[s * length : (s + 1) * length, start : start + HEAD_DIM]
                qkv[i, s * length : (s + 1) * length, start : start + HEAD_DIM] = turn(
                    piece, rope, 1.0
                ).astype(NARROW)
    for s in range(2):
        allowed = allowed_pairs(doc_row[s], doc_column[s], length)
        rows = slice(s * length, (s + 1) * length)
        for start in range(0, cols, HEAD_DIM):
            head = slice(start, start + HEAD_DIM)
            probs = probabilities(qkv[0, rows, head], qkv[1, rows, head], allowed)
            mixed[rows, head] = times(probs.astype(NARROW), qkv[2, rows, head]).astype(NARROW)
    result = times_transposed(mixed[...], weight[:, 3 * cols :])
    out_own[...] = result[:length]
    out_other[...] = result[length:].astype(NARROW)


def attend_back_kernel(
    own, other, weight, qkv, rope, doc_row, doc_column, grad_linear, grad_bias, out_own, out_other
):
    length = own.shape[0]
    cols = qkv.shape[2]
    scale = HEAD_DIM ** (-0.5)
    arriving = jnp.concatenate([own[...], other[...]], 0)
    grad_mixed = times(arriving, weight[:, 3 * cols :]).astype(NARROW)
    for start in range(0, cols, HEAD_DIM):
        head = slice(start, start + HEAD_DIM)
        sums = [jnp.zeros((1, HEAD_DIM), SINGLE) for _ in range(3)]
        for s in range(2):
            allowed = allowed_pairs(doc_row[s], doc_column[s], length)
            rows = slice(s * length, (s + 1) * length)
            query, key, value = (qkv[i, rows, head] for i in range(3))
            grad = grad_mixed[rows, head]
            probs = probabilities(query, key, allowed)
            grad_value = transposed_times(probs.astype(NARROW), grad)
            grad_probs = times_transposed(grad, value)
            inner = jnp.sum(probs * grad_probs, -1, keepdims=True)
            grad_scores = (probs * (grad_probs - inner)).astype(NARROW)
            grad_query = turn(times(grad_scores, key) * scale, rope, -1.0)
            grad_key = turn(transposed_times(grad_scores, query) * scale, rope, -1.0)
            for i, values in enumerate((grad_query, grad_key, grad_value)):
                sums[i] = sums[i] + jnp.sum(values, 0, keepdims=True)
                grad_linear[i, rows, head] = values.astype(NARROW)
        for i in range(3):
            grad_bias[:, i * cols + start : i * cols + start + HEAD_DIM] = sums[i]
    for i in range(3):
        result = times_transposed(grad_linear[i], weight[:, i * cols : (i + 1) * cols])
        out_own[i] = result[:length]
        out_other[i] = result[length:].astype(NARROW)


def heads_grad_kernel(chips, *refs):
    norms, branches = refs[: 2 * chips], refs[2 * chips : 4 * chips]
    linears, mixeds, out = refs[4 * chips : 5 * chips], refs[5 * chips : 6 * chips], refs[6 * chips]
    cols = mixeds[0].shape[1]
    rep, _, rows, _ = out.shape
    for i in range(4):
        total = None
        for m in range(chips):
            sides = norms[2 * m : 2 * m + 2] if i < 3 else branches[2 * m : 2 * m + 2]
            left = jnp.concatenate([values[i] if i < 3 else values[...] for values in sides], 0)
            right = linears[m][i] if i < 3 else mixeds[m][...]
            term = transposed_times(left, right)
            total = term if total is None else total + term
        total = total.astype(NARROW)
        for k in range(rep):
            out[k, 0, :, i * cols : (i + 1) * cols] = total[k * rows : (k + 1) * rows]


def hidden_kernel(chips, tokens, *refs):
    weights, (bias, act_out, slope_out) = refs[:chips], refs[chips:]
    part = weights[0].shape[1]
    total = bias[...]
    for m in range(chips):
        total = total + times(tokens[:, m * part : (m + 1) * part], weights[m][0])
    act, slope = gelu_parts(total)
    act_out[...] = act.astype(NARROW)
    slope_out[...] = slope


def put_places(outs, length, cols, result):
    many = result.shape[0] // length
    for k, out in enumerate(outs):

        @pl.when(pl.program_id(0) == k // many)
        def _():
            out[:, cols] = result[(k % many) * length : (k % many + 1) * length].astype(NARROW)


def branch_kernel(chips, merged, act, *refs):
    weights, refs = refs[:chips], refs[chips:]
    part = weights[0].shape[1]
    for m in range(chips):
        cols = slice(m * part, (m + 1) * part)
        result = times_transposed(act[...], weights[m][0])
        if merged:
            put_places(refs[1:], refs[1].shape[0], cols, result + refs[0][:, cols].astype(SINGLE))
        else:
            refs[0][:, cols] = result.astype(NARROW)


def hidden_back_kernel(chips, merged, grad, slope, *refs):
    firsts, seconds, refs = refs[:chips], refs[chips : 2 * chips], refs[2 * chips :]
    came, refs = (refs[0], refs[1:]) if merged else (None, refs)
    grad_low, grad_sum, *outs = refs
    part = firsts[0].shape[1]
    total = None
    for m in range(chips):
        term = times(grad[:, m * part : (m + 1) * part], seconds[m][0])
        total = term if m == 0 else total + term
    total = total * slope[...]

    @pl.when(pl.program_id(0) == 0)
    def _():
        grad_sum[...] = jnp.zeros_like(grad_sum)

    grad_sum[...] += jnp.sum(total, 0, keepdims=True)
    low = total.astype(NARROW)
    grad_low[...] = low
    for m in range(chips):
        cols = slice(m * part, (m + 1) * part)
        result = times_transposed(low, firsts[m][0])
        if merged:
            put_places(outs, outs[0].shape[0], cols, result + came[:, cols].astype(SINGLE))
        else:
            outs[0][:, cols] = result.astype(NARROW)


def outer_kernel(left_own, left_other, right_own, right_other, *outs):
    result = (
        transposed_times(left_own[...], right_own[...])
        + transposed_times(left_other[...], right_other[...])
    ).astype(NARROW)
    for m, out in enumerate(outs):

        @pl.when(pl.program_id(0) == m)
        def _():
            out[...] = result


def merge_kernel(first, count, own, came, *refs):
    total = own[...] + came[...].astype(SINGLE)
    refs[-1][...] = total.astype(NARROW)
    if len(refs) > 1:

        @pl.when((pl.program_id(0) >= first) & (pl.program_id(0) < first + count))
        def _():
            refs[-1][...] = (total + refs[0][...].astype(SINGLE)).astype(NARROW)


def pack_hidden_kernel(rep, line, first, second, *outs):
    cols = outs[0].shape[3]
    for k in range(rep):
        for c in range(2):
            start = pl.multiple_of((c * rep + (line[0] ^ k)) * cols, cols)
            outs[k][c, 0] = first[:, pl.ds(start, cols)].astype(NARROW)
            outs[k][c, 1] = second[:, pl.ds(start, cols)].astype(NARROW)


def join_hidden_kernel(rep, core, line, swapped, *refs):
    owns, out = refs[:rep], refs[rep]
    for k in range(rep):
        for i in range(2):
            out[i, core[0], line[0] ^ k] = owns[k][core[0], i]
            out[i, 1 - core[0], line[0] ^ k] = swapped[k, i]


def pack_heads_kernel(query, key, value, out_weight, out):
    cols = query.shape[1]
    for i, weight in enumerate((query, key, value, out_weight)):
        out[0, :, i * cols : (i + 1) * cols] = weight[...].astype(NARROW)


class Order:
    def __init__(self, legal):
        self.legal = legal
        self.last = ()

    def hold(self, *values):
        tied = lax.optimization_barrier(tuple(values) + self.last)[: len(values)]
        return tied[0] if len(values) == 1 else tied

    def wait(self, *values):
        tied = lax.optimization_barrier(tuple(values) + self.last)[: len(values)]
        self.last = (tied[0],)
        return tied[0] if len(values) == 1 else list(tied)

    def scope(self, steps):
        inside = lambda: steps(Order(self.legal))
        shapes = jax.eval_shape(inside)
        never = lambda: jax.tree.map(lambda leaf: jnp.zeros(leaf.shape, leaf.dtype), shapes)
        results = lax.cond(self.hold(self.legal), inside, never)
        smallest = min(jax.tree.leaves(results), key=lambda leaf: leaf.size)
        self.last = (smallest,)
        return results


def on_device(
    chips,
    rep,
    history,
    mix_in,
    doc_ids,
    doc_group,
    group_weight,
    norm_gain,
    norm_bias,
    w_qkv,
    b_qkv,
    w_out,
    b_out,
    w_fc1,
    b_fc1,
    w_fc2,
    b_fc2,
    w_mix1,
    b_mix1,
    w_mix2,
    b_mix2,
    cotangent,
):
    entries, length, width = history.shape
    count = cotangent.shape[0]
    rows = w_qkv.shape[0]
    hidden = w_fc1.shape[1]
    hid = b_mix1.shape[0]
    mixes = b_mix2.shape[0]
    fsdp = 2 * chips
    group = 2 * rep
    devices = fsdp * rep
    cols = width // fsdp
    hid_cols = hidden // group
    part = width // chips
    chip = lax.axis_index("chip")
    core = lax.axis_index("core")
    line = lax.axis_index("rep")
    chip_at = chip.astype(jnp.int32).reshape(1)
    core_at = core.astype(jnp.int32).reshape(1)
    line_at = line.astype(jnp.int32).reshape(1)
    shape = jax.ShapeDtypeStruct

    def swap_core(values):
        return lax.ppermute(values, "core", [(0, 1), (1, 0)])

    def hop_chip(values, m):
        return lax.ppermute(values, "chip", [(i, i ^ m) for i in range(chips)])

    def hop_rep(values, k):
        return lax.ppermute(values, "rep", [(i, i ^ k) for i in range(rep)])

    def merge(own, came):
        return (own.astype(SINGLE) + came.astype(SINGLE)).astype(NARROW)

    def pieces(values, axis):
        size = values.shape[axis] // 2
        return (
            lax.slice_in_dim(values, 0, size, axis=axis),
            lax.slice_in_dim(values, size, 2 * size, axis=axis),
        )

    square = chips == 4
    around = range(1, 3 if square else chips)
    far = chips - 1

    def pass_on(first, axis):
        if not square:
            return ()
        return hop_chip(pieces(first[0], axis)[0], 2), hop_chip(pieces(first[1], axis)[1], 1)

    def joined_halves(halves, axis):
        return [jnp.concatenate(halves, axis)] if square else []

    def send_far(far, axis):
        if not square:
            return ()
        upper, lower = pieces(far, axis)
        return hop_chip(upper, 1), hop_chip(lower, 2)

    def take_along(terms, halves, axis):
        if not square:
            return terms
        upper, lower = halves
        near = pieces(terms[0], axis)
        far = pieces(terms[1], axis)
        return [
            jnp.concatenate([near[0], merge(near[1], lower)], axis),
            jnp.concatenate([merge(far[0], upper), far[1]], axis),
        ]

    order = Order(doc_ids[0, 0] >= 0)
    steps = length // ROWS
    block = 256
    blocks = rep * length // block
    tall = lambda n: spec((n, ROWS, width), lambda i: (0, i, 0))
    flat = lambda n: spec((ROWS, n), lambda i: (i, 0))
    tall2 = lambda n: spec((n, MIX_ROWS, width), lambda i: (0, i, 0))
    flat2 = lambda n: spec((MIX_ROWS, n), lambda i: (i, 0))
    token_block = lambda n: spec((block, n), lambda i: (i, 0))
    weight_specs = lambda which: [spec((1, part, hid_cols), lambda *_: (which, 0, 0))] * (
        3 if square else chips
    ) + [spec((1, part, hid_cols))] * square
    in_vmem = pl.BlockSpec(memory_space=pltpu.VMEM)

    small = (norm_gain, norm_bias, b_qkv, b_out, b_fc1, b_fc2, doc_ids)
    packed = jnp.concatenate([values.reshape(-1).astype(NARROW) for values in small])
    packed = order.wait(jnp.broadcast_to(packed[None], (devices, packed.shape[0])))
    gathered = lax.all_to_all(packed, AXES, 0, 0, tiled=True)
    hidden_sends = pl.pallas_call(
        functools.partial(pack_hidden_kernel, rep),
        in_specs=[scalar_spec()] + [in_vmem] * 2,
        out_shape=[shape((2, 2, rows, hid_cols), NARROW)] * rep,
        compiler_params=params(),
        cost_estimate=cost(10**6, 6 * 10**6),
        name="pack_hidden",
    )(line_at, *order.hold(w_fc1, w_fc2))
    hidden_sends = order.wait(*hidden_sends)
    head_block = lambda i: spec((rows, cols), lambda j: (0, i * fsdp + j))
    from_qkv, from_out = order.hold(w_qkv, w_out)
    heads_sends = pl.pallas_call(
        pack_heads_kernel,
        grid=(fsdp,),
        in_specs=[head_block(0), head_block(1), head_block(2), head_block(0)],
        out_specs=spec((1, rows, 4 * cols), lambda j: (j, 0, 0)),
        out_shape=shape((fsdp, rows, 4 * cols), NARROW),
        compiler_params=params(),
        cost_estimate=cost(10**6, 3 * 10**6),
        name="pack_heads",
    )(from_qkv, from_qkv, from_qkv, from_out)
    heads_sends = order.wait(heads_sends)
    mix_padded = order.wait(jnp.pad(mix_in, ((0, 0), (0, LANES - count * entries))))
    gathered = order.wait(gathered)
    heads_came = lax.all_to_all(order.hold(heads_sends), RING, 0, 0, tiled=True)
    hidden_going = order.hold(*hidden_sends)
    hidden_hops = [hop_rep(hidden_going[k], k) for k in range(1, rep)]

    def fields_of(gathered):
        fields, start = [], 0
        for values in small:
            fields.append(gathered[:, start : start + values.size])
            start += values.size
        return fields

    def open_layer(inner):
        fields = fields_of(gathered)
        gains = fields[0].reshape(devices, 3, rows).transpose(1, 0, 2).reshape(3, width)
        shifts = fields[1].reshape(devices, 2, rows).transpose(1, 0, 2).reshape(2, width)
        affine = jnp.stack([gains[0], shifts[0], gains[1], shifts[1]]).astype(SINGLE)
        normed = pl.pallas_call(
            functools.partial(streams_kernel, chips),
            grid=(steps,),
            in_specs=[scalar_spec(), tall(entries), flat(LANES), spec((4, width))],
            out_specs=[tall(3), flat(width), flat(width)],
            out_shape=[
                shape((3, length, width), NARROW),
                shape((length, width), NARROW),
                shape((length, width), SINGLE),
            ],
            scratch_shapes=[pltpu.VMEM((count, ROWS, width), SINGLE)],
            compiler_params=params(),
            cost_estimate=cost(10**8, 10**7),
            name="streams",
        )(chip_at, history, mix_padded, affine)
        normed = inner.wait(*normed)
        qkv_near = [hop_chip(normed[0], m) for m in around]
        documents, group_of, weight_of = inner.hold(doc_ids[0], doc_group[0], group_weight)
        doc_match = documents[:, None] == jnp.arange(doc_group.shape[1], dtype=jnp.int32)[None, :]
        token_group = jnp.sum(jnp.where(doc_match, group_of[None, :], 0), axis=1)
        group_match = (
            token_group[:, None] == jnp.arange(group_weight.shape[0], dtype=jnp.int32)[None, :]
        )
        token_weight = jnp.sum(jnp.where(group_match, weight_of[None, :], 0.0), 1, keepdims=True)
        dots = pl.pallas_call(
            history_dots_kernel,
            grid=(steps,),
            in_specs=[tall(entries), tall(count), flat(1)],
            out_specs=flat(LANES),
            out_shape=shape((length, LANES), SINGLE),
            compiler_params=params(),
            cost_estimate=cost(10**8, 10**7),
            name="history_dots",
        )(history, cotangent, token_weight)
        dots = inner.wait(dots)
        return normed, affine, dots, token_weight, inner.wait(*qkv_near)

    normed, affine, dots, token_weight, qkv_near = order.scope(open_layer)
    qkv_norm, resid_norm, last = normed
    heads_came = order.wait(heads_came)
    hidden_came = [hidden_sends[0], *order.wait(*hidden_hops)]

    first_mix = order.hold(w_mix1).astype(NARROW).reshape(1, -1)
    first_mix = order.wait(jnp.broadcast_to(first_mix, (devices, rows * hid)))
    first_mix = lax.all_to_all(first_mix, AXES, 0, 0, tiled=True)
    resid_norm = order.hold(resid_norm)
    resid_hops = [hop_rep(resid_norm, k) for k in range(1, rep)]

    def join_hidden(inner):
        for_other = jnp.stack(
            [lax.dynamic_index_in_dim(values, 1 - core, 0, False) for values in hidden_came]
        )
        joined = pl.pallas_call(
            functools.partial(join_hidden_kernel, rep),
            in_specs=[scalar_spec()] * 2 + [in_vmem] * (rep + 1),
            out_shape=shape((2, 2, rep, rows, hid_cols), NARROW),
            compiler_params=params(),
            cost_estimate=cost(10**6, 5 * 10**6),
            name="join_hidden",
        )(core_at, line_at, swap_core(for_other), *hidden_came)
        return joined.reshape(2, part, hid_cols)

    def prepare(inner):
        fields = fields_of(inner.hold(gathered))
        gain = fields[0].reshape(devices, 3, rows)[:, 2].reshape(1, width).astype(SINGLE)
        qkv_bias = fields[2].reshape(3, fsdp, cols).astype(SINGLE)
        branch_bias = fields[3].reshape(1, width).astype(SINGLE)
        branch_bias = branch_bias + fields[5].reshape(1, width).astype(SINGLE)
        first_bias = fields[4].reshape(group, hid_cols).astype(SINGLE)
        docs_all = fields[6].reshape(chips, 2, rep, length)
        my_qkv_bias = lax.dynamic_index_in_dim(qkv_bias, chip * 2 + core, 1, False)
        my_first_bias = lax.dynamic_index_in_dim(first_bias, core * rep + line, 0, True)
        docs_line = lax.dynamic_index_in_dim(docs_all, line, 2, False).astype(SINGLE)
        doc_rows = []
        for m in range(chips):
            pair = lax.dynamic_index_in_dim(docs_line, chip ^ m, 0, False)
            doc_rows.append(jnp.where(core == 0, pair, pair[::-1]))
        position = jnp.arange(length).astype(SINGLE)
        frequency = 10000.0 ** (-jnp.arange(0, ROT, 2).astype(SINGLE) / ROT)
        angle = position[:, None] * frequency[None, :]
        cosine, sine = jnp.cos(angle), jnp.sin(angle)
        nothing = jnp.zeros_like(sine)
        rest = HEAD_DIM - ROT
        rope = jnp.stack(
            [
                jnp.concatenate([cosine, cosine, jnp.ones((length, rest), SINGLE)], 1),
                jnp.concatenate([-sine, nothing, jnp.zeros((length, rest), SINGLE)], 1),
                jnp.concatenate([nothing, sine, jnp.zeros((length, rest), SINGLE)], 1),
            ]
        )
        pairs = [(pair[:, None, :], pair[:, :, None]) for pair in doc_rows]
        ready = (gain, my_qkv_bias.reshape(1, 3 * cols), my_first_bias, branch_bias, rope, pairs)
        leaves, tree = jax.tree.flatten(ready)
        return jax.tree.unflatten(tree, inner.wait(*leaves))

    def spread_weights(inner):
        joined = inner.scope(join_hidden)
        near = [hop_chip(joined, m) for m in around]
        prepared = inner.scope(prepare)
        near = inner.wait(*near)
        return joined, near, prepared

    hidden_own, hidden_near, prepared = order.scope(spread_weights)
    gain, my_qkv_bias, my_first_bias, branch_bias, rope, doc_pairs = prepared
    resid_hops = order.wait(*resid_hops)
    first_mix = order.wait(first_mix)

    heads_all = lax.all_gather(order.hold(heads_came), "rep", axis=0)

    def hidden_side(firsts, tokens):
        return pl.pallas_call(
            functools.partial(hidden_kernel, chips),
            grid=(blocks,),
            in_specs=[token_block(width)] + weight_specs(0) + [spec((1, hid_cols))],
            out_specs=[token_block(hid_cols)] * 2,
            out_shape=[
                shape((rep * length, hid_cols), NARROW),
                shape((rep * length, hid_cols), SINGLE),
            ],
            compiler_params=params(),
            cost_estimate=cost(2 * rep * length * width * hid_cols, 10**7),
            name="hidden",
        )(tokens, *firsts, my_first_bias)

    side = shape((rep * length, width), NARROW)
    places = [shape((length, width), NARROW)] * rep
    place_specs = [spec((length, width))] * rep

    def branch_side(seconds, act, *came):
        return pl.pallas_call(
            functools.partial(branch_kernel, chips, bool(came)),
            grid=(blocks,),
            in_specs=[token_block(hid_cols)] + weight_specs(1) + [token_block(width)] * len(came),
            out_specs=place_specs if came else token_block(width),
            out_shape=places if came else side,
            compiler_params=params(),
            cost_estimate=cost(2 * rep * length * width * hid_cols, 10**7),
            name="branch",
        )(act, *seconds, *came)


    qkv_first = [qkv_norm, *qkv_near]

    def feed_forward(inner):
        ends = []
        mix_first = jnp.pad(inner.hold(first_mix).reshape(width, hid), ((0, 0), (0, LANES - hid)))
        if square:
            upper = hop_chip(inner.hold(hidden_near[0])[0:1], 2)
            lower = hop_chip(inner.hold(hidden_near[1])[1:2], 1)
        whole = inner.wait(jnp.stack([resid_norm, *resid_hops]))
        other = inner.wait(swap_core(whole))
        qkv_other = inner.scope(lambda _: [swap_core(values) for values in qkv_first])
        mix_first = inner.wait(mix_first)
        if square:
            ends = inner.wait(upper, lower)
            halves = pass_on(inner.hold(*qkv_near), 1)
        firsts = [hidden_own, *hidden_near, *ends[:1]]
        seconds = [hidden_own, *hidden_near, *ends[1:]]
        sides = [values.reshape(rep * length, width) for values in (whole, other)]
        act_other, slope_other = inner.wait(*hidden_side(firsts, inner.hold(sides[1])))

        def branch_both(inner):
            back = inner.wait(branch_side(seconds, act_other))
            came = swap_core(back)
            act_own, slope_own = inner.wait(*hidden_side(firsts, inner.hold(sides[0])))
            return act_own, slope_own, branch_side(seconds, act_own, inner.wait(came))

        act_own, slope_own, branch_places = inner.scope(branch_both)
        qkv_last = []
        if square:
            qkv_last.append(inner.wait(jnp.concatenate(inner.wait(*halves), 1)))
            qkv_other.append(inner.wait(swap_core(qkv_last[0])))
        acts, slopes = (act_own, act_other), (slope_own, slope_other)
        return ends, sides, acts, slopes, branch_places, qkv_last, qkv_other, mix_first

    ends, resid_sides, acts, slopes, branch_places, qkv_last, qkv_other, mix_first = order.scope(
        feed_forward
    )
    first_parts = [hidden_own, *hidden_near, *ends[:1]]
    second_parts = [hidden_own, *hidden_near, *ends[1:]]
    qkv_own = [*qkv_first, *qkv_last]
    heads_all = order.wait(heads_all)

    branch_places = order.hold(*branch_places)
    mlp_hops = [hop_rep(branch_places[k], k) for k in range(1, rep)]

    def attend(heads, own, other, m):
        return pl.pallas_call(
            attend_kernel,
            out_shape=[
                shape((3, 2 * length, cols), NARROW),
                shape((2 * length, cols), NARROW),
                shape((length, width), SINGLE),
                shape((length, width), NARROW),
            ],
            compiler_params=params(),
            cost_estimate=cost(4 * 2 * 2 * length * width * cols, 8 * 10**6),
            name="attend",
        )(own, other, heads, my_qkv_bias, rope, *doc_pairs[m])


    def add_up(own, came, first=0, *along):
        rows_of = 32
        half = length // 2 // rows_of
        block_of = lambda index: spec((3, rows_of, width), index)
        return pl.pallas_call(
            functools.partial(merge_kernel, first, half),
            grid=(2 * half,),
            in_specs=[block_of(lambda i: (0, i, 0))] * 2
            + [block_of(lambda i: (0, jnp.clip(i - first, 0, half - 1), 0))] * len(along),
            out_specs=block_of(lambda i: (0, i, 0)),
            out_shape=shape(own.shape, NARROW),
            compiler_params=params(),
            cost_estimate=cost(10**6, 10**7),
            name="merge",
        )(own, came, *along)

    def near_sums(inner, results, came, halves):
        terms = []
        for m in around:
            along = ()
            if square:
                along = (length // 2 // 32, halves[1]) if m == 1 else (0, halves[0])
            terms.append(inner.wait(add_up(results[m], came[m], *along)))
        return terms

    def attention(inner):
        heads = inner.wait(heads_all.transpose(1, 0, 2, 3).reshape(width, 4 * cols))
        results, came = [None] * chips, [None] * chips

        def step(m):
            own, other = inner.hold(qkv_own[m], qkv_other[m])
            results[m] = inner.wait(*attend(heads, own, other, m))

        step(far)
        came[far] = swap_core(inner.hold(results[far][3]))
        step(1)
        came[far] = inner.wait(came[far])
        halves = None
        if square:
            halves = send_far(inner.wait(merge(results[far][2], came[far])), 0)
        for m in range(2, far):
            step(m)
        if square:
            halves = inner.wait(*halves)
        middle = range(1, far)
        swapped = inner.wait(swap_core(inner.wait(jnp.stack([results[m][3] for m in middle]))))
        for m in middle:
            came[m] = swapped[m - 1]
        terms = [merge(results[m][2], came[m]) for m in around]
        terms = inner.wait(*take_along(terms, halves, 0))
        hops = [hop_chip(terms[m - 1], m) for m in around]
        step(0)
        hops = inner.wait(*hops)
        came[0] = inner.wait(swap_core(inner.hold(results[0][3])))
        lows = [values[0] for values in results]
        return heads, lows, [values[1] for values in results], results[0][2], [came[0], *hops]

    heads, qkv_low, mixed_low, attn_own, attn_rest = order.scope(attention)
    mlp_parts = [branch_places[0], *order.wait(*mlp_hops)]

    mix_second = jnp.pad(w_mix2, ((0, LANES - hid), (0, LANES - mixes)))
    mixed_results = pl.pallas_call(
        functools.partial(mix_kernel, chips, len(attn_rest), rep, entries),
        grid=(length // MIX_ROWS,),
        in_specs=[
            scalar_spec(),
            flat2(width),
            flat2(width),
            *[flat2(width)] * (len(attn_rest) + rep),
            spec((1, width)),
            spec((1, width)),
            spec((width, LANES)),
            spec((1, LANES)),
            spec((LANES, LANES)),
            spec((1, LANES)),
            tall2(count),
            flat2(1),
            flat2(LANES),
        ],
        out_specs=[flat2(width)] * 5
        + [flat2(LANES)] * 4
        + [spec((1, width))] * 2
        + [spec((1, LANES))] * 2,
        out_shape=[
            shape((length, width), SINGLE),
            shape((length, width), SINGLE),
            shape((length, width), NARROW),
            shape((length, width), NARROW),
            shape((length, width), NARROW),
            shape((length, LANES), NARROW),
            shape((length, LANES), SINGLE),
            shape((length, LANES), SINGLE),
            shape((length, LANES), SINGLE),
            shape((1, width), SINGLE),
            shape((1, width), SINGLE),
            shape((1, LANES), SINGLE),
            shape((1, LANES), SINGLE),
        ],
        scratch_shapes=[pltpu.VMEM((MIX_ROWS, width), SINGLE)],
        compiler_params=params(),
        cost_estimate=cost(2 * 10**8, 10**7),
        name="mixing",
    )(
        chip_at,
        last,
        attn_own,
        *attn_rest,
        *mlp_parts,
        branch_bias,
        gain,
        mix_first,
        jnp.pad(b_mix1, (0, LANES - hid))[None],
        mix_second,
        jnp.pad(b_mix2, (0, LANES - mixes))[None],
        cotangent,
        token_weight,
        dots,
    )
    (
        entry,
        grad_entry,
        grad_low,
        grad_turned,
        scaled_low,
        grad_pre_low,
        mix_act,
        grad_coef,
        coef,
        grad_rms_gain,
        grad_branch_bias,
        grad_pre_sum,
        grad_coef_sum,
    ) = order.wait(*mixed_results)

    grad_hops = [hop_rep(grad_turned, k) for k in range(1, rep)]

    def attend_back(own, other, heads, qkv, rope, pair):
        return pl.pallas_call(
            attend_back_kernel,
            out_shape=[
                shape((3, 2 * length, cols), NARROW),
                shape((1, 3 * cols), SINGLE),
                shape((3, length, width), SINGLE),
                shape((3, length, width), NARROW),
            ],
            compiler_params=params(),
            cost_estimate=cost(4 * 2 * 2 * length * width * cols, 8 * 10**6),
            name="attend_back",
        )(own, other, heads, qkv, rope, *pair)


    def back(inner, m, own, other):
        own, other = inner.hold(own, other)
        return inner.wait(*attend_back(own, other, heads, qkv_low[m], rope, doc_pairs[m]))

    def spread_branch(inner):
        swapped = inner.wait(swap_core(grad_low))
        near = [hop_chip(inner.hold(grad_low), m) for m in around]
        result = back(inner, 0, grad_low, swapped)
        near = inner.wait(*near)
        halves = pass_on(near, 0)
        next_streams = pl.pallas_call(
            next_kernel,
            grid=(steps,),
            in_specs=[tall(entries), flat(width), flat(LANES)],
            out_specs=tall(count),
            out_shape=shape((count, length, width), NARROW),
            compiler_params=params(),
            cost_estimate=cost(10**8, 10**7),
            name="next_streams",
        )(inner.hold(history), entry, coef)
        next_streams = inner.wait(next_streams)
        if square:
            near.append(inner.wait(jnp.concatenate(inner.wait(*halves), 0)))
        others = list(swap_core(jnp.stack(near)))
        others = inner.wait(*others)
        last = back(inner, far, near[far - 1], others[far - 1])
        grad_w_mix2 = transposed_times(mix_act, grad_coef, EXACT)[:hid, :mixes]
        grad_w_mix1 = transposed_times(scaled_low, grad_pre_low)[:, :hid]
        grad_w_mix1, grad_w_mix2 = inner.wait(grad_w_mix1, grad_w_mix2)
        return result, last, near, [swapped, *others], next_streams, grad_w_mix1, grad_w_mix2

    returned, terms = [None] * chips, [None] * chips
    returned[0], returned[far], branch_near, branch_other, *rest = order.scope(spread_branch)
    next_streams, grad_w_mix1, grad_w_mix2 = rest
    branch_own = [grad_low, *branch_near]
    grad_hops = order.wait(*grad_hops)

    interleave = lambda a, b: [values for pair in zip(a, b) for values in pair]
    row_block = width // fsdp

    def hidden_back_side(firsts, seconds, grad, slope, *came):
        return pl.pallas_call(
            functools.partial(hidden_back_kernel, chips, bool(came)),
            grid=(blocks,),
            in_specs=[token_block(width), token_block(hid_cols)]
            + weight_specs(0)
            + weight_specs(1)
            + [token_block(width)] * len(came),
            out_specs=[token_block(hid_cols), spec((1, hid_cols))]
            + (place_specs if came else [token_block(width)]),
            out_shape=[shape((rep * length, hid_cols), NARROW), shape((1, hid_cols), SINGLE)]
            + (places if came else [side]),
            compiler_params=params(),
            cost_estimate=cost(4 * rep * length * width * hid_cols, 2 * 10**7),
            name="hidden_back",
        )(grad, slope, *firsts, *seconds, *came)

    def outer(inner, lefts, rights):
        whole = lambda n: spec((rep * length, n))
        return inner.wait(
            *pl.pallas_call(
                outer_kernel,
                grid=(chips,),
                in_specs=[spec((rep * length, part), lambda i: (0, i))] * 2 + [whole(hid_cols)] * 2,
                out_specs=[spec((part, hid_cols))] * chips,
                out_shape=[shape((part, hid_cols), NARROW)] * chips,
                compiler_params=params(),
                cost_estimate=cost(4 * rep * length * width * hid_cols, 2 * 10**7),
                name="outer",
            )(*lefts, *rights)
        )

    def feed_forward_back(inner):
        whole = inner.wait(jnp.stack([grad_turned, *grad_hops]))
        came = [swap_core(returned[far][3]), swap_core(whole), swap_core(returned[0][3])]
        grad_own = whole.reshape(rep * length, width)
        low_own, sum_own, back_own = inner.wait(
            *hidden_back_side(first_parts, second_parts, inner.hold(grad_own), slopes[0])
        )
        came = inner.wait(*came)
        far_term = inner.wait(add_up(returned[far][2], came[0]))
        halves = send_far(far_term, 1) if square else ()

        def other_side(inner):
            grad_sides = (grad_own, came[1].reshape(rep * length, width))
            low_other, sum_other, back = inner.wait(
                *hidden_back_side(first_parts, second_parts, grad_sides[1], slopes[1])
            )
            back = swap_core(back)
            grads = outer(inner, (inner.hold(grad_sides[0]), grad_sides[1]), acts)
            back = inner.wait(back)
            merged = [
                merge(back_own[k * length : (k + 1) * length], back[k * length : (k + 1) * length])
                for k in range(rep)
            ]
            return grads, low_other, sum_own + sum_other, merged

        grads, low_other, first_bias, merged = inner.scope(other_side)
        halves = inner.wait(*halves) if square else [far_term]
        return grads, low_own, low_other, first_bias, merged, halves, came[0], came[2]

    second_grads, low_own, low_other, grad_first_bias, grad_resid, halves, far_came, own_came = (
        order.scope(feed_forward_back)
    )

    def attention_back(inner):
        results = {0: returned[0], far: returned[far]}
        middle = range(1, far)
        swaps = []
        for m in middle:
            results[m] = back(inner, m, branch_own[m], branch_other[m])
            swaps.append(swap_core(results[m][3]))
        linears = inner.hold(*[results[m][0] for m in range(chips)])
        grad_heads = pl.pallas_call(
            functools.partial(heads_grad_kernel, chips),
            grid=(fsdp,),
            in_specs=[spec((3, length, row_block), lambda i: (0, 0, i))] * fsdp
            + [spec((length, row_block), lambda i: (0, i))] * fsdp
            + [spec((3, 2 * length, cols))] * chips
            + [spec((2 * length, cols))] * chips,
            out_specs=spec((rep, 1, rows, 4 * cols), lambda i: (0, i, 0, 0)),
            out_shape=shape((rep, fsdp, rows, 4 * cols), NARROW),
            compiler_params=params(),
            cost_estimate=cost(8 * fsdp * length * width * cols, 3 * 10**7),
            name="heads_grad",
        )(
            *interleave(qkv_own, qkv_other),
            *interleave(branch_own, branch_other),
            *linears,
            *mixed_low,
        )
        grad_heads = inner.wait(grad_heads)
        swaps = inner.wait(*swaps)
        owns = [results[m][2] for m in range(chips)]
        near_terms = near_sums(inner, owns, [None, *swaps, far_came], halves)
        return grad_heads, near_terms, [results[m][1] for m in range(chips)]

    def residual_back(inner):
        hops = inner.hold(*grad_resid)
        hops = [hop_rep(hops[k], k) for k in range(1, rep)]
        results = inner.scope(attention_back)
        return inner.wait(*hops), *results

    resid_hops, grad_heads, near_terms, qkv_biases = order.scope(residual_back)
    grad_resid = [grad_resid[0], *resid_hops]

    def by_owner(vector):
        return vector.reshape(-1, devices, rows).transpose(1, 0, 2).reshape(devices, -1)

    grad_heads = lax.psum_scatter(grad_heads, "rep", scatter_dimension=0, tiled=False)
    widths = [rows, 3 * cols * fsdp // devices, rows, rows * hid]
    held_bias = order.hold(grad_branch_bias)
    qkv_bias_all = lax.dynamic_update_index_in_dim(
        jnp.zeros((3, fsdp, cols), SINGLE), sum(qkv_biases).reshape(3, cols), chip * 2 + core, 1
    )
    tail = jnp.concatenate(
        [grad_pre_sum[0, :hid], grad_w_mix2.reshape(-1), grad_coef_sum[0, :mixes]]
    )
    sums = [
        by_owner(grad_rms_gain[0]),
        qkv_bias_all.reshape(devices, -1),
        held_bias.reshape(devices, -1),
        grad_w_mix1.reshape(devices, -1),
        jnp.broadcast_to(tail[None], (devices, tail.shape[0])),
    ]
    sums = order.wait(jnp.concatenate(sums, 1))
    sums = lax.all_to_all(sums, AXES, 0, 0, tiled=True)

    def total_hidden(inner, own, hops):
        total = own.astype(SINGLE)
        for values in inner.wait(*hops):
            total = total + values.astype(SINGLE)
        return inner.wait(total.astype(NARROW).reshape(group, rows, hid_cols))

    def whole_rows(came):
        return came.transpose(1, 0, 2).reshape(rows, hidden).astype(SINGLE)

    def exchange(sums):
        widths = [values.shape[1] for values in sums]
        return widths, lax.all_to_all(jnp.concatenate(sums, 1), AXES, 0, 0, tiled=True)

    def send_terms(inner):
        held = inner.hold(*near_terms)
        qkv_back = [hop_chip(held[m - 1], m) for m in around]
        first_grads = outer(inner, (inner.hold(resid_sides[0]), resid_sides[1]), (low_own, low_other))
        return first_grads, inner.wait(*qkv_back)

    first_grads, qkv_back = order.scope(send_terms)

    def near_of(inner, grads):
        halves = send_far(inner.hold(grads[far]), 0)
        if not square:
            return inner.wait(*grads[1:])
        halves = inner.wait(*halves)
        return inner.wait(*take_along(grads[1:far], halves, 0))

    qkv_rest = [own_came, *qkv_back]

    def close_layer(inner):
        held = near_of(inner, second_grads)
        second_hops = [hop_chip(held[m - 1], m) for m in around]
        close_from = inner.hold(history, cotangent)
        grad_history, grad_mix_in, grad_affine = pl.pallas_call(
            functools.partial(close_kernel, chips, len(qkv_rest), rep),
            grid=(steps,),
            in_specs=[
                scalar_spec(),
                tall(entries),
                tall(count),
                flat(LANES),
                flat(1),
                flat(LANES),
                spec((4, width)),
                flat(width),
                *[tall(3)] * (1 + len(qkv_rest)),
                *[flat(width)] * rep,
            ],
            out_specs=[tall(entries), flat(count * entries), spec((4, width))],
            out_shape=[
                shape((entries, length, width), SINGLE),
                shape((length, count * entries), SINGLE),
                shape((4, width), SINGLE),
            ],
            scratch_shapes=[
                pltpu.VMEM((count, ROWS, width), SINGLE),
                pltpu.VMEM((ROWS, width), SINGLE),
                pltpu.VMEM((5 * count * ROWS, width), NARROW),
            ],
            compiler_params=params(),
            cost_estimate=cost(2 * 10**8, 2 * 10**7),
            name="close",
        )(
            chip_at,
            *close_from,
            coef,
            token_weight,
            mix_padded,
            affine,
            grad_entry,
            returned[0][2],
            *qkv_rest,
            *grad_resid,
        )
        grad_history, grad_mix_in, grad_affine = inner.wait(grad_history, grad_mix_in, grad_affine)

        return grad_history, grad_mix_in, grad_affine, total_hidden(inner, second_grads[0], second_hops)

    grad_history, grad_mix_in, grad_affine, second_total = order.scope(close_layer)
    sums = order.wait(sums)
    second_came = lax.all_to_all(order.hold(second_total), GROUP, 0, 0, tiled=True)

    def collect_first(inner):
        held = near_of(inner, first_grads)
        first_hops = [hop_chip(held[m - 1], m) for m in around]
        total = inner.wait(jnp.sum(inner.hold(sums), 0))
        return total, total_hidden(inner, first_grads[0], first_hops)

    total, first_total = order.scope(collect_first)
    second_came = order.wait(second_came)
    first_bias_all = lax.dynamic_update_index_in_dim(
        jnp.zeros((group, hid_cols), SINGLE), grad_first_bias[0], core * rep + line, 0
    )
    every = order.wait(
        jnp.concatenate([by_owner(grad_affine), first_bias_all.reshape(devices, -1)], 1)
    )
    every = order.wait(lax.all_to_all(every, AXES, 0, 0, tiled=True))
    first_came = lax.all_to_all(order.hold(first_total), GROUP, 0, 0, tiled=True)
    grad_w_fc2 = order.wait(whole_rows(second_came))
    every = order.wait(jnp.sum(every, 0))
    grad_heads = order.wait(grad_heads)

    def around_ring(inner):
        split = inner.hold(grad_heads).reshape(chips, 2, rows, 4 * cols)
        parts = [lax.dynamic_index_in_dim(split, chip ^ m, 0, False) for m in range(chips)]
        parts = [parts[0]] + [hop_chip(parts[m], m) for m in range(1, chips)]
        parts = jnp.stack(inner.wait(*parts))
        mine = lax.dynamic_index_in_dim(parts, core, 1, False)
        came = swap_core(lax.dynamic_index_in_dim(parts, 1 - core, 1, False))
        result = jnp.zeros((chips, 2, rows, 4 * cols), NARROW)
        for m in range(chips):
            pair = jnp.where(core == 0, jnp.stack([mine[m], came[m]]), jnp.stack([came[m], mine[m]]))
            result = lax.dynamic_update_index_in_dim(result, pair, chip ^ m, 0)
        result = result.reshape(fsdp, rows, 4, cols).transpose(1, 2, 0, 3).astype(SINGLE)
        return result[:, :3].reshape(rows, 3 * width), result[:, 3].reshape(rows, width)

    grad_w_qkv, grad_w_out = order.scope(around_ring)
    first_came = order.wait(first_came)
    grad_w_fc1 = whole_rows(first_came)
    outs, start = [], 0
    for size in widths:
        outs.append(total[start : start + size])
        start += size
    outs.append(total[start:])
    affine_sums = every[: 4 * rows].reshape(4, rows)
    gain_grads = jnp.stack([affine_sums[0], affine_sums[2], outs[0]])
    bias_grads = jnp.stack([affine_sums[1], affine_sums[3]])
    return (
        next_streams,
        grad_history,
        grad_mix_in,
        gain_grads,
        bias_grads,
        grad_w_qkv,
        outs[1],
        grad_w_out,
        outs[2],
        grad_w_fc1,
        every[4 * rows :],
        grad_w_fc2,
        outs[2],
        outs[3].reshape(rows, hid),
        outs[4][:hid],
        outs[4][hid : hid + hid * mixes].reshape(hid, mixes),
        outs[4][hid + hid * mixes :],
    )


def solution(mesh):
    fsdp, rep = mesh.shape["fsdp"], mesh.shape["rep"]
    chips = fsdp // 2
    finer = Mesh(mesh.devices.reshape(chips, 2, rep), AXES)
    rows = P(AXES, None)
    line = P(AXES)
    streams = P(None, AXES, None)
    columns = P(None, AXES)
    in_specs = (
        streams,
        rows,
        rows,
        rows,
        P(),
        columns,
        columns,
        rows,
        line,
        rows,
        line,
        rows,
        line,
        rows,
        line,
        rows,
        P(),
        P(),
        P(),
        streams,
    )
    out_specs = (
        streams,
        streams,
        rows,
        columns,
        columns,
        rows,
        line,
        rows,
        line,
        rows,
        line,
        rows,
        line,
        rows,
        P(),
        P(),
        P(),
    )
    return jax.shard_map(
        functools.partial(on_device, chips, rep),
        mesh=finer,
        in_specs=in_specs,
        out_specs=out_specs,
        check_vma=False,
    )
```

time: 4940 us -> 734 us (0.15)
  waiting for transfers between devices: 4160 us -> 221 us
  blocking collectives: 324 us -> 0 us
  matrix products: 235 us -> 2.52 us
  Pallas kernels: 0 us -> 231 us
  starting transfers between devices: 0.67 us -> 92.6 us
  other arithmetic: 111 us -> 51.8 us
    reduce_scatter x4 -> x1, waiting for transfers between devices: 3320 us -> 0.01 us  [on_device(): lax.psum_scatter(grad_heads, 'rep', scatter_dimension=0, tiled=False)]
    unnamed x16 -> x2, waiting for transfers between devices: 604 us -> 0.03 us
    all_gather x4 -> x0, blocking collectives: 281 us -> none  [the longest x1 83.5 us: on_device(): lax.all_gather(w_mix1.astype(NARROW), ('fsdp', 'rep'), axis=0, tiled=True)]
    dot_general x30 -> x2, matrix products: 235 us -> 2.52 us  [transposed_times(): lax.dot_general(left, right, (((0,), (0,)), ((), ())), precision=precisio...]
    pallas_call x0 -> x28, Pallas kernels: none -> 231 us  [the longest x4 35.6 us: attend_back(): pl.pallas_call(attend_back_kernel, out_shape=[shape((3, 2 * length, cols)...]
    all_gather x4 -> x1, waiting for transfers between devices: 232 us -> 5.44 us  [on_device(): heads_all = lax.all_gather(order.hold(heads_came), 'rep', axis=0)]
    ppermute x0 -> x65, waiting for transfers between devices: none -> 191 us  [the longest x31 168 us: hop_chip(): return lax.ppermute(values, 'chip', [(i, i ^ m) for i in range(chips)])]
    unnamed x352 -> x63, local copies, waits for them, and re-layouts: 71.6 us -> 5.32 us
  transfers between devices with their start and end apart: 12 -> 74, of which waited for: 9 -> 30; matrix products, arithmetic and copies ran while one was open for 6% -> 17% of each run, Pallas kernels for 0% -> 30%
where the time goes in v2:
time: 734 us; the launch traced here: 728 us
  Pallas kernels  231 us (31%)
  waiting for transfers between devices  221 us (30%)
  local copies, waits for them, and re-layouts  98.5 us (13%)
  starting transfers between devices  92.6 us (13%)
  other arithmetic  51.8 us (7%)
  between operations  15 us (2%)
  loops' own time  14.9 us (2%)
    ppermute x31, waiting for transfers between devices, hop_chip(): return lax.ppermute(values, 'chip', [(i, i ^ m) for i in range(chips)])  168 us
    ppermute x31, starting transfers between devices, hop_chip(): return lax.ppermute(values, 'chip', [(i, i ^ m) for i in range(chips)])  36.6 us
    pallas_call x4, Pallas kernels, attend_back(): pl.pallas_call(attend_back_kernel, out_shape=[shape((3, 2 * length, cols)...  35.6 us
    pallas_call x1, Pallas kernels, close_layer(): pl.pallas_call(functools.partial(close_kernel, chips, len(qkv_rest), rep)...  28.8 us
    pallas_call x4, Pallas kernels, attend(): pl.pallas_call(attend_kernel, out_shape=[shape((3, 2 * length, cols), NAR...  28.5 us
    all_to_all x1, waiting for transfers between devices, on_device(): lax.all_to_all(order.hold(second_total), GROUP, 0, 0, tiled=True)  25 us
    ppermute x19, waiting for transfers between devices, swap_core(): return lax.ppermute(values, 'core', [(0, 1), (1, 0)])  22.8 us
    ppermute x15, starting transfers between devices, hop_rep(): return lax.ppermute(values, 'rep', [(i, i ^ k) for i in range(rep)])  22.1 us
  transfers between devices with their start and end apart: 74, of which 30 were waited for; matrix products, arithmetic and copies ran while one was open for 17% of the time, Pallas kernels for 30%

profile of v2, /device:TPU:0, one launch (start us, length us, event | category | flops | bytes accessed | tf_op | source)
XLA Modules:
  0.0 728.1 jit_solution(5072173993083253144)
XLA Ops:
  39.3 48.4 %conditional.17 = (bf16[3,128,2048]{2,1,0:T(8,128)(2,1)}, bf16[128,2048]{1,0:T(8,128)(2,1)}, f32[128,2048]{1,0:T(8,128)}, f32[4,2048]{1,0:T(4,128)}, f32[128,128...) conditional(s32[]{:T(128)} %convert_element_type.352, ...), branch_computations={%region_0.1_spmd, %region_1.4_spmd} | conditional | flops 275264 | bytes 12950332 | solution.py:585
  40.1 9.9 %streams.1 = (bf16[3,128,2048]{2,1,0:T(8,128)(2,1)}, bf16[128,2048]{1,0:T(8,128)(2,1)}, f32[128,2048]{1,0:T(8,128)}) custom-call(s32[1]{0:T(128)} %get-tuple-element.464.chip, bf16[9,128,2048]{2,1,0:T(8,128)(2,1)} %get-tuple-element.465.hist, f32[128,128]{1,0:T(8,128)S(1)} %get-tuple-element.466.mix, f32[4,2048]{1,0:T(4,128)S(1)} %maximum_convert_fusion.affine), custom_call_target="tpu_custom_call" | custom-call | flops 100000 | bytes 10000 | tf_op jit(solution)/shard_map/cond/branch_1_fun/streams/pallas_call | solution.py:741
  55.5 9.9 %history_dots.1 = f32[128,128]{1,0:T(8,128)S(1)} custom-call(bf16[9,128,2048]{2,1,0:T(8,128)(2,1)} %get-tuple-element.465.hist, bf16[4,128,2048]{2,1,0:T(8,128)(2,1)S(1)} %get-tuple-element.471.cot, f32[128,1]{1,0:T(8,128)} %copy.253.weight), custom_call_target="tpu_custom_call" | custom-call | flops 100000 | bytes 10000 | tf_op jit(solution)/shard_map/cond/branch_1_fun/history_dots/pallas_call | solution.py:765
  65.4 20.9 %collective-permute-done.45 = bf16[3,128,2048]{2,1,0:T(8,128)(2,1)} collective-permute-done((bf16[3,128,2048]{2,1,0:T(8,128)(2,1)}, bf16[3,128,2048]{2,1,0:T(8,128)(2,1)}, u32[]{:S(2)}, u32[]{:S(2)}) %collective-permute-start.45) | collective-permute-done | bytes 1572896 | tf_op jit(solution)/shard_map/cond/branch_1_fun/ppermute | solution.py:639
  99.1 58.6 %conditional.18 = (bf16[2,512,1024]{2,1,0:T(8,128)(2,1)}, bf16[2,512,1024]{2,1,0:T(8,128)(2,1)}, bf16[2,512,1024]{2,1,0:T(8,128)(2,1)}, f32[1,2048]{1,0:T(1,128)...) conditional(s32[]{:T(128)} %convert_element_type.354, ...), branch_computations={%region_4.5_spmd, %region_5.10_spmd} | conditional | flops 1799371 | bytes 30460312 | solution.py:585
  99.2 9.1 %conditional = (bf16[2,512,1024]{2,1,0:T(8,128)(2,1)}) conditional(s32[]{:T(128)} %convert_element_type.259, () %tuple.90, (s32[]{:T(128)}, bf16[2,2,64,1024]{3,2,1,0:T(8,128)(2,1)S(1)}, bf16[2,2,64,1024]{3,2,1,0:T(8,128)(2,1)}, bf16[2,2,64,1024]{3,2,1,0:T(8,128)(2,1)}, bf16[2,2,64,1024]{3,2,1,0:T(8,128)(2,1)}, /*index=5*/s32[1]{0:T(128)}) %tuple.91), branch_computations={%region_6.6_spmd, %region_7.7_spmd} | conditional | flops 1573868 | bytes 12588042 | solution.py:585
  117.3 39.0 %collective-permute-done.23 = bf16[2,512,1024]{2,1,0:T(8,128)(2,1)} collective-permute-done((bf16[2,512,1024]{2,1,0:T(8,128)(2,1)}, bf16[2,512,1024]{2,1,0:T(8,128)(2,1)}, u32[]{:S(2)}, u32[]{:S(2)}) %collective-permute-start.23) | collective-permute-done | bytes 2097184 | tf_op jit(solution)/shard_map/cond/branch_1_fun/ppermute | solution.py:639
  158.2 75.5 %conditional.19 = (bf16[1,512,1024]{2,1,0:T(8,128)(2,1)S(1)}, bf16[1,512,1024]{2,1,0:T(8,128)(2,1)S(1)}, bf16[512,2048]{1,0:T(8,128)(2,1)}, bf16[512,2048]{1,0:T...) conditional(s32[]{:T(128)} %convert_element_type.355, ...), branch_computations={%region_10.11_spmd, %region_11.16_spmd} | conditional | flops 14881390 | bytes 102457264 | solution.py:585
  179.3 10.0 %collective-permute-done.12.refs_3_ = bf16[1,512,1024]{2,1,0:T(8,128)(2,1)S(1)} collective-permute-done((bf16[1,512,1024]{2,1,0:T(8,128)(2,1)}, bf16[1,512,1024]{2,1,0:T(8,128)(2,1)S(1)}, u32[]{:S(2)}, u32[]{:S(2)}) %collective-permute-start.12) | collective-permute-done | bytes 1048608 | tf_op jit(solution)/shard_map/cond/branch_1_fun/ppermute | solution.py:639
  205.7 20.9 %conditional.3 = (bf16[512,1024]{1,0:T(8,128)(2,1)}, f32[512,1024]{1,0:T(8,128)}, bf16[128,2048]{1,0:T(8,128)(2,1)}, bf16[128,2048]{1,0:T(8,128)(2,1)}, bf16[128...) conditional(s32[]{:T(128)} %convert_element_type.262, () %tuple.114, (bf16[512,1024]{1,0:T(8,128)(2,1)S(1)}, ...), branch_computations={%region_14.14_spmd, %region_15.15_spmd} | conditional | flops 6442449 | bytes 16807332 | solution.py:585
  246.2 70.0 %conditional.20 = (bf16[2048,1024]{1,0:T(8,128)(2,1)}, bf16[3,256,256]{2,1,0:T(8,128)(2,1)S(1)}, bf16[3,256,256]{2,1,0:T(8,128)(2,1)}, bf16[3,256,256]{2,1,0:T(8...) conditional(s32[]{:T(128)} %convert_element_type.356, ...), branch_computations={%region_16.17_spmd, %region_17.18_spmd} | conditional | flops 10324276 | bytes 51945200 | solution.py:585
  329.1 52.7 %conditional.21 = (bf16[3,256,256]{2,1,0:T(8,128)(2,1)}, f32[1,768]{1,0:T(1,128)}, f32[3,128,2048]{2,1,0:T(8,128)}, bf16[3,128,2048]{2,1,0:T(8,128)(2,1)}, bf16[...) conditional(s32[]{:T(128)} %convert_element_type.357, ...), branch_computations={%region_18.19_spmd, %region_19.20_spmd} | conditional | flops 63441720 | bytes 55881840 | solution.py:585
  334.8 9.0 %attend_back.4 = (bf16[3,256,256]{2,1,0:T(8,128)(2,1)}, f32[1,768]{1,0:T(1,128)}, f32[3,128,2048]{2,1,0:T(8,128)}, bf16[3,128,2048]{2,1,0:T(8,128)(2,1)}) custom-call(bf16[128,2048]{1,0:T(8,128)(2,1)} %get-tuple-element.665.own, bf16[128,2048]{1,0:T(8,128)(2,1)} %collective-permute-done.47.other, bf16[2048,1024]{1,0:T(8,128)(2,1)} %get-tuple-element.652.weight, ...), custom_call_target="tpu_custom_call" | custom-call | flops 1073741 | bytes 8000 | tf_op jit(solution)/shard_map/cond/branch_1_fun/attend_back/pallas_call | solution.py:1079
  381.8 46.7 %conditional.22 = (bf16[512,1024]{1,0:T(8,128)(2,1)}, bf16[512,1024]{1,0:T(8,128)(2,1)}, bf16[512,1024]{1,0:T(8,128)(2,1)}, bf16[512,1024]{1,0:T(8,128)(2,1)}, b...) conditional(s32[]{:T(128)} %convert_element_type.358, ...), branch_computations={%region_20.21_spmd, %region_21.24_spmd} | conditional | flops 20226958 | bytes 87131176 | solution.py:585
  384.7 9.5 %hidden_back.3 = (bf16[512,1024]{1,0:T(8,128)(2,1)}, f32[1,1024]{1,0:T(1,128)S(1)}, bf16[512,2048]{1,0:T(8,128)(2,1)}) custom-call(bf16[512,2048]{1,0:T(8,128)(2,1)S(1)} %bitcast.170, f32[512,1024]{1,0:T(8,128)} %get-tuple-element.732.slope, bf16[2,512,1024]{2,1,0:T(8,128)(2,1)} %get-tuple-element.733.refs_0_.refs_4_, ...), custom_call_target="tpu_custom_call" | custom-call | flops 4294967 | bytes 20000 | tf_op jit(solution)/shard_map/cond/branch_1_fun/hidden_back/pallas_call | solution.py:1134
  404.9 23.2 %conditional.4 = (bf16[512,1024]{1,0:T(8,128)(2,1)}, bf16[512,1024]{1,0:T(8,128)(2,1)}, bf16[512,1024]{1,0:T(8,128)(2,1)}, bf16[512,1024]{1,0:T(8,128)(2,1)}, bf...) conditional(s32[]{:T(128)} %convert_element_type.289, ...), branch_computations={%region_22.22_spmd, %region_23.23_spmd} | conditional | flops 12785262 | bytes 35720488 | solution.py:585
  404.9 9.8 %hidden_back.2 = (bf16[512,1024]{1,0:T(8,128)(2,1)}, f32[1,1024]{1,0:T(1,128)}, bf16[512,2048]{1,0:T(8,128)(2,1)}) custom-call(bf16[512,2048]{1,0:T(8,128)(2,1)} %bitcast.176, f32[512,1024]{1,0:T(8,128)} %get-tuple-element.700.slope, bf16[2,512,1024]{2,1,0:T(8,128)(2,1)} %get-tuple-element.701.refs_0_.refs_4_, ...), custom_call_target="tpu_custom_call" | custom-call | flops 4294967 | bytes 20000 | tf_op jit(solution)/shard_map/cond/branch_1_fun/cond/branch_1_fun/hidden_back/pallas_call | solution.py:1134
  414.8 9.2 %outer.2 = (bf16[512,1024]{1,0:T(8,128)(2,1)}, bf16[512,1024]{1,0:T(8,128)(2,1)}, bf16[512,1024]{1,0:T(8,128)(2,1)}, bf16[512,1024]{1,0:T(8,128)(2,1)}) custom-call(bf16[512,2048]{1,0:T(8,128)(2,1)S(1)} %copy-done.6, bf16[512,2048]{1,0:T(8,128)(2,1)} %bitcast.177, bf16[512,1024]{1,0:T(8,128)(2,1)} %get-tuple-element.708.right_own, ...), custom_call_target="tpu_custom_call" | custom-call | flops 4294967 | bytes 20000 | tf_op jit(solution)/shard_map/cond/branch_1_fun/cond/branch_1_fun/outer/pallas_call | solution.py:1153
  428.5 48.2 %conditional.23 = (bf16[128,2048]{1,0:T(8,128)(2,1)}, bf16[128,2048]{1,0:T(8,128)(2,1)}, bf16[128,2048]{1,0:T(8,128)(2,1)}, bf16[4,8,64,1024]{3,2,1,0:T(8,128)(2...) conditional(s32[]{:T(128)} %convert_element_type.359, ...), branch_computations={%region_24.25_spmd, %region_25.28_spmd} | conditional | flops 6444450 | bytes 39916708 | solution.py:585
  433.0 43.7 %conditional.5 = (bf16[4,8,64,1024]{3,2,1,0:T(8,128)(2,1)}, bf16[3,128,2048]{2,1,0:T(8,128)(2,1)}, bf16[3,128,2048]{2,1,0:T(8,128)(2,1)}, f32[1,768]{1,0:T(1,128...) conditional(s32[]{:T(128)} %convert_element_type.290, () %tuple.182, ...), branch_computations={%region_26.26_spmd, %region_27.27_spmd} | conditional | flops 6444449 | bytes 33624776 | solution.py:585
  454.1 12.4 %heads_grad.1 = bf16[4,8,64,1024]{3,2,1,0:T(8,128)(2,1)} custom-call(bf16[3,128,2048]{2,1,0:T(8,128)(2,1)} %get-tuple-element.764.refs_0_, bf16[3,128,2048]{2,1,0:T(8,128)(2,1)} %get-tuple-element.765.refs_1_, bf16[3,128,2048]{2,1,0:T(8,128)(2,1)} %get-tuple-element.766.refs_2_, bf16[3,128,2048]{2,1,0:T(8,128)(2,1)} %get-tuple-element.767.refs_3_, ...), custom_call_target="tpu_custom_call" | custom-call | flops 4294967 | bytes 30000 | tf_op jit(solution)/shard_map/cond/branch_1_fun/cond/branch_1_fun/heads_grad/pallas_call | solution.py:1206
  486.5 50.1 %conditional.24 = (bf16[512,1024]{1,0:T(8,128)(2,1)}, bf16[512,1024]{1,0:T(8,128)(2,1)}, bf16[512,1024]{1,0:T(8,128)(2,1)}, bf16[512,1024]{1,0:T(8,128)(2,1)}, b...) conditional(s32[]{:T(128)} %convert_element_type.360, () %tuple.321, (bf16[512,2048]{1,0:T(8,128)(2,1)}, ...), branch_computations={%region_28.29_spmd, %region_29.30_spmd} | conditional | flops 4294967 | bytes 12603040 | solution.py:585
  489.7 9.6 %outer.3 = (bf16[512,1024]{1,0:T(8,128)(2,1)}, bf16[512,1024]{1,0:T(8,128)(2,1)}, bf16[512,1024]{1,0:T(8,128)(2,1)}, bf16[512,1024]{1,0:T(8,128)(2,1)}) custom-call(bf16[512,2048]{1,0:T(8,128)(2,1)} %get-tuple-element.874.left_own, bf16[512,2048]{1,0:T(8,128)(2,1)} %get-tuple-element.875.left_other, bf16[512,1024]{1,0:T(8,128)(2,1)} %get-tuple-element.876.right_own, ...), custom_call_target="tpu_custom_call" | custom-call | flops 4294967 | bytes 20000 | tf_op jit(solution)/shard_map/cond/branch_1_fun/outer/pallas_call | solution.py:1153
  499.3 37.3 %collective-permute-done.10 = bf16[3,128,2048]{2,1,0:T(8,128)(2,1)} collective-permute-done((bf16[3,128,2048]{2,1,0:T(8,128)(2,1)}, bf16[3,128,2048]{2,1,0:T(8,128)(2,1)}, u32[]{:S(2)}, u32[]{:S(2)}) %collective-permute-start.10) | collective-permute-done | bytes 1572896 | tf_op jit(solution)/shard_map/cond/branch_1_fun/ppermute | solution.py:639
  536.6 56.8 %conditional.25 = (f32[9,128,2048]{2,1,0:T(8,128)}, f32[128,36]{1,0:T(8,128)}, f32[4,2048]{1,0:T(4,128)}, bf16[8,64,1024]{2,1,0:T(8,128)(2,1)S(1)}, f32[128,36]{0,1:T(8,128)S(1)}) conditional(s32[]{:T(128)} %convert_element_type.361, () %tuple.324, (bf16[512,1024]{1,0:T(8,128)(2,1)}, bf16[512,1024]{1,0:T(8,128)(2,1)}, ...), branch_computations={%region_30.31_spmd, %region_31.32_spmd} | conditional | flops 9637184 | bytes 28369640 | solution.py:585
  542.3 10.0 %collective-permute-done.37 = bf16[256,1024]{1,0:T(8,128)(2,1)S(1)} collective-permute-done((bf16[256,1024]{1,0:T(8,128)(2,1)S(1)}, bf16[256,1024]{1,0:T(8,128)(2,1)S(1)}, u32[]{:S(2)}, u32[]{:S(2)}) %collective-permute-start.37) | collective-permute-done | bytes 524320 | tf_op jit(solution)/shard_map/cond/branch_1_fun/ppermute | solution.py:639
  561.1 28.8 %close.1 = (f32[9,128,2048]{2,1,0:T(8,128)}, f32[128,36]{1,0:T(8,128)}, f32[4,2048]{1,0:T(4,128)}) custom-call(s32[1]{0:T(128)} %get-tuple-element.888.chip, bf16[9,128,2048]{2,1,0:T(8,128)(2,1)} %get-tuple-element.897.hist, bf16[4,128,2048]{2,1,0:T(8,128)(2,1)S(1)} %get-tuple-element.898.cot, f32[128,128]{1,0:T(8,128)} %get-tuple-element.899.coef, ...), custom_call_target="tpu_custom_call" | custom-call | flops 200000 | bytes 20000 | tf_op jit(solution)/shard_map/cond/branch_1_fun/close/pallas_call | solution.py:1295
  601.5 25.0 %all-to-all-done.4 = bf16[8,64,1024]{2,1,0:T(8,128)(2,1)S(1)} async-done(((bf16[8,64,1024]{2,1,0:T(8,128)(2,1)}), bf16[8,64,1024]{2,1,0:T(8,128)(2,1)S(1)}, u32[]{:S(2)}, u32[]{:S(2)}) %all-to-all-start.4) | async-done | bytes 1048608 | tf_op jit(solution)/shard_map/all_to_all | solution.py:1342
  629.9 48.0 %conditional.26 = (f32[10860]{0:T(1024)}, bf16[8,64,1024]{2,1,0:T(8,128)(2,1)}, f32[64]{0:T(128)}, f32[192]{0:T(256)S(1)}, f32[64]{0:T(128)S(1)}, /*index=5*/f32...) conditional(s32[]{:T(128)} %convert_element_type.365, ...), branch_computations={%region_33.34_spmd, %region_34.36_spmd} | conditional | flops 9773844 | bytes 29947924 | solution.py:585
  636.5 9.1 %collective-permute-done.41 = bf16[256,1024]{1,0:T(8,128)(2,1)S(1)} collective-permute-done((bf16[256,1024]{1,0:T(8,128)(2,1)S(1)}, bf16[256,1024]{1,0:T(8,128)(2,1)S(1)}, u32[]{:S(2)}, u32[]{:S(2)}) %collective-permute-start.41) | collective-permute-done | bytes 524320 | tf_op jit(solution)/shard_map/cond/branch_1_fun/ppermute | solution.py:639
  661.0 12.9 %collective-permute-done.43 = bf16[512,1024]{1,0:T(8,128)(2,1)} collective-permute-done((bf16[512,1024]{1,0:T(8,128)(2,1)S(1)}, bf16[512,1024]{1,0:T(8,128)(2,1)}, u32[]{:S(2)}, u32[]{:S(2)}) %collective-permute-start.43) | collective-permute-done | bytes 1048608 | tf_op jit(solution)/shard_map/cond/branch_1_fun/ppermute | solution.py:639
  687.2 31.5 %conditional.27 = (f32[64,6144]{1,0:T(8,128)}, f32[64,2048]{1,0:T(8,128)}) conditional(s32[]{:T(128)} %convert_element_type.366, () %tuple.337, (s32[]{:T(128)}, bf16[8,64,1024]{2,1,0:T(8,128)(2,1)}, s32[]{:T(128)}) %tuple.479), branch_computations={%region_37.38_spmd, %region_38.39_spmd} | conditional | flops 6291482 | bytes 30409288 | solution.py:585
  (478 shorter events, 440.3 us)
Async XLA Ops:
  30.7 57.0 %all-to-all-start.1 = ((bf16[8,64,1024]{2,1,0:T(8,128)(2,1)}), bf16[8,64,1024]{2,1,0:T(8,128)(2,1)S(1)}, u32[]{:S(2)}, u32[]{:S(2)}) async-start(bf16[8,64,1024]{2,1,0:T(8,128)(2,1)} %pack_heads.1), calls=%async_computation.1 | async-start | bytes 2097152 | tf_op jit(solution)/shard_map/all_to_all | solution.py:725
  34.8 52.9 %collective-permute-start.53 = (bf16[2,2,64,1024]{3,2,1,0:T(8,128)(2,1)}, bf16[2,2,64,1024]{3,2,1,0:T(8,128)(2,1)}, u32[]{:S(2)}, u32[]{:S(2)}) collective-permute-start(bf16[2,2,64,1024]{3,2,1,0:T(8,128)(2,1)} %get-tuple-element.1188), channel_id=1, source_target_pairs={{0,1},{1,0},{2,3},{3,2},{4,5},{5,4},{6,7},{7,6},{8,9},{9,8},{10,11... | collective-permute-start | bytes 1572872 | tf_op jit(solution)/shard_map/ppermute | solution.py:642
  36.3 51.4 %collective-permute-start.54 = (bf16[2,2,64,1024]{3,2,1,0:T(8,128)(2,1)}, bf16[2,2,64,1024]{3,2,1,0:T(8,128)(2,1)}, u32[]{:S(2)}, u32[]{:S(2)}) collective-permute-start(bf16[2,2,64,1024]{3,2,1,0:T(8,128)(2,1)} %get-tuple-element.1189), channel_id=1, source_target_pairs={{0,2},{1,3},{2,0},{3,1},{4,6},{5,7},{6,4},{7,5},{8,10},{9,11},{10,... | collective-permute-start | bytes 1572872 | tf_op jit(solution)/shard_map/ppermute | solution.py:642
  38.7 49.0 %collective-permute-start.55 = (bf16[2,2,64,1024]{3,2,1,0:T(8,128)(2,1)}, bf16[2,2,64,1024]{3,2,1,0:T(8,128)(2,1)}, u32[]{:S(2)}, u32[]{:S(2)}) collective-permute-start(bf16[2,2,64,1024]{3,2,1,0:T(8,128)(2,1)} %get-tuple-element.1190), channel_id=1, source_target_pairs={{0,3},{1,2},{2,1},{3,0},{4,7},{5,6},{6,5},{7,4},{8,11},{9,10},{10,... | collective-permute-start | bytes 1572872 | tf_op jit(solution)/shard_map/ppermute | solution.py:642
  50.0 36.3 %collective-permute-start.45 = (bf16[3,128,2048]{2,1,0:T(8,128)(2,1)}, bf16[3,128,2048]{2,1,0:T(8,128)(2,1)}, u32[]{:S(2)}, u32[]{:S(2)}) collective-permute-start(bf16[3,128,2048]{2,1,0:T(8,128)(2,1)} %get-tuple-element.2316), channel_id=1, source_target_pairs={{0,8},{8,0},{16,24},{24,16},{1,9},{9,1},{17,25},{25,17},{2,10},{10... | collective-permute-start | bytes 4718600 | tf_op jit(solution)/shard_map/cond/branch_1_fun/ppermute | solution.py:639
  52.0 35.7 %collective-permute-start.46 = (bf16[3,128,2048]{2,1,0:T(8,128)(2,1)}, bf16[3,128,2048]{2,1,0:T(8,128)(2,1)}, u32[]{:S(2)}, u32[]{:S(2)}) collective-permute-start(bf16[3,128,2048]{2,1,0:T(8,128)(2,1)} %get-tuple-element.2316), channel_id=1, source_target_pairs={{0,16},{8,24},{16,0},{24,8},{1,17},{9,25},{17,1},{25,9},{2,18},{10... | collective-permute-start | bytes 4718600 | tf_op jit(solution)/shard_map/cond/branch_1_fun/ppermute | solution.py:639
  90.0 67.7 %all-to-all-start.2 = ((bf16[32,2,3200]{2,1,0:T(2,128)(2,1)}), bf16[32,2,3200]{2,1,0:T(2,128)(2,1)S(1)}, u32[]{:S(2)}, u32[]{:S(2)}) async-start(bf16[32,2,3200]{2,1,0:T(2,128)(2,1)} %reshape.512), calls=%async_computation.2 | async-start | bytes 819200 | tf_op jit(solution)/shard_map/all_to_all | solution.py:785
  94.6 144.5 %all-gather.3.cloned.1.call-start = ((), (), s32[]{:S(2)}) async-start(), calls=%async_computation.9 | async-start | bytes 5242880 | tf_op jit(solution)/shard_map/all_gather | solution.py:848
  94.7 63.0 %collective-permute-start.56 = (bf16[128,2048]{1,0:T(8,128)(2,1)}, bf16[128,2048]{1,0:T(8,128)(2,1)}, u32[]{:S(2)}, u32[]{:S(2)}) collective-permute-start(bf16[128,2048]{1,0:T(8,128)(2,1)} %get-tuple-element.1195), channel_id=1, source_target_pairs={{0,1},{1,0},{2,3},{3,2},{4,5},{5,4},{6,7},{7,6},{8,9},{9,8},{10,11... | collective-permute-start | bytes 1572872 | tf_op jit(solution)/shard_map/ppermute | solution.py:642
  96.5 61.2 %collective-permute-start.57 = (bf16[128,2048]{1,0:T(8,128)(2,1)}, bf16[128,2048]{1,0:T(8,128)(2,1)}, u32[]{:S(2)}, u32[]{:S(2)}) collective-permute-start(bf16[128,2048]{1,0:T(8,128)(2,1)} %get-tuple-element.1195), channel_id=1, source_target_pairs={{0,2},{1,3},{2,0},{3,1},{4,6},{5,7},{6,4},{7,5},{8,10},{9,11},{10,... | collective-permute-start | bytes 1572872 | tf_op jit(solution)/shard_map/ppermute | solution.py:642
  98.9 58.8 %collective-permute-start.58 = (bf16[128,2048]{1,0:T(8,128)(2,1)}, bf16[128,2048]{1,0:T(8,128)(2,1)}, u32[]{:S(2)}, u32[]{:S(2)}) collective-permute-start(bf16[128,2048]{1,0:T(8,128)(2,1)} %get-tuple-element.1195), channel_id=1, source_target_pairs={{0,3},{1,2},{2,1},{3,0},{4,7},{5,6},{6,5},{7,4},{8,11},{9,10},{10,... | collective-permute-start | bytes 1572872 | tf_op jit(solution)/shard_map/ppermute | solution.py:642
  108.2 48.0 %collective-permute-start.23 = (bf16[2,512,1024]{2,1,0:T(8,128)(2,1)}, bf16[2,512,1024]{2,1,0:T(8,128)(2,1)}, u32[]{:S(2)}, u32[]{:S(2)}) collective-permute-start(bf16[2,512,1024]{2,1,0:T(8,128)(2,1)} %get-tuple-element.2587), channel_id=1, source_target_pairs={{0,8},{8,0},{16,24},{24,16},{1,9},{9,1},{17,25},{25,17},{2,10},{10... | collective-permute-start | bytes 6291464 | tf_op jit(solution)/shard_map/cond/branch_1_fun/ppermute | solution.py:639
  110.0 47.7 %collective-permute-start.24 = (bf16[2,512,1024]{2,1,0:T(8,128)(2,1)}, bf16[2,512,1024]{2,1,0:T(8,128)(2,1)}, u32[]{:S(2)}, u32[]{:S(2)}) collective-permute-start(bf16[2,512,1024]{2,1,0:T(8,128)(2,1)} %get-tuple-element.2587), channel_id=1, source_target_pairs={{0,16},{8,24},{16,0},{24,8},{1,17},{9,25},{17,1},{25,9},{2,18},{10... | collective-permute-start | bytes 6291464 | tf_op jit(solution)/shard_map/cond/branch_1_fun/ppermute | solution.py:639
  158.2 529.0 %reduce-scatter.2.cloned.1.call-start = ((), (), s32[]{:S(2)}) async-start(), calls=%async_computation.8 | async-start | bytes 5242880 | tf_op jit(solution)/shard_map/reduce_scatter | solution.py:1242
  195.4 31.1 %collective-permute-start.15 = (bf16[3,64,2048]{2,1,0:T(8,128)(2,1)}, bf16[3,64,2048]{2,1,0:T(8,128)(2,1)}, u32[]{:S(2)}, u32[]{:S(2)}) collective-permute-start(bf16[3,64,2048]{2,1,0:T(8,128)(2,1)} %slice.228), channel_id=1, source_target_pairs={{0,16},{8,24},{16,0},{24,8},{1,17},{9,25},{17,1},{25,9},{2,18},{10... | collective-permute-start | bytes 2359304 | tf_op jit(solution)/shard_map/cond/branch_1_fun/ppermute | solution.py:639
  239.1 77.1 %collective-permute-start.59 = (bf16[128,2048]{1,0:T(8,128)(2,1)}, bf16[128,2048]{1,0:T(8,128)(2,1)}, u32[]{:S(2)}, u32[]{:S(2)}) collective-permute-start(bf16[128,2048]{1,0:T(8,128)(2,1)} %get-tuple-element.1238), channel_id=1, source_target_pairs={{0,1},{1,0},{2,3},{3,2},{4,5},{5,4},{6,7},{7,6},{8,9},{9,8},{10,11... | collective-permute-start | bytes 1572872 | tf_op jit(solution)/shard_map/ppermute | solution.py:642
  239.1 77.1 %collective-permute-start.60 = (bf16[128,2048]{1,0:T(8,128)(2,1)}, bf16[128,2048]{1,0:T(8,128)(2,1)}, u32[]{:S(2)}, u32[]{:S(2)}) collective-permute-start(bf16[128,2048]{1,0:T(8,128)(2,1)} %get-tuple-element.1239), channel_id=1, source_target_pairs={{0,2},{1,3},{2,0},{3,1},{4,6},{5,7},{6,4},{7,5},{8,10},{9,11},{10,... | collective-permute-start | bytes 1572872 | tf_op jit(solution)/shard_map/ppermute | solution.py:642
  240.3 75.9 %collective-permute-start.61 = (bf16[128,2048]{1,0:T(8,128)(2,1)}, bf16[128,2048]{1,0:T(8,128)(2,1)}, u32[]{:S(2)}, u32[]{:S(2)}) collective-permute-start(bf16[128,2048]{1,0:T(8,128)(2,1)} %get-tuple-element.1240), channel_id=1, source_target_pairs={{0,3},{1,2},{2,1},{3,0},{4,7},{5,6},{6,5},{7,4},{8,11},{9,10},{10,... | collective-permute-start | bytes 1572872 | tf_op jit(solution)/shard_map/ppermute | solution.py:642
  324.6 57.1 %collective-permute-start.62 = (bf16[128,2048]{1,0:T(8,128)(2,1)}, bf16[128,2048]{1,0:T(8,128)(2,1)}, u32[]{:S(2)}, u32[]{:S(2)}) collective-permute-start(bf16[128,2048]{1,0:T(8,128)(2,1)} %get-tuple-element.1275), channel_id=1, source_target_pairs={{0,1},{1,0},{2,3},{3,2},{4,5},{5,4},{6,7},{7,6},{8,9},{9,8},{10,11... | collective-permute-start | bytes 1572872 | tf_op jit(solution)/shard_map/ppermute | solution.py:642
  324.7 57.1 %collective-permute-start.63 = (bf16[128,2048]{1,0:T(8,128)(2,1)}, bf16[128,2048]{1,0:T(8,128)(2,1)}, u32[]{:S(2)}, u32[]{:S(2)}) collective-permute-start(bf16[128,2048]{1,0:T(8,128)(2,1)} %get-tuple-element.1275), channel_id=1, source_target_pairs={{0,2},{1,3},{2,0},{3,1},{4,6},{5,7},{6,4},{7,5},{8,10},{9,11},{10,... | collective-permute-start | bytes 1572872 | tf_op jit(solution)/shard_map/ppermute | solution.py:642
  326.1 55.7 %collective-permute-start.64 = (bf16[128,2048]{1,0:T(8,128)(2,1)}, bf16[128,2048]{1,0:T(8,128)(2,1)}, u32[]{:S(2)}, u32[]{:S(2)}) collective-permute-start(bf16[128,2048]{1,0:T(8,128)(2,1)} %get-tuple-element.1275), channel_id=1, source_target_pairs={{0,3},{1,2},{2,1},{3,0},{4,7},{5,6},{6,5},{7,4},{8,11},{9,10},{10,... | collective-permute-start | bytes 1572872 | tf_op jit(solution)/shard_map/ppermute | solution.py:642
  428.5 48.1 %collective-permute-start.6 = (bf16[128,2048]{1,0:T(8,128)(2,1)}, bf16[128,2048]{1,0:T(8,128)(2,1)}, u32[]{:S(2)}, u32[]{:S(2)}) collective-permute-start(bf16[128,2048]{1,0:T(8,128)(2,1)} %get-tuple-element.826), channel_id=1, source_target_pairs={{0,1},{1,0},{2,3},{3,2},{4,5},{5,4},{6,7},{7,6},{8,9},{9,8},{10,11... | collective-permute-start | bytes 1572872 | tf_op jit(solution)/shard_map/cond/branch_1_fun/ppermute | solution.py:642
  428.6 48.1 %collective-permute-start.7 = (bf16[128,2048]{1,0:T(8,128)(2,1)}, bf16[128,2048]{1,0:T(8,128)(2,1)}, u32[]{:S(2)}, u32[]{:S(2)}) collective-permute-start(bf16[128,2048]{1,0:T(8,128)(2,1)} %get-tuple-element.827), channel_id=1, source_target_pairs={{0,2},{1,3},{2,0},{3,1},{4,6},{5,7},{6,4},{7,5},{8,10},{9,11},{10,... | collective-permute-start | bytes 1572872 | tf_op jit(solution)/shard_map/cond/branch_1_fun/ppermute | solution.py:642
  430.0 46.7 %collective-permute-start.8 = (bf16[128,2048]{1,0:T(8,128)(2,1)}, bf16[128,2048]{1,0:T(8,128)(2,1)}, u32[]{:S(2)}, u32[]{:S(2)}) collective-permute-start(bf16[128,2048]{1,0:T(8,128)(2,1)} %get-tuple-element.828), channel_id=1, source_target_pairs={{0,3},{1,2},{2,1},{3,0},{4,7},{5,6},{6,5},{7,4},{8,11},{9,10},{10,... | collective-permute-start | bytes 1572872 | tf_op jit(solution)/shard_map/cond/branch_1_fun/ppermute | solution.py:642
  483.8 111.1 %all-to-all-start.3 = ((f32[32,1,10860]{2,1,0:T(1,128)}), f32[32,1,10860]{2,1,0:T(1,128)S(1)}, u32[]{:S(2)}, u32[]{:S(2)}) async-start(f32[32,1,10860]{2,1,0:T(1,128)} %all_to_all.48), calls=%async_computation.3 | async-start | bytes 2785280 | tf_op jit(solution)/shard_map/all_to_all | solution.py:1259
  486.5 50.0 %collective-permute-start.10 = (bf16[3,128,2048]{2,1,0:T(8,128)(2,1)}, bf16[3,128,2048]{2,1,0:T(8,128)(2,1)}, u32[]{:S(2)}, u32[]{:S(2)}) collective-permute-start(bf16[3,128,2048]{2,1,0:T(8,128)(2,1)} %get-tuple-element.885), channel_id=1, source_target_pairs={{0,16},{8,24},{16,0},{24,8},{1,17},{9,25},{17,1},{25,9},{2,18},{10... | collective-permute-start | bytes 4718600 | tf_op jit(solution)/shard_map/cond/branch_1_fun/ppermute | solution.py:639
  488.3 48.3 %collective-permute-start.9 = (bf16[3,128,2048]{2,1,0:T(8,128)(2,1)}, bf16[3,128,2048]{2,1,0:T(8,128)(2,1)}, u32[]{:S(2)}, u32[]{:S(2)}) collective-permute-start(bf16[3,128,2048]{2,1,0:T(8,128)(2,1)} %get-tuple-element.884), channel_id=1, source_target_pairs={{0,8},{8,0},{16,24},{24,16},{1,9},{9,1},{17,25},{25,17},{2,10},{10... | collective-permute-start | bytes 4718600 | tf_op jit(solution)/shard_map/cond/branch_1_fun/ppermute | solution.py:639
  556.9 34.0 %collective-permute-start.39 = (bf16[512,1024]{1,0:T(8,128)(2,1)}, bf16[512,1024]{1,0:T(8,128)(2,1)}, u32[]{:S(2)}, u32[]{:S(2)}) collective-permute-start(bf16[512,1024]{1,0:T(8,128)(2,1)} %pad_maximum_fusion.9), channel_id=1, source_target_pairs={{0,8},{8,0},{16,24},{24,16},{1,9},{9,1},{17,25},{25,17},{2,10},{10... | collective-permute-start | bytes 3145736 | tf_op jit(solution)/shard_map/cond/branch_1_fun/ppermute | solution.py:639
  558.3 32.6 %collective-permute-start.40 = (bf16[512,1024]{1,0:T(8,128)(2,1)}, bf16[512,1024]{1,0:T(8,128)(2,1)}, u32[]{:S(2)}, u32[]{:S(2)}) collective-permute-start(bf16[512,1024]{1,0:T(8,128)(2,1)} %pad_maximum_fusion.10), channel_id=1, source_target_pairs={{0,16},{8,24},{16,0},{24,8},{1,17},{9,25},{17,1},{25,9},{2,18},{10... | collective-permute-start | bytes 3145736 | tf_op jit(solution)/shard_map/cond/branch_1_fun/ppermute | solution.py:639
  595.0 31.5 %all-to-all-start.4 = ((bf16[8,64,1024]{2,1,0:T(8,128)(2,1)}), bf16[8,64,1024]{2,1,0:T(8,128)(2,1)S(1)}, u32[]{:S(2)}, u32[]{:S(2)}) async-start(bf16[8,64,1024]{2,1,0:T(8,128)(2,1)} %copy-done.18), calls=%async_computation.4 | async-start | bytes 2097152 | tf_op jit(solution)/shard_map/all_to_all | solution.py:1342
  627.3 50.6 %all-to-all-start.5 = ((f32[32,1,512]{2,1,0:T(1,128)}), f32[32,1,512]{2,1,0:T(1,128)S(1)}, u32[]{:S(2)}, u32[]{:S(2)}) async-start(f32[32,1,512]{2,1,0:T(1,128)} %copy.289), calls=%async_computation.5 | async-start | bytes 131072 | tf_op jit(solution)/shard_map/all_to_all | solution.py:1358
  677.9 40.8 %all-to-all-start.6 = ((bf16[8,64,1024]{2,1,0:T(8,128)(2,1)}), bf16[8,64,1024]{2,1,0:T(8,128)(2,1)S(1)}, u32[]{:S(2)}, u32[]{:S(2)}) async-start(bf16[8,64,1024]{2,1,0:T(8,128)(2,1)} %get-tuple-element.1369), calls=%async_computation.7 | async-start | bytes 2097152 | tf_op jit(solution)/shard_map/all_to_all | solution.py:1359
  (100 other events, 1059.2 us)
Sparse Core Ops, SparseCore 0:
  158.3 80.7 all-gather.2
  476.8 98.3 reduce-scatter.1

commit v3 on v2

--- a/solution.py
+++ b/solution.py
@@ -81,17 +81,22 @@
 def places(first, count):
     row = lax.broadcasted_iota(jnp.int32, (LANES, count * ROWS), 0)
     col = lax.broadcasted_iota(jnp.int32, (LANES, count * ROWS), 1)
-    return (row == first + col // ROWS).astype(SINGLE)
+    return (row == first + col // ROWS).astype(NARROW)
+
+
+def two_parts(values):
+    high = values.astype(NARROW)
+    return jnp.concatenate([high, (values - high.astype(SINGLE)).astype(NARROW)], 0)
 
 
 def spread_out(coef, count, entries, stride):
     mask = same_token((ROWS, entries * ROWS))
+    parts = two_parts(coef)
     highs, lows = [], []
     for s in range(count):
-        full = jnp.where(mask, times(coef, places(s * stride, entries), EXACT), 0.0)
-        high = full.astype(NARROW)
-        highs.append(high)
-        lows.append((full - high.astype(SINGLE)).astype(NARROW))
+        full = times(parts, places(s * stride, entries))
+        highs.append(jnp.where(mask, full[:ROWS], 0.0).astype(NARROW))
+        lows.append(jnp.where(mask, full[ROWS:], 0.0).astype(NARROW))
     return jnp.concatenate(highs, 0), jnp.concatenate(lows, 0)
 
 
@@ -100,9 +105,9 @@
     total = None
     for s in range(count):
         own = jnp.where(mask, products[s * ROWS : (s + 1) * ROWS], 0.0)
-        term = times_transposed(own, places(s * stride, entries), EXACT)
+        term = times_transposed(two_parts(own), places(s * stride, entries))
         total = term if s == 0 else total + term
-    return total
+    return total[:ROWS] + total[ROWS:]
 
 
 def blend_streams(hist, mix, streams):
@@ -369,9 +374,10 @@
     return values * rope[0] + sign * (forward * rope[1] + backward * rope[2])
 
 
-def allowed_pairs(row, column, length):
-    query = lax.broadcasted_iota(jnp.int32, (length, length), 0)
-    key = lax.broadcasted_iota(jnp.int32, (length, length), 1)
+def allowed_pairs(row, column):
+    size = row.shape[1]
+    query = lax.broadcasted_iota(jnp.int32, (size, size), 0)
+    key = lax.broadcasted_iota(jnp.int32, (size, size), 1)
     return (key <= query) & (row == column)
 
 
@@ -387,22 +393,15 @@
     for i in range(3):
         tokens = jnp.concatenate([own[i], other[i]], 0)
         linear = times(tokens, weight[:, i * cols : (i + 1) * cols]) + bias[:, i * cols : (i + 1) * cols]
-        if i == 2:
-            qkv[i] = linear.astype(NARROW)
-            continue
-        for s in range(2):
-            for start in range(0, cols, HEAD_DIM):
-                piece = linear[s * length : (s + 1) * length, start : start + HEAD_DIM]
-                qkv[i, s * length : (s + 1) * length, start : start + HEAD_DIM] = turn(
-                    piece, rope, 1.0
-                ).astype(NARROW)
-    for s in range(2):
-        allowed = allowed_pairs(doc_row[s], doc_column[s], length)
-        rows = slice(s * length, (s + 1) * length)
         for start in range(0, cols, HEAD_DIM):
             head = slice(start, start + HEAD_DIM)
-            probs = probabilities(qkv[0, rows, head], qkv[1, rows, head], allowed)
-            mixed[rows, head] = times(probs.astype(NARROW), qkv[2, rows, head]).astype(NARROW)
+            piece = linear[:, head]
+            qkv[i, :, head] = (turn(piece, rope, 1.0) if i < 2 else piece).astype(NARROW)
+    allowed = allowed_pairs(doc_row[...], doc_column[...])
+    for start in range(0, cols, HEAD_DIM):
+        head = slice(start, start + HEAD_DIM)
+        probs = probabilities(qkv[0, :, head], qkv[1, :, head], allowed)
+        mixed[:, head] = times(probs.astype(NARROW), qkv[2, :, head]).astype(NARROW)
     result = times_transposed(mixed[...], weight[:, 3 * cols :])
     out_own[...] = result[:length]
     out_other[...] = result[length:].astype(NARROW)
@@ -416,26 +415,23 @@
     scale = HEAD_DIM ** (-0.5)
     arriving = jnp.concatenate([own[...], other[...]], 0)
     grad_mixed = times(arriving, weight[:, 3 * cols :]).astype(NARROW)
+    allowed = allowed_pairs(doc_row[...], doc_column[...])
     for start in range(0, cols, HEAD_DIM):
         head = slice(start, start + HEAD_DIM)
-        sums = [jnp.zeros((1, HEAD_DIM), SINGLE) for _ in range(3)]
-        for s in range(2):
-            allowed = allowed_pairs(doc_row[s], doc_column[s], length)
-            rows = slice(s * length, (s + 1) * length)
-            query, key, value = (qkv[i, rows, head] for i in range(3))
-            grad = grad_mixed[rows, head]
-            probs = probabilities(query, key, allowed)
-            grad_value = transposed_times(probs.astype(NARROW), grad)
-            grad_probs = times_transposed(grad, value)
-            inner = jnp.sum(probs * grad_probs, -1, keepdims=True)
-            grad_scores = (probs * (grad_probs - inner)).astype(NARROW)
-            grad_query = turn(times(grad_scores, key) * scale, rope, -1.0)
-            grad_key = turn(transposed_times(grad_scores, query) * scale, rope, -1.0)
-            for i, values in enumerate((grad_query, grad_key, grad_value)):
-                sums[i] = sums[i] + jnp.sum(values, 0, keepdims=True)
-                grad_linear[i, rows, head] = values.astype(NARROW)
-        for i in range(3):
-            grad_bias[:, i * cols + start : i * cols + start + HEAD_DIM] = sums[i]
+        query, key, value = (qkv[i, :, head] for i in range(3))
+        grad = grad_mixed[:, head]
+        probs = probabilities(query, key, allowed)
+        grad_value = transposed_times(probs.astype(NARROW), grad)
+        grad_probs = times_transposed(grad, value)
+        inner = jnp.sum(probs * grad_probs, -1, keepdims=True)
+        grad_scores = (probs * (grad_probs - inner)).astype(NARROW)
+        grad_query = turn(times(grad_scores, key) * scale, rope, -1.0)
+        grad_key = turn(transposed_times(grad_scores, query) * scale, rope, -1.0)
+        for i, values in enumerate((grad_query, grad_key, grad_value)):
+            grad_bias[:, i * cols + start : i * cols + start + HEAD_DIM] = jnp.sum(
+                values, 0, keepdims=True
+            )
+            grad_linear[i, :, head] = values.astype(NARROW)
     for i in range(3):
         result = times_transposed(grad_linear[i], weight[:, i * cols : (i + 1) * cols])
         out_own[i] = result[:length]
@@ -709,7 +705,7 @@
     hidden_sends = order.wait(*hidden_sends)
     head_block = lambda i: spec((rows, cols), lambda j: (0, i * fsdp + j))
     from_qkv, from_out = order.hold(w_qkv, w_out)
-    heads_sends = pl.pallas_call(
+    heads = pl.pallas_call(
         pack_heads_kernel,
         grid=(fsdp,),
         in_specs=[head_block(0), head_block(1), head_block(2), head_block(0)],
@@ -719,12 +715,11 @@
         cost_estimate=cost(10**6, 3 * 10**6),
         name="pack_heads",
     )(from_qkv, from_qkv, from_qkv, from_out)
-    heads_sends = order.wait(heads_sends)
-    mix_padded = order.wait(jnp.pad(mix_in, ((0, 0), (0, LANES - count * entries))))
+    heads = order.wait(heads)
     gathered = order.wait(gathered)
-    heads_came = lax.all_to_all(order.hold(heads_sends), RING, 0, 0, tiled=True)
     hidden_going = order.hold(*hidden_sends)
     hidden_hops = [hop_rep(hidden_going[k], k) for k in range(1, rep)]
+    heads_came = lax.all_to_all(order.hold(heads), RING, 0, 0, tiled=True)
 
     def fields_of(gathered):
         fields, start = [], 0
@@ -734,6 +729,7 @@
         return fields
 
     def open_layer(inner):
+        mix_padded = jnp.pad(mix_in, ((0, 0), (0, LANES - count * entries)))
         fields = fields_of(gathered)
         gains = fields[0].reshape(devices, 3, rows).transpose(1, 0, 2).reshape(3, width)
         shifts = fields[1].reshape(devices, 2, rows).transpose(1, 0, 2).reshape(2, width)
@@ -773,16 +769,13 @@
             name="history_dots",
         )(history, cotangent, token_weight)
         dots = inner.wait(dots)
-        return normed, affine, dots, token_weight, inner.wait(*qkv_near)
-
-    normed, affine, dots, token_weight, qkv_near = order.scope(open_layer)
+        return normed, affine, dots, token_weight, inner.wait(*qkv_near), mix_padded
+
+    normed, affine, dots, token_weight, qkv_near, mix_padded = order.scope(open_layer)
+    heads_came = order.wait(heads_came)
     qkv_norm, resid_norm, last = normed
-    heads_came = order.wait(heads_came)
     hidden_came = [hidden_sends[0], *order.wait(*hidden_hops)]
 
-    first_mix = order.hold(w_mix1).astype(NARROW).reshape(1, -1)
-    first_mix = order.wait(jnp.broadcast_to(first_mix, (devices, rows * hid)))
-    first_mix = lax.all_to_all(first_mix, AXES, 0, 0, tiled=True)
     resid_norm = order.hold(resid_norm)
     resid_hops = [hop_rep(resid_norm, k) for k in range(1, rep)]
 
@@ -801,6 +794,8 @@
         return joined.reshape(2, part, hid_cols)
 
     def prepare(inner):
+        mix_copies = jnp.pad(w_mix1.astype(NARROW), ((0, 0), (0, LANES - hid)))
+        mix_copies = inner.wait(jnp.broadcast_to(mix_copies[None], (devices, rows, LANES)))
         fields = fields_of(inner.hold(gathered))
         gain = fields[0].reshape(devices, 3, rows)[:, 2].reshape(1, width).astype(SINGLE)
         qkv_bias = fields[2].reshape(3, fsdp, cols).astype(SINGLE)
@@ -814,7 +809,8 @@
         doc_rows = []
         for m in range(chips):
             pair = lax.dynamic_index_in_dim(docs_line, chip ^ m, 0, False)
-            doc_rows.append(jnp.where(core == 0, pair, pair[::-1]))
+            pair = pair + doc_group.shape[1] * jnp.arange(2, dtype=SINGLE)[:, None]
+            doc_rows.append(jnp.where(core == 0, pair, pair[::-1]).reshape(1, 2 * length))
         position = jnp.arange(length).astype(SINGLE)
         frequency = 10000.0 ** (-jnp.arange(0, ROT, 2).astype(SINGLE) / ROT)
         angle = position[:, None] * frequency[None, :]
@@ -828,22 +824,23 @@
                 jnp.concatenate([nothing, sine, jnp.zeros((length, rest), SINGLE)], 1),
             ]
         )
-        pairs = [(pair[:, None, :], pair[:, :, None]) for pair in doc_rows]
+        rope = jnp.concatenate([rope, rope], 1)
+        pairs = [(pair, pair.reshape(2 * length, 1)) for pair in doc_rows]
         ready = (gain, my_qkv_bias.reshape(1, 3 * cols), my_first_bias, branch_bias, rope, pairs)
         leaves, tree = jax.tree.flatten(ready)
-        return jax.tree.unflatten(tree, inner.wait(*leaves))
+        return mix_copies, jax.tree.unflatten(tree, inner.wait(*leaves))
 
     def spread_weights(inner):
         joined = inner.scope(join_hidden)
         near = [hop_chip(joined, m) for m in around]
-        prepared = inner.scope(prepare)
+        mix_copies, prepared = inner.scope(prepare)
+        first_mix = lax.all_to_all(inner.hold(mix_copies), AXES, 0, 0, tiled=True)
         near = inner.wait(*near)
-        return joined, near, prepared
-
-    hidden_own, hidden_near, prepared = order.scope(spread_weights)
+        return joined, near, inner.wait(first_mix).reshape(width, LANES), prepared
+
+    hidden_own, hidden_near, mix_first, prepared = order.scope(spread_weights)
     gain, my_qkv_bias, my_first_bias, branch_bias, rope, doc_pairs = prepared
     resid_hops = order.wait(*resid_hops)
-    first_mix = order.wait(first_mix)
 
     heads_all = lax.all_gather(order.hold(heads_came), "rep", axis=0)
 
@@ -883,14 +880,12 @@
 
     def feed_forward(inner):
         ends = []
-        mix_first = jnp.pad(inner.hold(first_mix).reshape(width, hid), ((0, 0), (0, LANES - hid)))
         if square:
             upper = hop_chip(inner.hold(hidden_near[0])[0:1], 2)
             lower = hop_chip(inner.hold(hidden_near[1])[1:2], 1)
         whole = inner.wait(jnp.stack([resid_norm, *resid_hops]))
         other = inner.wait(swap_core(whole))
         qkv_other = inner.scope(lambda _: [swap_core(values) for values in qkv_first])
-        mix_first = inner.wait(mix_first)
         if square:
             ends = inner.wait(upper, lower)
             halves = pass_on(inner.hold(*qkv_near), 1)
@@ -911,9 +906,9 @@
             qkv_last.append(inner.wait(jnp.concatenate(inner.wait(*halves), 1)))
             qkv_other.append(inner.wait(swap_core(qkv_last[0])))
         acts, slopes = (act_own, act_other), (slope_own, slope_other)
-        return ends, sides, acts, slopes, branch_places, qkv_last, qkv_other, mix_first
-
-    ends, resid_sides, acts, slopes, branch_places, qkv_last, qkv_other, mix_first = order.scope(
+        return ends, sides, acts, slopes, branch_places, qkv_last, qkv_other
+
+    ends, resid_sides, acts, slopes, branch_places, qkv_last, qkv_other = order.scope(
         feed_forward
     )
     first_parts = [hidden_own, *hidden_near, *ends[:1]]
@@ -1170,38 +1165,52 @@
             *hidden_back_side(first_parts, second_parts, inner.hold(grad_own), slopes[0])
         )
         came = inner.wait(*came)
+        grad_other = came[1].reshape(rep * length, width)
         far_term = inner.wait(add_up(returned[far][2], came[0]))
         halves = send_far(far_term, 1) if square else ()
-
-        def other_side(inner):
-            grad_sides = (grad_own, came[1].reshape(rep * length, width))
-            low_other, sum_other, back = inner.wait(
-                *hidden_back_side(first_parts, second_parts, grad_sides[1], slopes[1])
-            )
-            back = swap_core(back)
-            grads = outer(inner, (inner.hold(grad_sides[0]), grad_sides[1]), acts)
-            back = inner.wait(back)
-            merged = [
-                merge(back_own[k * length : (k + 1) * length], back[k * length : (k + 1) * length])
-                for k in range(rep)
-            ]
-            return grads, low_other, sum_own + sum_other, merged
-
-        grads, low_other, first_bias, merged = inner.scope(other_side)
+        low_other, sum_other, back = inner.wait(
+            *hidden_back_side(first_parts, second_parts, inner.hold(grad_other), slopes[1])
+        )
+
+        def sums_of_cores(_):
+            came = swap_core(back)
+            at = lambda values, k: values[k * length : (k + 1) * length]
+            return [merge(at(back_own, k), at(came, k)) for k in range(rep)]
+
+        merged = inner.scope(sums_of_cores)
         halves = inner.wait(*halves) if square else [far_term]
-        return grads, low_own, low_other, first_bias, merged, halves, came[0], came[2]
-
-    second_grads, low_own, low_other, grad_first_bias, grad_resid, halves, far_came, own_came = (
-        order.scope(feed_forward_back)
+        lows = (low_own, low_other)
+        return (grad_own, grad_other), lows, sum_own + sum_other, merged, halves, came[0], came[2]
+
+    grad_sides, grad_hidden, grad_first_bias, grad_resid, halves, far_came, own_came = order.scope(
+        feed_forward_back
     )
+
+    def total_hidden(inner, own, hops):
+        total = own.astype(SINGLE)
+        for values in inner.wait(*hops):
+            total = total + values.astype(SINGLE)
+        return inner.wait(total.astype(NARROW).reshape(group, rows, hid_cols))
+
+    def whole_rows(came):
+        return came.transpose(1, 0, 2).reshape(rows, hidden).astype(SINGLE)
+
+    def exchange(sums):
+        widths = [values.shape[1] for values in sums]
+        return widths, lax.all_to_all(jnp.concatenate(sums, 1), AXES, 0, 0, tiled=True)
 
     def attention_back(inner):
         results = {0: returned[0], far: returned[far]}
-        middle = range(1, far)
-        swaps = []
-        for m in middle:
+        second_grads = outer(inner, (inner.hold(grad_sides[0]), grad_sides[1]), acts)
+        halves_out = send_far(inner.hold(second_grads[far]), 0)
+        results[1] = back(inner, 1, branch_own[1], branch_other[1])
+        held = second_grads[1:]
+        if square:
+            halves_out = inner.wait(*halves_out)
+            held = inner.wait(*take_along(second_grads[1:far], halves_out, 0))
+        hops = [hop_chip(held[m - 1], m) for m in around]
+        for m in range(2, far):
             results[m] = back(inner, m, branch_own[m], branch_other[m])
-            swaps.append(swap_core(results[m][3]))
         linears = inner.hold(*[results[m][0] for m in range(chips)])
         grad_heads = pl.pallas_call(
             functools.partial(heads_grad_kernel, chips),
@@ -1222,10 +1231,9 @@
             *mixed_low,
         )
         grad_heads = inner.wait(grad_heads)
-        swaps = inner.wait(*swaps)
-        owns = [results[m][2] for m in range(chips)]
-        near_terms = near_sums(inner, owns, [None, *swaps, far_came], halves)
-        return grad_heads, near_terms, [results[m][1] for m in range(chips)]
+        hops = inner.wait(*hops)
+        middle = [results[m] for m in range(1, far)]
+        return grad_heads, middle, second_grads[0], hops
 
     def residual_back(inner):
         hops = inner.hold(*grad_resid)
@@ -1233,64 +1241,72 @@
         results = inner.scope(attention_back)
         return inner.wait(*hops), *results
 
-    resid_hops, grad_heads, near_terms, qkv_biases = order.scope(residual_back)
+    resid_hops, grad_heads, returned[1:far], second_own_grad, second_hops = order.scope(residual_back)
+    qkv_biases = [results[1] for results in returned]
     grad_resid = [grad_resid[0], *resid_hops]
 
     def by_owner(vector):
         return vector.reshape(-1, devices, rows).transpose(1, 0, 2).reshape(devices, -1)
 
     grad_heads = lax.psum_scatter(grad_heads, "rep", scatter_dimension=0, tiled=False)
+    def second_sum(inner):
+        return total_hidden(inner, second_own_grad, second_hops)
+
+    second_total = order.scope(second_sum)
+    second_came = lax.all_to_all(order.hold(second_total), GROUP, 0, 0, tiled=True)
+
+    def send_terms(inner):
+        middle = range(1, far)
+        swaps = [swap_core(inner.hold(returned[m][3])) for m in middle]
+        first_grads = outer(inner, (inner.hold(resid_sides[0]), resid_sides[1]), grad_hidden)
+        swaps = list(inner.wait(*swaps)) if len(swaps) > 1 else [inner.wait(*swaps)]
+        owns = [results[2] for results in returned]
+        near_terms = near_sums(inner, owns, [None, *swaps, far_came], halves)
+        qkv_back = [hop_chip(near_terms[m - 1], m) for m in around]
+        first_halves = send_far(inner.hold(first_grads[far]), 0)
+
+        def pack_sums(_):
+            qkv_bias_all = lax.dynamic_update_index_in_dim(
+                jnp.zeros((3, fsdp, cols), SINGLE),
+                sum(qkv_biases).reshape(3, cols),
+                chip * 2 + core,
+                1,
+            )
+            tail = jnp.concatenate(
+                [grad_pre_sum[0, :hid], grad_w_mix2.reshape(-1), grad_coef_sum[0, :mixes]]
+            )
+            sums = [
+                by_owner(grad_rms_gain[0]),
+                qkv_bias_all.reshape(devices, -1),
+                grad_branch_bias.reshape(devices, -1),
+                grad_w_mix1.reshape(devices, -1),
+                jnp.broadcast_to(tail[None], (devices, tail.shape[0])),
+            ]
+            size = sum(values.shape[1] for values in sums)
+            empty = -size % (ROWS * LANES)
+            sums.append(jnp.zeros((devices, empty), SINGLE))
+            return jnp.concatenate(sums, 1).astype(NARROW).reshape(devices, ROWS, -1)
+
+        sums = inner.scope(pack_sums)
+        held = first_grads[1:]
+        if square:
+            first_halves = inner.wait(*first_halves)
+        qkv_back = inner.wait(*qkv_back)
+        if square:
+            held = inner.wait(*take_along(first_grads[1:far], first_halves, 0))
+        return first_grads[0], held, qkv_back, sums
+
+    first_own_grad, first_terms, qkv_back, sums = order.scope(send_terms)
+    second_came = order.wait(second_came)
+    sums = order.hold(sums)
+    sums = lax.all_to_all(sums, AXES, 0, 0, tiled=True)
     widths = [rows, 3 * cols * fsdp // devices, rows, rows * hid]
-    held_bias = order.hold(grad_branch_bias)
-    qkv_bias_all = lax.dynamic_update_index_in_dim(
-        jnp.zeros((3, fsdp, cols), SINGLE), sum(qkv_biases).reshape(3, cols), chip * 2 + core, 1
-    )
-    tail = jnp.concatenate(
-        [grad_pre_sum[0, :hid], grad_w_mix2.reshape(-1), grad_coef_sum[0, :mixes]]
-    )
-    sums = [
-        by_owner(grad_rms_gain[0]),
-        qkv_bias_all.reshape(devices, -1),
-        held_bias.reshape(devices, -1),
-        grad_w_mix1.reshape(devices, -1),
-        jnp.broadcast_to(tail[None], (devices, tail.shape[0])),
-    ]
-    sums = order.wait(jnp.concatenate(sums, 1))
-    sums = lax.all_to_all(sums, AXES, 0, 0, tiled=True)
-
-    def total_hidden(inner, own, hops):
-        total = own.astype(SINGLE)
-        for values in inner.wait(*hops):
-            total = total + values.astype(SINGLE)
-        return inner.wait(total.astype(NARROW).reshape(group, rows, hid_cols))
-
-    def whole_rows(came):
-        return came.transpose(1, 0, 2).reshape(rows, hidden).astype(SINGLE)
-
-    def exchange(sums):
-        widths = [values.shape[1] for values in sums]
-        return widths, lax.all_to_all(jnp.concatenate(sums, 1), AXES, 0, 0, tiled=True)
-
-    def send_terms(inner):
-        held = inner.hold(*near_terms)
-        qkv_back = [hop_chip(held[m - 1], m) for m in around]
-        first_grads = outer(inner, (inner.hold(resid_sides[0]), resid_sides[1]), (low_own, low_other))
-        return first_grads, inner.wait(*qkv_back)
-
-    first_grads, qkv_back = order.scope(send_terms)
-
-    def near_of(inner, grads):
-        halves = send_far(inner.hold(grads[far]), 0)
-        if not square:
-            return inner.wait(*grads[1:])
-        halves = inner.wait(*halves)
-        return inner.wait(*take_along(grads[1:far], halves, 0))
 
     qkv_rest = [own_came, *qkv_back]
 
     def close_layer(inner):
-        held = near_of(inner, second_grads)
-        second_hops = [hop_chip(held[m - 1], m) for m in around]
+        held = inner.hold(*first_terms)
+        first_hops = [hop_chip(held[m - 1], m) for m in around]
         close_from = inner.hold(history, cotangent)
         grad_history, grad_mix_in, grad_affine = pl.pallas_call(
             functools.partial(close_kernel, chips, len(qkv_rest), rep),
@@ -1335,20 +1351,10 @@
         )
         grad_history, grad_mix_in, grad_affine = inner.wait(grad_history, grad_mix_in, grad_affine)
 
-        return grad_history, grad_mix_in, grad_affine, total_hidden(inner, second_grads[0], second_hops)
-
-    grad_history, grad_mix_in, grad_affine, second_total = order.scope(close_layer)
+        return grad_history, grad_mix_in, grad_affine, total_hidden(inner, first_own_grad, first_hops)
+
+    grad_history, grad_mix_in, grad_affine, first_total = order.scope(close_layer)
     sums = order.wait(sums)
-    second_came = lax.all_to_all(order.hold(second_total), GROUP, 0, 0, tiled=True)
-
-    def collect_first(inner):
-        held = near_of(inner, first_grads)
-        first_hops = [hop_chip(held[m - 1], m) for m in around]
-        total = inner.wait(jnp.sum(inner.hold(sums), 0))
-        return total, total_hidden(inner, first_grads[0], first_hops)
-
-    total, first_total = order.scope(collect_first)
-    second_came = order.wait(second_came)
     first_bias_all = lax.dynamic_update_index_in_dim(
         jnp.zeros((group, hid_cols), SINGLE), grad_first_bias[0], core * rep + line, 0
     )
@@ -1359,6 +1365,7 @@
     first_came = lax.all_to_all(order.hold(first_total), GROUP, 0, 0, tiled=True)
     grad_w_fc2 = order.wait(whole_rows(second_came))
     every = order.wait(jnp.sum(every, 0))
+    total = order.wait(jnp.sum(sums.astype(SINGLE), 0).reshape(-1))
     grad_heads = order.wait(grad_heads)
 
     def around_ring(inner):
@@ -1403,7 +1410,7 @@
         outs[3].reshape(rows, hid),
         outs[4][:hid],
         outs[4][hid : hid + hid * mixes].reshape(hid, mixes),
-        outs[4][hid + hid * mixes :],
+        outs[4][hid + hid * mixes : hid + hid * mixes + mixes],
     )
 
 

time: 734 us -> 654 us (0.89)
  waiting for transfers between devices: 221 us -> 164 us
  Pallas kernels: 231 us -> 211 us
  blocking collectives: 0 us -> 11.7 us
    ppermute x31, waiting for transfers between devices: 168 us -> 129 us  [hop_chip(): return lax.ppermute(values, 'chip', [(i, i ^ m) for i in range(chips)])]
    all_to_all x1, waiting for transfers between devices: 25 us -> 0.01 us  [on_device(): lax.all_to_all(order.hold(second_total), GROUP, 0, 0, tiled=True)]
    all_to_all x0 -> x1, blocking collectives: none -> 11.7 us  [on_device(): every = order.wait(lax.all_to_all(every, AXES, 0, 0, tiled=True))]
    pallas_call x1, Pallas kernels: 28.8 us -> 18.6 us  [close_layer(): pl.pallas_call(functools.partial(close_kernel, chips, len(qkv_rest), rep)...]
    cond x69 -> x78, local copies, waits for them, and re-layouts: 9.6 us -> 16.2 us
    another operation x15 -> x19, local copies, waits for them, and re-layouts: 19.1 us -> 22.3 us
    another operation x17 -> x18, loops' own time: 14.9 us -> 13.2 us  [scope(): results = lax.cond(self.hold(self.legal), inside, never)]
  transfers between devices with their start and end apart: 74 -> 73, of which waited for: 30 -> 29; matrix products, arithmetic and copies ran while one was open for 17% -> 19% of each run, Pallas kernels for 30% -> 31%
where the time goes in v3:
time: 654 us; the launch traced here: 648 us
  Pallas kernels  211 us (32%)
  waiting for transfers between devices  164 us (25%)
  local copies, waits for them, and re-layouts  95.7 us (15%)
  starting transfers between devices  88.8 us (14%)
  other arithmetic  47.1 us (7%)
  between operations  14.8 us (2%)
  loops' own time  13.2 us (2%)
  blocking collectives  11.7 us (2%)
    ppermute x31, waiting for transfers between devices, hop_chip(): return lax.ppermute(values, 'chip', [(i, i ^ m) for i in range(chips)])  129 us
    ppermute x31, starting transfers between devices, hop_chip(): return lax.ppermute(values, 'chip', [(i, i ^ m) for i in range(chips)])  34.9 us
    pallas_call x4, Pallas kernels, attend_back(): pl.pallas_call(attend_back_kernel, out_shape=[shape((3, 2 * length, cols)...  31.5 us
    ppermute x19, waiting for transfers between devices, swap_core(): return lax.ppermute(values, 'core', [(0, 1), (1, 0)])  27.1 us
    pallas_call x4, Pallas kernels, attend(): pl.pallas_call(attend_kernel, out_shape=[shape((3, 2 * length, cols), NAR...  26.5 us
    another operation x19, local copies, waits for them, and re-layouts  22.3 us
    ppermute x15, starting transfers between devices, hop_rep(): return lax.ppermute(values, 'rep', [(i, i ^ k) for i in range(rep)])  22.1 us
    pallas_call x2, Pallas kernels, hidden_back_side(): pl.pallas_call(functools.partial(hidden_back_kernel, chips, bool(came)),...  19.4 us
  transfers between devices with their start and end apart: 73, of which 29 were waited for; matrix products, arithmetic and copies ran while one was open for 19% of the time, Pallas kernels for 31%

profile of v3, /device:TPU:0, one launch (start us, length us, event | category | flops | bytes accessed | tf_op | source)
XLA Modules:
  0.0 647.8 jit_solution(16361796111359821797)
XLA Ops:
  39.2 47.6 %conditional.18 = (bf16[3,128,2048]{2,1,0:T(8,128)(2,1)}, bf16[128,2048]{1,0:T(8,128)(2,1)}, f32[128,2048]{1,0:T(8,128)}, f32[4,2048]{1,0:T(4,128)}, f32[128,128...) conditional(s32[]{:T(128)} %convert_element_type.363, ...), branch_computations={%region_0.0_spmd, %region_1.4_spmd} | conditional | flops 275264 | bytes 13333348 | solution.py:581
  40.2 9.0 %streams.1 = (bf16[3,128,2048]{2,1,0:T(8,128)(2,1)}, bf16[128,2048]{1,0:T(8,128)(2,1)}, f32[128,2048]{1,0:T(8,128)}) custom-call(s32[1]{0:T(128)} %get-tuple-element.488.chip, bf16[9,128,2048]{2,1,0:T(8,128)(2,1)} %get-tuple-element.489.hist, f32[128,128]{1,0:T(8,128)S(1)} %pad.15.mix, f32[4,2048]{1,0:T(4,128)S(1)} %maximum_convert_fusion.affine), custom_call_target="tpu_custom_call" | custom-call | flops 100000 | bytes 10000 | tf_op jit(solution)/shard_map/cond/branch_1_fun/streams/pallas_call | solution.py:737
  62.1 23.3 %collective-permute-done.39 = bf16[3,128,2048]{2,1,0:T(8,128)(2,1)} collective-permute-done((bf16[3,128,2048]{2,1,0:T(8,128)(2,1)}, bf16[3,128,2048]{2,1,0:T(8,128)(2,1)}, u32[]{:S(2)}, u32[]{:S(2)}) %collective-permute-start.39) | collective-permute-done | bytes 1572896 | tf_op jit(solution)/shard_map/cond/branch_1_fun/ppermute | solution.py:635
  91.3 63.7 %conditional.19 = (bf16[2,512,1024]{2,1,0:T(8,128)(2,1)}, bf16[2,512,1024]{2,1,0:T(8,128)(2,1)}, bf16[2,512,1024]{2,1,0:T(8,128)(2,1)}, bf16[2048,128]{1,0:T(8,1...) conditional(s32[]{:T(128)} %convert_element_type.364, ...), branch_computations={%region_4.5_spmd, %region_5.10_spmd} | conditional | flops 2200013 | bytes 34943488 | solution.py:581
  91.4 9.2 %conditional = (bf16[2,512,1024]{2,1,0:T(8,128)(2,1)}) conditional(s32[]{:T(128)} %convert_element_type.268, () %tuple.89, (s32[]{:T(128)}, bf16[2,2,64,1024]{3,2,1,0:T(8,128)(2,1)}, bf16[2,2,64,1024]{3,2,1,0:T(8,128)(2,1)}, bf16[2,2,64,1024]{3,2,1,0:T(8,128)(2,1)}, bf16[2,2,64,1024]{3,2,1,0:T(8,128)(2,1)}, /*index=5*/s32[1]{0:T(128)}) %tuple.90), branch_computations={%region_6.6_spmd, %region_7.7_spmd} | conditional | flops 1573868 | bytes 14685222 | solution.py:581
  102.6 11.8 %conditional.1 = (bf16[32,64,128]{2,1,0:T(8,128)(2,1)}, f32[1,2048]{1,0:T(1,128)}, f32[1,768]{1,0:T(1,128)}, f32[1,1024]{1,0:T(1,128)}, f32[1,2048]{1,0:T(1,128)...) conditional(s32[]{:T(128)} %convert_element_type.269, () %tuple.92, ...), branch_computations={%region_8.8_spmd, %region_9.9_spmd} | conditional | flops 626143 | bytes 1907839 | solution.py:581
  119.2 34.3 %collective-permute-done.18 = bf16[2,512,1024]{2,1,0:T(8,128)(2,1)} collective-permute-done((bf16[2,512,1024]{2,1,0:T(8,128)(2,1)}, bf16[2,512,1024]{2,1,0:T(8,128)(2,1)}, u32[]{:S(2)}, u32[]{:S(2)}) %collective-permute-start.18) | collective-permute-done | bytes 2097184 | tf_op jit(solution)/shard_map/cond/branch_1_fun/ppermute | solution.py:635
  155.2 74.9 %conditional.20 = (bf16[1,512,1024]{2,1,0:T(8,128)(2,1)S(1)}, bf16[1,512,1024]{2,1,0:T(8,128)(2,1)S(1)}, bf16[512,2048]{1,0:T(8,128)(2,1)}, bf16[512,2048]{1,0:T...) conditional(s32[]{:T(128)} %convert_element_type.365, ...), branch_computations={%region_10.11_spmd, %region_11.16_spmd} | conditional | flops 14881390 | bytes 100704168 | solution.py:581
  163.8 8.3 %conditional.2 = (bf16[3,128,2048]{2,1,0:T(8,128)(2,1)}, bf16[3,128,2048]{2,1,0:T(8,128)(2,1)}, bf16[3,128,2048]{2,1,0:T(8,128)(2,1)}) conditional(s32[]{:T(128)} %convert_element_type.270, () %tuple.108, (bf16[3,128,2048]{2,1,0:T(8,128)(2,1)}, bf16[3,128,2048]{2,1,0:T(8,128)(2,1)}, bf16[3,128,2048]{2,1,0:T(8,128)(2,1)}) %tuple.109), branch_computations={%region_12.12_spmd, %region_13.13_spmd} | conditional | bytes 18874512 | solution.py:581
  172.0 12.7 %collective-permute-done.5.refs_3_ = bf16[1,512,1024]{2,1,0:T(8,128)(2,1)S(1)} collective-permute-done((bf16[1,512,1024]{2,1,0:T(8,128)(2,1)S(1)}, bf16[1,512,1024]{2,1,0:T(8,128)(2,1)S(1)}, u32[]{:S(2)}, u32[]{:S(2)}) %collective-permute-start.5) | collective-permute-done | bytes 1048608 | tf_op jit(solution)/shard_map/cond/branch_1_fun/ppermute | solution.py:635
  201.8 21.2 %conditional.3 = (bf16[512,1024]{1,0:T(8,128)(2,1)}, f32[512,1024]{1,0:T(8,128)}, bf16[128,2048]{1,0:T(8,128)(2,1)}, bf16[128,2048]{1,0:T(8,128)(2,1)}, bf16[128...) conditional(s32[]{:T(128)} %convert_element_type.271, () %tuple.114, (bf16[512,1024]{1,0:T(8,128)(2,1)S(1)}, ...), branch_computations={%region_14.14_spmd, %region_15.15_spmd} | conditional | flops 6442449 | bytes 16807332 | solution.py:581
  242.0 66.7 %conditional.21 = (bf16[2048,1024]{1,0:T(8,128)(2,1)}, bf16[3,256,256]{2,1,0:T(8,128)(2,1)S(1)}, bf16[3,256,256]{2,1,0:T(8,128)(2,1)}, bf16[3,256,256]{2,1,0:T(8...) conditional(s32[]{:T(128)} %convert_element_type.366, ...), branch_computations={%region_16.17_spmd, %region_17.18_spmd} | conditional | flops 10324276 | bytes 51945200 | solution.py:581
  308.8 8.4 %mixing.1 = (f32[128,2048]{1,0:T(8,128)}, f32[128,2048]{1,0:T(8,128)}, bf16[128,2048]{1,0:T(8,128)(2,1)}, bf16[128,2048]{1,0:T(8,128)(2,1)}, bf16[128,2048]{1,0:...) custom-call(s32[1]{0:T(128)} %bitcast.69.chip, ...), custom_call_target="tpu_custom_call" | custom-call | flops 200000 | bytes 10000 | tf_op jit(solution)/shard_map/mixing/pallas_call | solution.py:998
  321.7 45.2 %conditional.22 = (bf16[3,256,256]{2,1,0:T(8,128)(2,1)}, f32[1,768]{1,0:T(1,128)S(1)}, f32[3,128,2048]{2,1,0:T(8,128)}, bf16[3,128,2048]{2,1,0:T(8,128)(2,1)}, b...) conditional(s32[]{:T(128)} %convert_element_type.367, ...), branch_computations={%region_18.19_spmd, %region_19.20_spmd} | conditional | flops 63441720 | bytes 52123440 | solution.py:581
  327.4 7.9 %attend_back.4 = (bf16[3,256,256]{2,1,0:T(8,128)(2,1)}, f32[1,768]{1,0:T(1,128)S(1)}, f32[3,128,2048]{2,1,0:T(8,128)}, bf16[3,128,2048]{2,1,0:T(8,128)(2,1)}) custom-call(bf16[128,2048]{1,0:T(8,128)(2,1)} %get-tuple-element.706.own, bf16[128,2048]{1,0:T(8,128)(2,1)} %collective-permute-done.47.other, bf16[2048,1024]{1,0:T(8,128)(2,1)} %get-tuple-element.693.weight, ...), custom_call_target="tpu_custom_call" | custom-call | flops 1073741 | bytes 8000 | tf_op jit(solution)/shard_map/cond/branch_1_fun/attend_back/pallas_call | solution.py:1074
  366.9 43.5 %conditional.23 = (bf16[512,2048]{1,0:T(8,128)(2,1)}, bf16[512,2048]{1,0:T(8,128)(2,1)}, bf16[512,1024]{1,0:T(8,128)(2,1)}, bf16[512,1024]{1,0:T(8,128)(2,1)}, f...) conditional(s32[]{:T(128)} %convert_element_type.368, ...), branch_computations={%region_20.21_spmd, %region_21.24_spmd} | conditional | flops 15931991 | bytes 55653644 | solution.py:581
  371.1 9.7 %hidden_back.2 = (bf16[512,1024]{1,0:T(8,128)(2,1)}, f32[1,1024]{1,0:T(1,128)}, bf16[512,2048]{1,0:T(8,128)(2,1)}) custom-call(bf16[512,2048]{1,0:T(8,128)(2,1)} %bitcast.46.grad, f32[512,1024]{1,0:T(8,128)} %get-tuple-element.748.slope, bf16[2,512,1024]{2,1,0:T(8,128)(2,1)} %get-tuple-element.749.refs_0_.refs_4_, ...), custom_call_target="tpu_custom_call" | custom-call | flops 4294967 | bytes 20000 | tf_op jit(solution)/shard_map/cond/branch_1_fun/hidden_back/pallas_call | solution.py:1129
  391.8 9.7 %hidden_back.3 = (bf16[512,1024]{1,0:T(8,128)(2,1)}, f32[1,1024]{1,0:T(1,128)}, bf16[512,2048]{1,0:T(8,128)(2,1)}) custom-call(bf16[512,2048]{1,0:T(8,128)(2,1)} %bitcast.47.grad, f32[512,1024]{1,0:T(8,128)} %get-tuple-element.763.slope, bf16[2,512,1024]{2,1,0:T(8,128)(2,1)} %get-tuple-element.749.refs_0_.refs_4_, ...), custom_call_target="tpu_custom_call" | custom-call | flops 4294967 | bytes 20000 | tf_op jit(solution)/shard_map/cond/branch_1_fun/hidden_back/pallas_call | solution.py:1129
  411.0 54.7 %conditional.24 = (bf16[128,2048]{1,0:T(8,128)(2,1)}, bf16[128,2048]{1,0:T(8,128)(2,1)}, bf16[128,2048]{1,0:T(8,128)(2,1)}, bf16[4,8,64,1024]{3,2,1,0:T(8,128)(2...) conditional(s32[]{:T(128)} %convert_element_type.369, ...), branch_computations={%region_24.25_spmd, %region_25.28_spmd} | conditional | flops 17028872 | bytes 40965384 | solution.py:581
  415.4 50.3 %conditional.5 = (bf16[4,8,64,1024]{3,2,1,0:T(8,128)(2,1)}, f32[1,768]{1,0:T(1,128)}, f32[3,128,2048]{2,1,0:T(8,128)}, bf16[3,128,2048]{2,1,0:T(8,128)(2,1)}, f3...) conditional(s32[]{:T(128)} %convert_element_type.305, ...), branch_computations={%region_26.26_spmd, %region_27.27_spmd} | conditional | flops 17028872 | bytes 34673428 | solution.py:581
  415.4 9.5 %outer.2 = (bf16[512,1024]{1,0:T(8,128)(2,1)}, bf16[512,1024]{1,0:T(8,128)(2,1)}, bf16[512,1024]{1,0:T(8,128)(2,1)}, bf16[512,1024]{1,0:T(8,128)(2,1)}) custom-call(bf16[512,2048]{1,0:T(8,128)(2,1)} %get-tuple-element.798.left_own, bf16[512,2048]{1,0:T(8,128)(2,1)} %get-tuple-element.799.left_other, bf16[512,1024]{1,0:T(8,128)(2,1)} %get-tuple-element.800.right_own, ...), custom_call_target="tpu_custom_call" | custom-call | flops 4294967 | bytes 20000 | tf_op jit(solution)/shard_map/cond/branch_1_fun/cond/branch_1_fun/outer/pallas_call | solution.py:1148
  429.5 7.9 %attend_back.6 = (bf16[3,256,256]{2,1,0:T(8,128)(2,1)}, f32[1,768]{1,0:T(1,128)}, f32[3,128,2048]{2,1,0:T(8,128)}, bf16[3,128,2048]{2,1,0:T(8,128)(2,1)}) custom-call(bf16[128,2048]{1,0:T(8,128)(2,1)S(1)} %get-tuple-element.803.own.refs_10_, bf16[128,2048]{1,0:T(8,128)(2,1)} %get-tuple-element.804.other.refs_11_, ...), custom_call_target="tpu_custom_call" | custom-call | flops 1073741 | bytes 8000 | tf_op jit(solution)/shard_map/cond/branch_1_fun/cond/branch_1_fun/attend_back/pallas_call | solution.py:1074
  452.5 12.3 %heads_grad.1 = bf16[4,8,64,1024]{3,2,1,0:T(8,128)(2,1)} custom-call(bf16[3,128,2048]{2,1,0:T(8,128)(2,1)} %get-tuple-element.781.refs_0_, bf16[3,128,2048]{2,1,0:T(8,128)(2,1)} %get-tuple-element.782.refs_1_, bf16[3,128,2048]{2,1,0:T(8,128)(2,1)} %get-tuple-element.783.refs_2_, bf16[3,128,2048]{2,1,0:T(8,128)(2,1)} %get-tuple-element.784.refs_3_, ...), custom_call_target="tpu_custom_call" | custom-call | flops 4294967 | bytes 30000 | tf_op jit(solution)/shard_map/cond/branch_1_fun/cond/branch_1_fun/heads_grad/pallas_call | solution.py:1215
  473.0 73.1 %conditional.26 = (bf16[512,1024]{1,0:T(8,128)(2,1)}, bf16[512,1024]{1,0:T(8,128)(2,1)}, bf16[512,1024]{1,0:T(8,128)(2,1)}, bf16[3,128,2048]{2,1,0:T(8,128)(2,1)...) conditional(s32[]{:T(128)} %convert_element_type.371, () %tuple.317, ...), branch_computations={%region_30.31_spmd, %region_31.34_spmd} | conditional | flops 10595597 | bytes 75619880 | solution.py:581
  473.8 9.5 %outer.3 = (bf16[512,1024]{1,0:T(8,128)(2,1)}, bf16[512,1024]{1,0:T(8,128)(2,1)}, bf16[512,1024]{1,0:T(8,128)(2,1)}, bf16[512,1024]{1,0:T(8,128)(2,1)}) custom-call(bf16[512,2048]{1,0:T(8,128)(2,1)} %get-tuple-element.923.left_own, bf16[512,2048]{1,0:T(8,128)(2,1)} %get-tuple-element.924.left_other, bf16[512,1024]{1,0:T(8,128)(2,1)} %get-tuple-element.925.right_own, ...), custom_call_target="tpu_custom_call" | custom-call | flops 4294967 | bytes 20000 | tf_op jit(solution)/shard_map/cond/branch_1_fun/outer/pallas_call | solution.py:1148
  500.3 21.0 %conditional.6 = (bf16[32,16,768]{2,1,0:T(8,128)(2,1)}) conditional(s32[]{:T(128)} %convert_element_type.312, () %tuple.195, (f32[1,2048]{1,0:T(1,128)S(1)}, f32[1,768]{1,0:T(1,128)S(1)}, f32[1,768]{1,0:T(1,128)}, f32[1,768]{1,0:T(1,128)}, f32[1,768]{1,0:T(1,128)S(1)}, /*index=5*/s32[]{:T(128)}, s32[]{:T(128)}, f32[1,2048]{1,0:T(1,128)S(1)}, ...), branch_computations={%region_32.32_spmd, %region_33.33_spmd} | conditional | flops 7173 | bytes 5324702 | solution.py:581
  521.3 20.7 %collective-permute-done.43 = bf16[256,1024]{1,0:T(8,128)(2,1)} collective-permute-done((bf16[256,1024]{1,0:T(8,128)(2,1)}, bf16[256,1024]{1,0:T(8,128)(2,1)}, u32[]{:S(2)}, u32[]{:S(2)}) %collective-permute-start.43) | collective-permute-done | bytes 524320 | tf_op jit(solution)/shard_map/cond/branch_1_fun/ppermute | solution.py:635
  551.7 36.9 %conditional.27 = (f32[9,128,2048]{2,1,0:T(8,128)}, f32[128,36]{1,0:T(8,128)}, f32[4,2048]{1,0:T(4,128)S(1)}, bf16[8,64,1024]{2,1,0:T(8,128)(2,1)}, f32[128,36]{0,1:T(8,128)S(1)}) conditional(s32[]{:T(128)} %convert_element_type.372, () %tuple.321, (bf16[9,128,2048]{2,1,0:T(8,128)(2,1)}, bf16[4,128,2048]{2,1,0:T(8,128)(2,1)S(1)}, s32[1]{0:T(128)}, ...), branch_computations={%region_34.35_spmd, %region_35.36_spmd} | conditional | flops 3345728 | bytes 12640920 | solution.py:581
  556.4 18.6 %close.1 = (f32[9,128,2048]{2,1,0:T(8,128)}, f32[128,36]{1,0:T(8,128)}, f32[4,2048]{1,0:T(4,128)S(1)}) custom-call(s32[1]{0:T(128)} %get-tuple-element.962.chip, bf16[9,128,2048]{2,1,0:T(8,128)(2,1)} %get-tuple-element.965.hist, bf16[4,128,2048]{2,1,0:T(8,128)(2,1)S(1)} %get-tuple-element.966.cot, f32[128,128]{1,0:T(8,128)} %get-tuple-element.967.coef, ...), custom_call_target="tpu_custom_call" | custom-call | flops 200000 | bytes 20000 | tf_op jit(solution)/shard_map/cond/branch_1_fun/close/pallas_call | solution.py:1311
  575.9 8.8 %collective-permute-done.12 = bf16[512,1024]{1,0:T(8,128)(2,1)} collective-permute-done((bf16[512,1024]{1,0:T(8,128)(2,1)}, bf16[512,1024]{1,0:T(8,128)(2,1)}, u32[]{:S(2)}, u32[]{:S(2)}) %collective-permute-start.12) | collective-permute-done | bytes 1048608 | tf_op jit(solution)/shard_map/cond/branch_1_fun/ppermute | solution.py:635
  589.0 11.7 %all_to_all.48 = f32[32,1,512]{2,1,0:T(1,128)S(1)} all-to-all(f32[32,1,512]{2,1,0:T(1,128)S(1)} %copy.226), channel_id=1, replica_groups=mesh['chip'=4,'core'=2,'rep'=4] {'chip','core','rep'}, dimensions={0} | all-to-all | bytes 131072 | tf_op jit(solution)/shard_map/all_to_all | solution.py:1364
  613.2 24.1 %conditional.28 = (f32[64,6144]{1,0:T(8,128)}, f32[64,2048]{1,0:T(8,128)}) conditional(s32[]{:T(128)} %convert_element_type.377, () %tuple.332, (s32[]{:T(128)}, bf16[8,64,1024]{2,1,0:T(8,128)(2,1)}, s32[]{:T(128)}) %tuple.481), branch_computations={%region_39.40_spmd, %region_40.41_spmd} | conditional | flops 6291482 | bytes 28312084 | solution.py:581
  (465 shorter events, 417.1 us)
Async XLA Ops:
  30.6 56.3 %all-to-all-start.2 = ((bf16[8,64,1024]{2,1,0:T(8,128)(2,1)}), bf16[8,64,1024]{2,1,0:T(8,128)(2,1)S(1)}, u32[]{:S(2)}, u32[]{:S(2)}) async-start(bf16[8,64,1024]{2,1,0:T(8,128)(2,1)} %pack_heads.1), calls=%async_computation.2 | async-start | bytes 2097152 | tf_op jit(solution)/shard_map/all_to_all | solution.py:722
  34.7 201.7 %all-gather.3.cloned.1.call-start = ((), (), s32[]{:S(2)}) async-start(), calls=%async_computation.9 | async-start | bytes 5242880 | tf_op jit(solution)/shard_map/all_gather | solution.py:845
  34.7 52.2 %collective-permute-start.53 = (bf16[2,2,64,1024]{3,2,1,0:T(8,128)(2,1)}, bf16[2,2,64,1024]{3,2,1,0:T(8,128)(2,1)}, u32[]{:S(2)}, u32[]{:S(2)}) collective-permute-start(bf16[2,2,64,1024]{3,2,1,0:T(8,128)(2,1)} %get-tuple-element.1233), channel_id=1, source_target_pairs={{0,1},{1,0},{2,3},{3,2},{4,5},{5,4},{6,7},{7,6},{8,9},{9,8},{10,11... | collective-permute-start | bytes 1572872 | tf_op jit(solution)/shard_map/ppermute | solution.py:638
  36.2 50.6 %collective-permute-start.54 = (bf16[2,2,64,1024]{3,2,1,0:T(8,128)(2,1)}, bf16[2,2,64,1024]{3,2,1,0:T(8,128)(2,1)}, u32[]{:S(2)}, u32[]{:S(2)}) collective-permute-start(bf16[2,2,64,1024]{3,2,1,0:T(8,128)(2,1)} %get-tuple-element.1234), channel_id=1, source_target_pairs={{0,2},{1,3},{2,0},{3,1},{4,6},{5,7},{6,4},{7,5},{8,10},{9,11},{10,... | collective-permute-start | bytes 1572872 | tf_op jit(solution)/shard_map/ppermute | solution.py:638
  38.7 48.2 %collective-permute-start.55 = (bf16[2,2,64,1024]{3,2,1,0:T(8,128)(2,1)}, bf16[2,2,64,1024]{3,2,1,0:T(8,128)(2,1)}, u32[]{:S(2)}, u32[]{:S(2)}) collective-permute-start(bf16[2,2,64,1024]{3,2,1,0:T(8,128)(2,1)} %get-tuple-element.1235), channel_id=1, source_target_pairs={{0,3},{1,2},{2,1},{3,0},{4,7},{5,6},{6,5},{7,4},{8,11},{9,10},{10,... | collective-permute-start | bytes 1572872 | tf_op jit(solution)/shard_map/ppermute | solution.py:638
  49.2 36.3 %collective-permute-start.39 = (bf16[3,128,2048]{2,1,0:T(8,128)(2,1)}, bf16[3,128,2048]{2,1,0:T(8,128)(2,1)}, u32[]{:S(2)}, u32[]{:S(2)}) collective-permute-start(bf16[3,128,2048]{2,1,0:T(8,128)(2,1)} %get-tuple-element.2562), channel_id=1, source_target_pairs={{0,8},{8,0},{16,24},{24,16},{1,9},{9,1},{17,25},{25,17},{2,10},{10... | collective-permute-start | bytes 4718600 | tf_op jit(solution)/shard_map/cond/branch_1_fun/ppermute | solution.py:635
  51.2 35.7 %collective-permute-start.40 = (bf16[3,128,2048]{2,1,0:T(8,128)(2,1)}, bf16[3,128,2048]{2,1,0:T(8,128)(2,1)}, u32[]{:S(2)}, u32[]{:S(2)}) collective-permute-start(bf16[3,128,2048]{2,1,0:T(8,128)(2,1)} %get-tuple-element.2562), channel_id=1, source_target_pairs={{0,16},{8,24},{16,0},{24,8},{1,17},{9,25},{17,1},{25,9},{2,18},{10... | collective-permute-start | bytes 4718600 | tf_op jit(solution)/shard_map/cond/branch_1_fun/ppermute | solution.py:635
  86.9 68.2 %collective-permute-start.56 = (bf16[128,2048]{1,0:T(8,128)(2,1)}, bf16[128,2048]{1,0:T(8,128)(2,1)S(1)}, u32[]{:S(2)}, u32[]{:S(2)}) collective-permute-start(bf16[128,2048]{1,0:T(8,128)(2,1)} %get-tuple-element.1237), channel_id=1, source_target_pairs={{0,1},{1,0},{2,3},{3,2},{4,5},{5,4},{6,7},{7,6},{8,9},{9,8},{10,11... | collective-permute-start | bytes 1572872 | tf_op jit(solution)/shard_map/ppermute | solution.py:638
  87.5 67.6 %collective-permute-start.57 = (bf16[128,2048]{1,0:T(8,128)(2,1)}, bf16[128,2048]{1,0:T(8,128)(2,1)S(1)}, u32[]{:S(2)}, u32[]{:S(2)}) collective-permute-start(bf16[128,2048]{1,0:T(8,128)(2,1)} %get-tuple-element.1237), channel_id=1, source_target_pairs={{0,2},{1,3},{2,0},{3,1},{4,6},{5,7},{6,4},{7,5},{8,10},{9,11},{10,... | collective-permute-start | bytes 1572872 | tf_op jit(solution)/shard_map/ppermute | solution.py:638
  90.9 64.2 %collective-permute-start.58 = (bf16[128,2048]{1,0:T(8,128)(2,1)}, bf16[128,2048]{1,0:T(8,128)(2,1)S(1)}, u32[]{:S(2)}, u32[]{:S(2)}) collective-permute-start(bf16[128,2048]{1,0:T(8,128)(2,1)} %get-tuple-element.1237), channel_id=1, source_target_pairs={{0,3},{1,2},{2,1},{3,0},{4,7},{5,6},{6,5},{7,4},{8,11},{9,10},{10,... | collective-permute-start | bytes 1572872 | tf_op jit(solution)/shard_map/ppermute | solution.py:638
  100.6 52.9 %collective-permute-start.18 = (bf16[2,512,1024]{2,1,0:T(8,128)(2,1)}, bf16[2,512,1024]{2,1,0:T(8,128)(2,1)}, u32[]{:S(2)}, u32[]{:S(2)}) collective-permute-start(bf16[2,512,1024]{2,1,0:T(8,128)(2,1)} %get-tuple-element.2812), channel_id=1, source_target_pairs={{0,8},{8,0},{16,24},{24,16},{1,9},{9,1},{17,25},{25,17},{2,10},{10... | collective-permute-start | bytes 6291464 | tf_op jit(solution)/shard_map/cond/branch_1_fun/ppermute | solution.py:635
  100.9 52.5 %collective-permute-start.19 = (bf16[2,512,1024]{2,1,0:T(8,128)(2,1)}, bf16[2,512,1024]{2,1,0:T(8,128)(2,1)}, u32[]{:S(2)}, u32[]{:S(2)}) collective-permute-start(bf16[2,512,1024]{2,1,0:T(8,128)(2,1)} %get-tuple-element.2812), channel_id=1, source_target_pairs={{0,16},{8,24},{16,0},{24,8},{1,17},{9,25},{17,1},{25,9},{2,18},{10... | collective-permute-start | bytes 6291464 | tf_op jit(solution)/shard_map/cond/branch_1_fun/ppermute | solution.py:635
  114.4 40.7 %all-to-all-start = ((bf16[32,64,128]{2,1,0:T(8,128)(2,1)}), bf16[32,64,128]{2,1,0:T(8,128)(2,1)}, u32[]{:S(2)}, u32[]{:S(2)}) async-start(bf16[32,64,128]{2,1,0:T(8,128)(2,1)} %get-tuple-element.546), calls=%async_computation | async-start | bytes 1048576 | tf_op jit(solution)/shard_map/cond/branch_1_fun/all_to_all | solution.py:837
  155.1 458.1 %reduce-scatter.2.cloned.1.call-start = ((), (), s32[]{:S(2)}) async-start(), calls=%async_computation.8 | async-start | bytes 5242880 | tf_op jit(solution)/shard_map/reduce_scatter | solution.py:1251
  190.4 32.6 %collective-permute-start.8 = (bf16[3,64,2048]{2,1,0:T(8,128)(2,1)}, bf16[3,64,2048]{2,1,0:T(8,128)(2,1)}, u32[]{:S(2)}, u32[]{:S(2)}) collective-permute-start(bf16[3,64,2048]{2,1,0:T(8,128)(2,1)} %slice.208), channel_id=1, source_target_pairs={{0,16},{8,24},{16,0},{24,8},{1,17},{9,25},{17,1},{25,9},{2,18},{10... | collective-permute-start | bytes 2359304 | tf_op jit(solution)/shard_map/cond/branch_1_fun/ppermute | solution.py:635
  236.4 72.4 %collective-permute-start.59 = (bf16[128,2048]{1,0:T(8,128)(2,1)}, bf16[128,2048]{1,0:T(8,128)(2,1)}, u32[]{:S(2)}, u32[]{:S(2)}) collective-permute-start(bf16[128,2048]{1,0:T(8,128)(2,1)} %get-tuple-element.1279), channel_id=1, source_target_pairs={{0,1},{1,0},{2,3},{3,2},{4,5},{5,4},{6,7},{7,6},{8,9},{9,8},{10,11... | collective-permute-start | bytes 1572872 | tf_op jit(solution)/shard_map/ppermute | solution.py:638
  236.4 72.4 %collective-permute-start.60 = (bf16[128,2048]{1,0:T(8,128)(2,1)}, bf16[128,2048]{1,0:T(8,128)(2,1)}, u32[]{:S(2)}, u32[]{:S(2)}) collective-permute-start(bf16[128,2048]{1,0:T(8,128)(2,1)} %get-tuple-element.1280), channel_id=1, source_target_pairs={{0,2},{1,3},{2,0},{3,1},{4,6},{5,7},{6,4},{7,5},{8,10},{9,11},{10,... | collective-permute-start | bytes 1572872 | tf_op jit(solution)/shard_map/ppermute | solution.py:638
  237.5 71.3 %collective-permute-start.61 = (bf16[128,2048]{1,0:T(8,128)(2,1)}, bf16[128,2048]{1,0:T(8,128)(2,1)}, u32[]{:S(2)}, u32[]{:S(2)}) collective-permute-start(bf16[128,2048]{1,0:T(8,128)(2,1)} %get-tuple-element.1281), channel_id=1, source_target_pairs={{0,3},{1,2},{2,1},{3,0},{4,7},{5,6},{6,5},{7,4},{8,11},{9,10},{10,... | collective-permute-start | bytes 1572872 | tf_op jit(solution)/shard_map/ppermute | solution.py:638
  317.2 49.7 %collective-permute-start.62 = (bf16[128,2048]{1,0:T(8,128)(2,1)}, bf16[128,2048]{1,0:T(8,128)(2,1)}, u32[]{:S(2)}, u32[]{:S(2)}) collective-permute-start(bf16[128,2048]{1,0:T(8,128)(2,1)} %get-tuple-element.1315), channel_id=1, source_target_pairs={{0,1},{1,0},{2,3},{3,2},{4,5},{5,4},{6,7},{7,6},{8,9},{9,8},{10,11... | collective-permute-start | bytes 1572872 | tf_op jit(solution)/shard_map/ppermute | solution.py:638
  317.3 49.6 %collective-permute-start.63 = (bf16[128,2048]{1,0:T(8,128)(2,1)}, bf16[128,2048]{1,0:T(8,128)(2,1)}, u32[]{:S(2)}, u32[]{:S(2)}) collective-permute-start(bf16[128,2048]{1,0:T(8,128)(2,1)} %get-tuple-element.1315), channel_id=1, source_target_pairs={{0,2},{1,3},{2,0},{3,1},{4,6},{5,7},{6,4},{7,5},{8,10},{9,11},{10,... | collective-permute-start | bytes 1572872 | tf_op jit(solution)/shard_map/ppermute | solution.py:638
  318.6 48.3 %collective-permute-start.64 = (bf16[128,2048]{1,0:T(8,128)(2,1)}, bf16[128,2048]{1,0:T(8,128)(2,1)}, u32[]{:S(2)}, u32[]{:S(2)}) collective-permute-start(bf16[128,2048]{1,0:T(8,128)(2,1)} %get-tuple-element.1315), channel_id=1, source_target_pairs={{0,3},{1,2},{2,1},{3,0},{4,7},{5,6},{6,5},{7,4},{8,11},{9,10},{10,... | collective-permute-start | bytes 1572872 | tf_op jit(solution)/shard_map/ppermute | solution.py:638
  411.0 54.7 %collective-permute-start.36 = (bf16[128,2048]{1,0:T(8,128)(2,1)}, bf16[128,2048]{1,0:T(8,128)(2,1)}, u32[]{:S(2)}, u32[]{:S(2)}) collective-permute-start(bf16[128,2048]{1,0:T(8,128)(2,1)} %get-tuple-element.854), channel_id=1, source_target_pairs={{0,1},{1,0},{2,3},{3,2},{4,5},{5,4},{6,7},{7,6},{8,9},{9,8},{10,11... | collective-permute-start | bytes 1572872 | tf_op jit(solution)/shard_map/cond/branch_1_fun/ppermute | solution.py:638
  411.0 54.7 %collective-permute-start.37 = (bf16[128,2048]{1,0:T(8,128)(2,1)}, bf16[128,2048]{1,0:T(8,128)(2,1)}, u32[]{:S(2)}, u32[]{:S(2)}) collective-permute-start(bf16[128,2048]{1,0:T(8,128)(2,1)} %get-tuple-element.855), channel_id=1, source_target_pairs={{0,2},{1,3},{2,0},{3,1},{4,6},{5,7},{6,4},{7,5},{8,10},{9,11},{10,... | collective-permute-start | bytes 1572872 | tf_op jit(solution)/shard_map/cond/branch_1_fun/ppermute | solution.py:638
  412.4 53.4 %collective-permute-start.38 = (bf16[128,2048]{1,0:T(8,128)(2,1)}, bf16[128,2048]{1,0:T(8,128)(2,1)}, u32[]{:S(2)}, u32[]{:S(2)}) collective-permute-start(bf16[128,2048]{1,0:T(8,128)(2,1)} %get-tuple-element.856), channel_id=1, source_target_pairs={{0,3},{1,2},{2,1},{3,0},{4,7},{5,6},{6,5},{7,4},{8,11},{9,10},{10,... | collective-permute-start | bytes 1572872 | tf_op jit(solution)/shard_map/cond/branch_1_fun/ppermute | solution.py:638
  469.3 76.8 %all-to-all-start.3 = ((bf16[8,64,1024]{2,1,0:T(8,128)(2,1)}), bf16[8,64,1024]{2,1,0:T(8,128)(2,1)S(1)}, u32[]{:S(2)}, u32[]{:S(2)}) async-start(bf16[8,64,1024]{2,1,0:T(8,128)(2,1)} %get-tuple-element.2814), calls=%async_computation.3 | async-start | bytes 2097152 | tf_op jit(solution)/shard_map/all_to_all | solution.py:1256
  493.4 52.7 %collective-permute-start.46 = (bf16[3,128,2048]{2,1,0:T(8,128)(2,1)}, bf16[3,128,2048]{2,1,0:T(8,128)(2,1)}, u32[]{:S(2)}, u32[]{:S(2)}) collective-permute-start(bf16[3,128,2048]{2,1,0:T(8,128)(2,1)} %merge.4), channel_id=1, source_target_pairs={{0,16},{8,24},{16,0},{24,8},{1,17},{9,25},{17,1},{25,9},{2,18},{10... | collective-permute-start | bytes 4718600 | tf_op jit(solution)/shard_map/cond/branch_1_fun/ppermute | solution.py:635
  494.0 52.1 %collective-permute-start.45 = (bf16[3,128,2048]{2,1,0:T(8,128)(2,1)}, bf16[3,128,2048]{2,1,0:T(8,128)(2,1)}, u32[]{:S(2)}, u32[]{:S(2)}) collective-permute-start(bf16[3,128,2048]{2,1,0:T(8,128)(2,1)} %merge.5), channel_id=1, source_target_pairs={{0,8},{8,0},{16,24},{24,16},{1,9},{9,1},{17,25},{25,17},{2,10},{10... | collective-permute-start | bytes 4718600 | tf_op jit(solution)/shard_map/cond/branch_1_fun/ppermute | solution.py:635
  495.7 46.3 %collective-permute-start.43 = (bf16[256,1024]{1,0:T(8,128)(2,1)}, bf16[256,1024]{1,0:T(8,128)(2,1)}, u32[]{:S(2)}, u32[]{:S(2)}) collective-permute-start(bf16[256,1024]{1,0:T(8,128)(2,1)} %get-tuple-element.2447), channel_id=1, source_target_pairs={{0,8},{8,0},{16,24},{24,16},{1,9},{9,1},{17,25},{25,17},{2,10},{10... | collective-permute-start | bytes 1572872 | tf_op jit(solution)/shard_map/cond/branch_1_fun/ppermute | solution.py:635
  497.1 44.9 %collective-permute-start.44 = (bf16[256,1024]{1,0:T(8,128)(2,1)}, bf16[256,1024]{1,0:T(8,128)(2,1)}, u32[]{:S(2)}, u32[]{:S(2)}) collective-permute-start(bf16[256,1024]{1,0:T(8,128)(2,1)} %get-tuple-element.2446), channel_id=1, source_target_pairs={{0,16},{8,24},{16,0},{24,8},{1,17},{9,25},{17,1},{25,9},{2,18},{10... | collective-permute-start | bytes 1572872 | tf_op jit(solution)/shard_map/cond/branch_1_fun/ppermute | solution.py:635
  546.1 42.8 %all-to-all-start.4 = ((bf16[32,16,768]{2,1,0:T(8,128)(2,1)}), bf16[32,16,768]{2,1,0:T(8,128)(2,1)}, u32[]{:S(2)}, u32[]{:S(2)}) async-start(bf16[32,16,768]{2,1,0:T(8,128)(2,1)} %get-tuple-element.1396), calls=%async_computation.4 | async-start | bytes 1572864 | tf_op jit(solution)/shard_map/all_to_all | solution.py:1302
  551.8 32.9 %collective-permute-start.12 = (bf16[512,1024]{1,0:T(8,128)(2,1)}, bf16[512,1024]{1,0:T(8,128)(2,1)}, u32[]{:S(2)}, u32[]{:S(2)}) collective-permute-start(bf16[512,1024]{1,0:T(8,128)(2,1)} %get-tuple-element.986), channel_id=1, source_target_pairs={{0,8},{8,0},{16,24},{24,16},{1,9},{9,1},{17,25},{25,17},{2,10},{10... | collective-permute-start | bytes 3145736 | tf_op jit(solution)/shard_map/cond/branch_1_fun/ppermute | solution.py:635
  600.7 36.6 %all-to-all-start.6 = ((bf16[8,64,1024]{2,1,0:T(8,128)(2,1)}), bf16[8,64,1024]{2,1,0:T(8,128)(2,1)}, u32[]{:S(2)}, u32[]{:S(2)}) async-start(bf16[8,64,1024]{2,1,0:T(8,128)(2,1)} %get-tuple-element.1409), calls=%async_computation.7 | async-start | bytes 2097152 | tf_op jit(solution)/shard_map/all_to_all | solution.py:1365
  (94 other events, 1255.7 us)
Sparse Core Ops, SparseCore 0:
  155.2 81.0 all-gather.2
  465.9 90.7 reduce-scatter.1

commit v4 on v3

--- a/solution.py
+++ b/solution.py
@@ -226,9 +226,9 @@
     for s in range(count):
         arriving = cot[s].astype(SINGLE)
         place = s * (entries + 1) + entries
-        total = jnp.sum(arriving * entry, -1, keepdims=True) * weight[...]
+        total = jnp.sum(arriving * entry, -1, keepdims=True) * weight[:, :1]
         grad_coef = jnp.where(lane == place, total, grad_coef)
-        grad = grad + (coef[:, place : place + 1] * weight[...]) * arriving
+        grad = grad + (coef[:, place : place + 1] * weight[:, :1]) * arriving
     grad_coef_out[...] = grad_coef
     grad_pre = slope * times_transposed(grad_coef, second[...], EXACT)
     grad_pre_narrow = grad_pre.astype(NARROW)
@@ -327,7 +327,7 @@
         scale = lax.rsqrt(mean(center * center) + NORM_EPSILON)
         unit = center * scale
         if s < 3:
-            arriving = qkv_own[s]
+            arriving = qkv_own[s].astype(SINGLE)
             for rest in qkv_rest:
                 arriving = arriving + rest[s].astype(SINGLE)
         else:
@@ -378,7 +378,7 @@
     size = row.shape[1]
     query = lax.broadcasted_iota(jnp.int32, (size, size), 0)
     key = lax.broadcasted_iota(jnp.int32, (size, size), 1)
-    return (key <= query) & (row == column)
+    return (key <= query) & (row == column[:, :1])
 
 
 def probabilities(query, key, allowed):
@@ -434,7 +434,7 @@
             grad_linear[i, :, head] = values.astype(NARROW)
     for i in range(3):
         result = times_transposed(grad_linear[i], weight[:, i * cols : (i + 1) * cols])
-        out_own[i] = result[:length]
+        out_own[i] = result[:length].astype(NARROW)
         out_other[i] = result[length:].astype(NARROW)
 
 
@@ -456,12 +456,17 @@
             out[k, 0, :, i * cols : (i + 1) * cols] = total[k * rows : (k + 1) * rows]
 
 
+def rows_of_weight(block):
+    group, _, rows, cols = block.shape
+    return block[...].reshape(group * rows, cols)
+
+
 def hidden_kernel(chips, tokens, *refs):
     weights, (bias, act_out, slope_out) = refs[:chips], refs[chips:]
-    part = weights[0].shape[1]
+    part = weights[0].shape[0] * weights[0].shape[2]
     total = bias[...]
     for m in range(chips):
-        total = total + times(tokens[:, m * part : (m + 1) * part], weights[m][0])
+        total = total + times(tokens[:, m * part : (m + 1) * part], rows_of_weight(weights[m]))
     act, slope = gelu_parts(total)
     act_out[...] = act.astype(NARROW)
     slope_out[...] = slope
@@ -478,10 +483,10 @@
 
 def branch_kernel(chips, merged, act, *refs):
     weights, refs = refs[:chips], refs[chips:]
-    part = weights[0].shape[1]
+    part = weights[0].shape[0] * weights[0].shape[2]
     for m in range(chips):
         cols = slice(m * part, (m + 1) * part)
-        result = times_transposed(act[...], weights[m][0])
+        result = times_transposed(act[...], rows_of_weight(weights[m]))
         if merged:
             put_places(refs[1:], refs[1].shape[0], cols, result + refs[0][:, cols].astype(SINGLE))
         else:
@@ -492,10 +497,10 @@
     firsts, seconds, refs = refs[:chips], refs[chips : 2 * chips], refs[2 * chips :]
     came, refs = (refs[0], refs[1:]) if merged else (None, refs)
     grad_low, grad_sum, *outs = refs
-    part = firsts[0].shape[1]
+    part = firsts[0].shape[0] * firsts[0].shape[2]
     total = None
     for m in range(chips):
-        term = times(grad[:, m * part : (m + 1) * part], seconds[m][0])
+        term = times(grad[:, m * part : (m + 1) * part], rows_of_weight(seconds[m]))
         total = term if m == 0 else total + term
     total = total * slope[...]
 
@@ -508,7 +513,7 @@
     grad_low[...] = low
     for m in range(chips):
         cols = slice(m * part, (m + 1) * part)
-        result = times_transposed(low, firsts[m][0])
+        result = times_transposed(low, rows_of_weight(firsts[m]))
         if merged:
             put_places(outs, outs[0].shape[0], cols, result + came[:, cols].astype(SINGLE))
         else:
@@ -528,7 +533,7 @@
 
 
 def merge_kernel(first, count, own, came, *refs):
-    total = own[...] + came[...].astype(SINGLE)
+    total = own[...].astype(SINGLE) + came[...].astype(SINGLE)
     refs[-1][...] = total.astype(NARROW)
     if len(refs) > 1:
 
@@ -537,27 +542,45 @@
             refs[-1][...] = (total + refs[0][...].astype(SINGLE)).astype(NARROW)
 
 
-def pack_hidden_kernel(rep, line, first, second, *outs):
-    cols = outs[0].shape[3]
-    for k in range(rep):
+def pack_hidden_kernel(first, second, out):
+    cols = out.shape[3]
+    for b in range(out.shape[0]):
+        out[b, 0] = first[:, b * cols : (b + 1) * cols].astype(NARROW)
+        out[b, 1] = second[:, b * cols : (b + 1) * cols].astype(NARROW)
+
+
+def join_heads_kernel(chips, chip, core, swapped, *refs):
+    parts, out = refs[:chips], refs[chips]
+    for m in range(chips):
+        place = 2 * (chip[0] ^ m)
+        out[place + core[0]] = parts[m][core[0]]
+        out[place + 1 - core[0]] = swapped[m]
+
+
+def pack_small_kernel(*refs):
+    out = refs[-1]
+    row = 0
+    out[...] = jnp.zeros_like(out)
+    for values in refs[:-1]:
+        for i in range(values.shape[0]):
+            for start in range(0, values.shape[1], LANES):
+                stop = min(start + LANES, values.shape[1])
+                piece = values[i : i + 1, start:stop].astype(NARROW)
+                out[:, row, : stop - start] = jnp.broadcast_to(piece, (out.shape[0], stop - start))
+                row += 1
+
+
+def pack_heads_kernel(chips, chip, qkv, out_weight, *outs):
+    cols = outs[0].shape[2] // 4
+    width = out_weight.shape[1]
+    for m in range(chips):
         for c in range(2):
-            start = pl.multiple_of((c * rep + (line[0] ^ k)) * cols, cols)
-            outs[k][c, 0] = first[:, pl.ds(start, cols)].astype(NARROW)
-            outs[k][c, 1] = second[:, pl.ds(start, cols)].astype(NARROW)
-
-
-def join_hidden_kernel(rep, core, line, swapped, *refs):
-    owns, out = refs[:rep], refs[rep]
-    for k in range(rep):
-        for i in range(2):
-            out[i, core[0], line[0] ^ k] = owns[k][core[0], i]
-            out[i, 1 - core[0], line[0] ^ k] = swapped[k, i]
-
-
-def pack_heads_kernel(query, key, value, out_weight, out):
-    cols = query.shape[1]
-    for i, weight in enumerate((query, key, value, out_weight)):
-        out[0, :, i * cols : (i + 1) * cols] = weight[...].astype(NARROW)
+            start = pl.multiple_of(((chip[0] ^ m) * 2 + c) * cols, cols)
+            for i in range(3):
+                outs[m][c, :, i * cols : (i + 1) * cols] = qkv[
+                    :, pl.ds(i * width + start, cols)
+                ].astype(NARROW)
+            outs[m][c, :, 3 * cols :] = out_weight[:, pl.ds(start, cols)].astype(NARROW)
 
 
 class Order:
@@ -685,54 +708,80 @@
     tall2 = lambda n: spec((n, MIX_ROWS, width), lambda i: (0, i, 0))
     flat2 = lambda n: spec((MIX_ROWS, n), lambda i: (i, 0))
     token_block = lambda n: spec((block, n), lambda i: (i, 0))
-    weight_specs = lambda which: [spec((1, part, hid_cols), lambda *_: (which, 0, 0))] * (
+    weight_block = (group, 1, rows, hid_cols)
+    weight_specs = lambda which: [spec(weight_block, lambda *_: (0, which, 0, 0))] * (
         3 if square else chips
-    ) + [spec((1, part, hid_cols))] * square
+    ) + [spec(weight_block)] * square
     in_vmem = pl.BlockSpec(memory_space=pltpu.VMEM)
 
     small = (norm_gain, norm_bias, b_qkv, b_out, b_fc1, b_fc2, doc_ids)
-    packed = jnp.concatenate([values.reshape(-1).astype(NARROW) for values in small])
-    packed = order.wait(jnp.broadcast_to(packed[None], (devices, packed.shape[0])))
+    flat_small = [values.reshape(-1, values.shape[-1]) for values in small]
+    rows_of = [values.shape[0] * -(-values.shape[1] // LANES) for values in flat_small]
+    packed = pl.pallas_call(
+        pack_small_kernel,
+        in_specs=[in_vmem] * len(small),
+        out_shape=shape((devices, -(-sum(rows_of) // ROWS) * ROWS, LANES), NARROW),
+        compiler_params=params(),
+        cost_estimate=cost(10**6, 10**6),
+        name="pack_small",
+    )(*flat_small)
+    packed = order.wait(packed)
     gathered = lax.all_to_all(packed, AXES, 0, 0, tiled=True)
     hidden_sends = pl.pallas_call(
-        functools.partial(pack_hidden_kernel, rep),
-        in_specs=[scalar_spec()] + [in_vmem] * 2,
-        out_shape=[shape((2, 2, rows, hid_cols), NARROW)] * rep,
+        pack_hidden_kernel,
+        in_specs=[in_vmem] * 2,
+        out_shape=shape((group, 2, rows, hid_cols), NARROW),
         compiler_params=params(),
         cost_estimate=cost(10**6, 6 * 10**6),
         name="pack_hidden",
-    )(line_at, *order.hold(w_fc1, w_fc2))
-    hidden_sends = order.wait(*hidden_sends)
-    head_block = lambda i: spec((rows, cols), lambda j: (0, i * fsdp + j))
-    from_qkv, from_out = order.hold(w_qkv, w_out)
-    heads = pl.pallas_call(
-        pack_heads_kernel,
-        grid=(fsdp,),
-        in_specs=[head_block(0), head_block(1), head_block(2), head_block(0)],
-        out_specs=spec((1, rows, 4 * cols), lambda j: (j, 0, 0)),
-        out_shape=shape((fsdp, rows, 4 * cols), NARROW),
+    )(*order.hold(w_fc1, w_fc2))
+    hidden_sends = order.wait(hidden_sends)
+    heads_sends = pl.pallas_call(
+        functools.partial(pack_heads_kernel, chips),
+        in_specs=[scalar_spec()] + [in_vmem] * 2,
+        out_shape=[shape((2, rows, 4 * cols), NARROW)] * chips,
         compiler_params=params(),
         cost_estimate=cost(10**6, 3 * 10**6),
         name="pack_heads",
-    )(from_qkv, from_qkv, from_qkv, from_out)
-    heads = order.wait(heads)
+    )(chip_at, *order.hold(w_qkv, w_out))
+    heads_sends = order.wait(*heads_sends)
     gathered = order.wait(gathered)
-    hidden_going = order.hold(*hidden_sends)
-    hidden_hops = [hop_rep(hidden_going[k], k) for k in range(1, rep)]
-    heads_came = lax.all_to_all(order.hold(heads), RING, 0, 0, tiled=True)
+    hidden_own = lax.all_to_all(order.hold(hidden_sends), GROUP, 0, 0, tiled=True)
 
     def fields_of(gathered):
-        fields, start = [], 0
-        for values in small:
-            fields.append(gathered[:, start : start + values.size])
-            start += values.size
+        fields, row = [], 0
+        for values, count_of in zip(flat_small, rows_of):
+            field = gathered[:, row : row + count_of]
+            if values.shape[1] <= LANES:
+                field = field[:, :, : values.shape[1]]
+            else:
+                field = field.reshape(devices, values.shape[0], -1)[:, :, : values.shape[1]]
+            fields.append(field)
+            row += count_of
         return fields
 
-    def open_layer(inner):
+    def join_heads(parts):
+        def steps(inner):
+            for_other = jnp.stack(
+                [lax.dynamic_index_in_dim(values, 1 - core, 0, False) for values in parts]
+            )
+            return pl.pallas_call(
+                functools.partial(join_heads_kernel, chips),
+                in_specs=[scalar_spec()] * 2 + [in_vmem] * (chips + 1),
+                out_shape=shape((fsdp, rows, 4 * cols), NARROW),
+                compiler_params=params(),
+                cost_estimate=cost(10**6, 3 * 10**6),
+                name="join_heads",
+            )(chip_at, core_at, swap_core(for_other), *parts)
+
+        return steps
+
+    def norm_streams(inner):
+        heads_hops = [hop_chip(heads_sends[m], m) for m in range(1, chips)]
         mix_padded = jnp.pad(mix_in, ((0, 0), (0, LANES - count * entries)))
         fields = fields_of(gathered)
-        gains = fields[0].reshape(devices, 3, rows).transpose(1, 0, 2).reshape(3, width)
-        shifts = fields[1].reshape(devices, 2, rows).transpose(1, 0, 2).reshape(2, width)
+        gains = fields[0].transpose(1, 0, 2).reshape(3, width)
+        shifts = fields[1].transpose(1, 0, 2).reshape(2, width)
         affine = jnp.stack([gains[0], shifts[0], gains[1], shifts[1]]).astype(SINGLE)
         normed = pl.pallas_call(
             functools.partial(streams_kernel, chips),
@@ -750,7 +799,11 @@
             name="streams",
         )(chip_at, history, mix_padded, affine)
         normed = inner.wait(*normed)
-        qkv_near = [hop_chip(normed[0], m) for m in around]
+        return normed, affine, mix_padded, inner.wait(*heads_hops)
+
+    def open_layer(inner):
+        normed, affine, mix_padded, heads_hops = inner.scope(norm_streams)
+        qkv_near = [hop_chip(inner.hold(normed[0]), m) for m in around]
         documents, group_of, weight_of = inner.hold(doc_ids[0], doc_group[0], group_weight)
         doc_match = documents[:, None] == jnp.arange(doc_group.shape[1], dtype=jnp.int32)[None, :]
         token_group = jnp.sum(jnp.where(doc_match, group_of[None, :], 0), axis=1)
@@ -758,10 +811,11 @@
             token_group[:, None] == jnp.arange(group_weight.shape[0], dtype=jnp.int32)[None, :]
         )
         token_weight = jnp.sum(jnp.where(group_match, weight_of[None, :], 0.0), 1, keepdims=True)
+        token_weight = inner.wait(jnp.broadcast_to(token_weight, (length, LANES)))
         dots = pl.pallas_call(
             history_dots_kernel,
             grid=(steps,),
-            in_specs=[tall(entries), tall(count), flat(1)],
+            in_specs=[tall(entries), tall(count), flat(LANES)],
             out_specs=flat(LANES),
             out_shape=shape((length, LANES), SINGLE),
             compiler_params=params(),
@@ -769,35 +823,21 @@
             name="history_dots",
         )(history, cotangent, token_weight)
         dots = inner.wait(dots)
-        return normed, affine, dots, token_weight, inner.wait(*qkv_near), mix_padded
-
-    normed, affine, dots, token_weight, qkv_near, mix_padded = order.scope(open_layer)
-    heads_came = order.wait(heads_came)
+        heads_came = inner.scope(join_heads([heads_sends[0], *heads_hops]))
+        return normed, affine, dots, token_weight, inner.wait(*qkv_near), mix_padded, heads_came
+
+    normed, affine, dots, token_weight, qkv_near, mix_padded, heads_came = order.scope(open_layer)
     qkv_norm, resid_norm, last = normed
-    hidden_came = [hidden_sends[0], *order.wait(*hidden_hops)]
+    hidden_own = order.wait(hidden_own)
 
     resid_norm = order.hold(resid_norm)
     resid_hops = [hop_rep(resid_norm, k) for k in range(1, rep)]
-
-    def join_hidden(inner):
-        for_other = jnp.stack(
-            [lax.dynamic_index_in_dim(values, 1 - core, 0, False) for values in hidden_came]
-        )
-        joined = pl.pallas_call(
-            functools.partial(join_hidden_kernel, rep),
-            in_specs=[scalar_spec()] * 2 + [in_vmem] * (rep + 1),
-            out_shape=shape((2, 2, rep, rows, hid_cols), NARROW),
-            compiler_params=params(),
-            cost_estimate=cost(10**6, 5 * 10**6),
-            name="join_hidden",
-        )(core_at, line_at, swap_core(for_other), *hidden_came)
-        return joined.reshape(2, part, hid_cols)
 
     def prepare(inner):
         mix_copies = jnp.pad(w_mix1.astype(NARROW), ((0, 0), (0, LANES - hid)))
         mix_copies = inner.wait(jnp.broadcast_to(mix_copies[None], (devices, rows, LANES)))
         fields = fields_of(inner.hold(gathered))
-        gain = fields[0].reshape(devices, 3, rows)[:, 2].reshape(1, width).astype(SINGLE)
+        gain = fields[0][:, 2].reshape(1, width).astype(SINGLE)
         qkv_bias = fields[2].reshape(3, fsdp, cols).astype(SINGLE)
         branch_bias = fields[3].reshape(1, width).astype(SINGLE)
         branch_bias = branch_bias + fields[5].reshape(1, width).astype(SINGLE)
@@ -825,20 +865,22 @@
             ]
         )
         rope = jnp.concatenate([rope, rope], 1)
-        pairs = [(pair, pair.reshape(2 * length, 1)) for pair in doc_rows]
+        pairs = [
+            (pair, jnp.broadcast_to(pair.reshape(2 * length, 1), (2 * length, LANES)))
+            for pair in doc_rows
+        ]
         ready = (gain, my_qkv_bias.reshape(1, 3 * cols), my_first_bias, branch_bias, rope, pairs)
         leaves, tree = jax.tree.flatten(ready)
         return mix_copies, jax.tree.unflatten(tree, inner.wait(*leaves))
 
     def spread_weights(inner):
-        joined = inner.scope(join_hidden)
-        near = [hop_chip(joined, m) for m in around]
+        near = [hop_chip(inner.hold(hidden_own), m) for m in around]
         mix_copies, prepared = inner.scope(prepare)
         first_mix = lax.all_to_all(inner.hold(mix_copies), AXES, 0, 0, tiled=True)
         near = inner.wait(*near)
-        return joined, near, inner.wait(first_mix).reshape(width, LANES), prepared
-
-    hidden_own, hidden_near, mix_first, prepared = order.scope(spread_weights)
+        return near, inner.wait(first_mix).reshape(width, LANES), prepared
+
+    hidden_near, mix_first, prepared = order.scope(spread_weights)
     gain, my_qkv_bias, my_first_bias, branch_bias, rope, doc_pairs = prepared
     resid_hops = order.wait(*resid_hops)
 
@@ -881,8 +923,8 @@
     def feed_forward(inner):
         ends = []
         if square:
-            upper = hop_chip(inner.hold(hidden_near[0])[0:1], 2)
-            lower = hop_chip(inner.hold(hidden_near[1])[1:2], 1)
+            upper = hop_chip(inner.hold(hidden_near[0])[:, 0:1], 2)
+            lower = hop_chip(inner.hold(hidden_near[1])[:, 1:2], 1)
         whole = inner.wait(jnp.stack([resid_norm, *resid_hops]))
         other = inner.wait(swap_core(whole))
         qkv_other = inner.scope(lambda _: [swap_core(values) for values in qkv_first])
@@ -1010,7 +1052,7 @@
             spec((LANES, LANES)),
             spec((1, LANES)),
             tall2(count),
-            flat2(1),
+            flat2(LANES),
             flat2(LANES),
         ],
         out_specs=[flat2(width)] * 5
@@ -1076,7 +1118,7 @@
             out_shape=[
                 shape((3, 2 * length, cols), NARROW),
                 shape((1, 3 * cols), SINGLE),
-                shape((3, length, width), SINGLE),
+                shape((3, length, width), NARROW),
                 shape((3, length, width), NARROW),
             ],
             compiler_params=params(),
@@ -1258,11 +1300,11 @@
     def send_terms(inner):
         middle = range(1, far)
         swaps = [swap_core(inner.hold(returned[m][3])) for m in middle]
-        first_grads = outer(inner, (inner.hold(resid_sides[0]), resid_sides[1]), grad_hidden)
         swaps = list(inner.wait(*swaps)) if len(swaps) > 1 else [inner.wait(*swaps)]
         owns = [results[2] for results in returned]
         near_terms = near_sums(inner, owns, [None, *swaps, far_came], halves)
         qkv_back = [hop_chip(near_terms[m - 1], m) for m in around]
+        first_grads = outer(inner, (inner.hold(resid_sides[0]), resid_sides[1]), grad_hidden)
         first_halves = send_far(inner.hold(first_grads[far]), 0)
 
         def pack_sums(_):
@@ -1298,13 +1340,12 @@
 
     first_own_grad, first_terms, qkv_back, sums = order.scope(send_terms)
     second_came = order.wait(second_came)
-    sums = order.hold(sums)
-    sums = lax.all_to_all(sums, AXES, 0, 0, tiled=True)
     widths = [rows, 3 * cols * fsdp // devices, rows, rows * hid]
 
     qkv_rest = [own_came, *qkv_back]
 
     def close_layer(inner):
+        every = lax.all_to_all(inner.hold(sums), AXES, 0, 0, tiled=True)
         held = inner.hold(*first_terms)
         first_hops = [hop_chip(held[m - 1], m) for m in around]
         close_from = inner.hold(history, cotangent)
@@ -1316,7 +1357,7 @@
                 tall(entries),
                 tall(count),
                 flat(LANES),
-                flat(1),
+                flat(LANES),
                 flat(LANES),
                 spec((4, width)),
                 flat(width),
@@ -1350,18 +1391,18 @@
             *grad_resid,
         )
         grad_history, grad_mix_in, grad_affine = inner.wait(grad_history, grad_mix_in, grad_affine)
-
-        return grad_history, grad_mix_in, grad_affine, total_hidden(inner, first_own_grad, first_hops)
-
-    grad_history, grad_mix_in, grad_affine, first_total = order.scope(close_layer)
-    sums = order.wait(sums)
-    first_bias_all = lax.dynamic_update_index_in_dim(
-        jnp.zeros((group, hid_cols), SINGLE), grad_first_bias[0], core * rep + line, 0
-    )
-    every = order.wait(
-        jnp.concatenate([by_owner(grad_affine), first_bias_all.reshape(devices, -1)], 1)
-    )
-    every = order.wait(lax.all_to_all(every, AXES, 0, 0, tiled=True))
+        every = inner.wait(every)
+        first_bias_all = lax.dynamic_update_index_in_dim(
+            jnp.zeros((group, hid_cols), SINGLE), grad_first_bias[0], core * rep + line, 0
+        )
+        late = [by_owner(grad_affine), first_bias_all.reshape(devices, -1)]
+        late = inner.wait(jnp.concatenate(late, 1))
+        late = lax.all_to_all(late, AXES, 0, 0, tiled=True)
+
+        first_total = total_hidden(inner, first_own_grad, first_hops)
+        return grad_history, grad_mix_in, first_total, inner.wait(late), every
+
+    grad_history, grad_mix_in, first_total, every, sums = order.scope(close_layer)
     first_came = lax.all_to_all(order.hold(first_total), GROUP, 0, 0, tiled=True)
     grad_w_fc2 = order.wait(whole_rows(second_came))
     every = order.wait(jnp.sum(every, 0))

time: 654 us -> 611 us (0.934)
  local copies, waits for them, and re-layouts: 95.7 us -> 80.3 us
  blocking collectives: 11.7 us -> 0 us
  loops' own time: 13.2 us -> 2.59 us
  other arithmetic: 47.1 us -> 38.1 us
    ppermute x31 -> x34, waiting for transfers between devices: 129 us -> 113 us  [hop_chip(): return lax.ppermute(values, 'chip', [(i, i ^ m) for i in range(chips)])]
    another operation x19 -> x13, local copies, waits for them, and re-layouts: 22.3 us -> 8.06 us
    all_to_all x1 -> x0, blocking collectives: 11.7 us -> none  [on_device(): every = order.wait(lax.all_to_all(every, AXES, 0, 0, tiled=True))]
    another operation x18 -> x19, loops' own time: 13.2 us -> 2.59 us  [scope(): results = lax.cond(self.hold(self.legal), inside, never)]
    all_to_all x2 -> x3, waiting for transfers between devices: 0.01 us -> 9.71 us  [the longest x1 6.96 us: close_layer(): every = lax.all_to_all(inner.hold(sums), AXES, 0, 0, tiled=True)]
    cond x78 -> x73, local copies, waits for them, and re-layouts: 16.2 us -> 9.58 us
    ppermute x19, waiting for transfers between devices: 27.1 us -> 33.8 us  [swap_core(): return lax.ppermute(values, 'core', [(0, 1), (1, 0)])]
    ppermute x15 -> x12, starting transfers between devices: 22.1 us -> 17.6 us  [hop_rep(): return lax.ppermute(values, 'rep', [(i, i ^ k) for i in range(rep)])]
  transfers between devices with their start and end apart: 73 -> 74, of which waited for: 29 -> 38; matrix products, arithmetic and copies ran while one was open for 19% -> 17% of each run, Pallas kernels for 31% -> 32%
where the time goes in v4:
time: 611 us; the launch traced here: 600 us
  Pallas kernels  205 us (34%)
  waiting for transfers between devices  167 us (27%)
  starting transfers between devices  91.5 us (15%)
  local copies, waits for them, and re-layouts  80.3 us (13%)
  other arithmetic  38.1 us (6%)
  between operations  14.7 us (2%)
    ppermute x34, waiting for transfers between devices, hop_chip(): return lax.ppermute(values, 'chip', [(i, i ^ m) for i in range(chips)])  113 us
    ppermute x34, starting transfers between devices, hop_chip(): return lax.ppermute(values, 'chip', [(i, i ^ m) for i in range(chips)])  37.2 us
    ppermute x19, waiting for transfers between devices, swap_core(): return lax.ppermute(values, 'core', [(0, 1), (1, 0)])  33.8 us
    pallas_call x4, Pallas kernels, attend_back(): pl.pallas_call(attend_back_kernel, out_shape=[shape((3, 2 * length, cols)...  29.6 us
    pallas_call x4, Pallas kernels, attend(): pl.pallas_call(attend_kernel, out_shape=[shape((3, 2 * length, cols), NAR...  26.5 us
    pallas_call x2, Pallas kernels, hidden_back_side(): pl.pallas_call(functools.partial(hidden_back_kernel, chips, bool(came)),...  18.9 us
    pallas_call x1, Pallas kernels, close_layer(): pl.pallas_call(functools.partial(close_kernel, chips, len(qkv_rest), rep)...  18.5 us
    pallas_call x2, Pallas kernels, outer(): pl.pallas_call(outer_kernel, grid=(chips,), in_specs=[spec((rep * length,...  18.3 us
  transfers between devices with their start and end apart: 74, of which 38 were waited for; matrix products, arithmetic and copies ran while one was open for 17% of the time, Pallas kernels for 32%

profile of v4, /device:TPU:0, one launch (start us, length us, event | category | flops | bytes accessed | tf_op | source)
XLA Modules:
  0.0 600.3 jit_solution(758487155495481685)
XLA Ops:
  28.3 51.8 %conditional.19 = (bf16[3,128,2048]{2,1,0:T(8,128)(2,1)}, bf16[128,2048]{1,0:T(8,128)(2,1)S(1)}, f32[128,2048]{1,0:T(8,128)}, f32[4,2048]{1,0:T(4,128)}, f32[128...) conditional(s32[]{:T(128)} %convert_element_type.329, ...), branch_computations={%region_0.0_spmd, %region_1.8_spmd} | conditional | flops 1062702 | bytes 25345874 | solution.py:604
  28.3 15.1 %conditional = (bf16[3,128,2048]{2,1,0:T(8,128)(2,1)}, bf16[128,2048]{1,0:T(8,128)(2,1)}, f32[128,2048]{1,0:T(8,128)}, f32[4,2048]{1,0:T(4,128)}, f32[128,128]{1...) conditional(s32[]{:T(128)} %convert_element_type.235, () %tuple.91, ...), branch_computations={%region_2.0_spmd, %region_3.3_spmd} | conditional | flops 165536 | bytes 4030550 | solution.py:604
  33.7 9.0 %streams.1 = (bf16[3,128,2048]{2,1,0:T(8,128)(2,1)}, bf16[128,2048]{1,0:T(8,128)(2,1)}, f32[128,2048]{1,0:T(8,128)}) custom-call(s32[1]{0:T(128)} %get-tuple-element.516.chip, bf16[9,128,2048]{2,1,0:T(8,128)(2,1)} %get-tuple-element.517.hist, f32[128,128]{1,0:T(8,128)} %pad.15.mix, f32[4,2048]{1,0:T(4,128)} %maximum_convert_fusion.affine), custom_call_target="tpu_custom_call" | custom-call | flops 100000 | bytes 10000 | tf_op jit(solution)/shard_map/cond/branch_1_fun/cond/branch_1_fun/streams/pallas_call | solution.py:786
  45.7 7.7 %history_dots.1 = f32[128,128]{1,0:T(8,128)S(1)} custom-call(bf16[9,128,2048]{2,1,0:T(8,128)(2,1)} %get-tuple-element.539.hist, bf16[4,128,2048]{2,1,0:T(8,128)(2,1)} %get-tuple-element.547.cot, f32[128,128]{1,0:T(8,128)S(1)} %broadcast_in_dim.54.weight), custom_call_target="tpu_custom_call" | custom-call | flops 100000 | bytes 10000 | tf_op jit(solution)/shard_map/cond/branch_1_fun/history_dots/pallas_call | solution.py:815
  60.6 18.6 %collective-permute-done.24 = bf16[3,128,2048]{2,1,0:T(8,128)(2,1)} collective-permute-done((bf16[3,128,2048]{2,1,0:T(8,128)(2,1)}, bf16[3,128,2048]{2,1,0:T(8,128)(2,1)}, u32[]{:S(2)}, u32[]{:S(2)}) %collective-permute-start.24) | collective-permute-done | bytes 1572896 | tf_op jit(solution)/shard_map/cond/branch_1_fun/ppermute | solution.py:658
  85.1 51.6 %conditional.20 = (bf16[8,2,64,1024]{3,2,1,0:T(8,128)(2,1)}, bf16[8,2,64,1024]{3,2,1,0:T(8,128)(2,1)}, bf16[2048,128]{1,0:T(8,128)(2,1)}, f32[1,2048]{1,0:T(1,12...) conditional(s32[]{:T(128)} %convert_element_type.330, ...), branch_computations={%region_8.9_spmd, %region_9.12_spmd} | conditional | flops 626144 | bytes 21155228 | solution.py:604
  87.5 12.4 %conditional.2 = (bf16[32,64,128]{2,1,0:T(8,128)(2,1)}, f32[1,2048]{1,0:T(1,128)}, f32[1,768]{1,0:T(1,128)}, f32[1,1024]{1,0:T(1,128)}, f32[1,2048]{1,0:T(1,128)...) conditional(s32[]{:T(128)} %convert_element_type.255, ...), branch_computations={%region_10.10_spmd, %region_11.11_spmd} | conditional | flops 626143 | bytes 2804863 | solution.py:604
  104.1 29.3 %collective-permute-done.6 = bf16[8,2,64,1024]{3,2,1,0:T(8,128)(2,1)} collective-permute-done((bf16[8,2,64,1024]{3,2,1,0:T(8,128)(2,1)S(1)}, bf16[8,2,64,1024]{3,2,1,0:T(8,128)(2,1)}, u32[]{:S(2)}, u32[]{:S(2)}) %collective-permute-start.6) | collective-permute-done | bytes 2097184 | tf_op jit(solution)/shard_map/cond/branch_1_fun/ppermute | solution.py:658
  136.8 76.2 %conditional.21 = (bf16[8,1,64,1024]{3,2,1,0:T(8,128)(2,1)}, bf16[8,1,64,1024]{3,2,1,0:T(8,128)(2,1)S(1)}, bf16[512,2048]{1,0:T(8,128)(2,1)}, bf16[512,2048]{1,0...) conditional(s32[]{:T(128)} %convert_element_type.331, ...), branch_computations={%region_12.13_spmd, %region_13.18_spmd} | conditional | flops 14881390 | bytes 88121168 | solution.py:604
  148.0 8.3 %conditional.3 = (bf16[3,128,2048]{2,1,0:T(8,128)(2,1)}, bf16[3,128,2048]{2,1,0:T(8,128)(2,1)}, bf16[3,128,2048]{2,1,0:T(8,128)(2,1)}) conditional(s32[]{:T(128)} %convert_element_type.256, () %tuple.123, (bf16[3,128,2048]{2,1,0:T(8,128)(2,1)}, bf16[3,128,2048]{2,1,0:T(8,128)(2,1)}, bf16[3,128,2048]{2,1,0:T(8,128)(2,1)}) %tuple.124), branch_computations={%region_14.14_spmd, %region_15.15_spmd} | conditional | bytes 18874512 | solution.py:604
  156.3 12.9 %collective-permute-done.7.refs_3_ = bf16[8,1,64,1024]{3,2,1,0:T(8,128)(2,1)} collective-permute-done((bf16[8,1,64,1024]{3,2,1,0:T(8,128)(2,1)}, bf16[8,1,64,1024]{3,2,1,0:T(8,128)(2,1)}, u32[]{:S(2)}, u32[]{:S(2)}) %collective-permute-start.7) | collective-permute-done | bytes 1048608 | tf_op jit(solution)/shard_map/cond/branch_1_fun/ppermute | solution.py:658
  185.2 20.8 %conditional.4 = (bf16[512,1024]{1,0:T(8,128)(2,1)}, f32[512,1024]{1,0:T(8,128)}, bf16[128,2048]{1,0:T(8,128)(2,1)}, bf16[128,2048]{1,0:T(8,128)(2,1)}, bf16[128...) conditional(s32[]{:T(128)} %convert_element_type.257, () %tuple.129, (bf16[512,1024]{1,0:T(8,128)(2,1)}, ...), branch_computations={%region_16.16_spmd, %region_17.17_spmd} | conditional | flops 6442449 | bytes 16807332 | solution.py:604
  224.3 49.6 %conditional.22 = (bf16[2048,1024]{1,0:T(8,128)(2,1)}, bf16[3,256,256]{2,1,0:T(8,128)(2,1)S(1)}, bf16[3,256,256]{2,1,0:T(8,128)(2,1)}, bf16[3,256,256]{2,1,0:T(8...) conditional(s32[]{:T(128)} %convert_element_type.332, ...), branch_computations={%region_18.19_spmd, %region_19.20_spmd} | conditional | flops 10324276 | bytes 51937008 | solution.py:604
  273.9 8.5 %mixing.1 = (f32[128,2048]{1,0:T(8,128)}, f32[128,2048]{1,0:T(8,128)}, bf16[128,2048]{1,0:T(8,128)(2,1)}, bf16[128,2048]{1,0:T(8,128)(2,1)}, bf16[128,2048]{1,0:...) custom-call(s32[1]{0:T(128)} %bitcast.70.chip, ...), custom_call_target="tpu_custom_call" | custom-call | flops 200000 | bytes 10000 | tf_op jit(solution)/shard_map/mixing/pallas_call | solution.py:1040
  286.9 45.0 %conditional.23 = (bf16[3,256,256]{2,1,0:T(8,128)(2,1)}, f32[1,768]{1,0:T(1,128)}, bf16[3,128,2048]{2,1,0:T(8,128)(2,1)}, bf16[3,128,2048]{2,1,0:T(8,128)(2,1)},...) conditional(s32[]{:T(128)} %convert_element_type.333, ...), branch_computations={%region_20.21_spmd, %region_21.22_spmd} | conditional | flops 63441720 | bytes 45827804 | solution.py:604
  291.4 7.5 %attend_back.4 = (bf16[3,256,256]{2,1,0:T(8,128)(2,1)}, f32[1,768]{1,0:T(1,128)}, bf16[3,128,2048]{2,1,0:T(8,128)(2,1)}, bf16[3,128,2048]{2,1,0:T(8,128)(2,1)}) custom-call(bf16[128,2048]{1,0:T(8,128)(2,1)} %get-tuple-element.756.own, bf16[128,2048]{1,0:T(8,128)(2,1)} %collective-permute-done.50.other, bf16[2048,1024]{1,0:T(8,128)(2,1)} %get-tuple-element.743.weight, ...), custom_call_target="tpu_custom_call" | custom-call | flops 1073741 | bytes 8000 | tf_op jit(solution)/shard_map/cond/branch_1_fun/attend_back/pallas_call | solution.py:1116
  331.9 42.9 %conditional.24 = (bf16[512,2048]{1,0:T(8,128)(2,1)}, bf16[512,2048]{1,0:T(8,128)(2,1)}, bf16[512,1024]{1,0:T(8,128)(2,1)S(1)}, bf16[512,1024]{1,0:T(8,128)(2,1)...) conditional(s32[]{:T(128)} %convert_element_type.334, ...), branch_computations={%region_22.23_spmd, %region_23.26_spmd} | conditional | flops 15931991 | bytes 64025896 | solution.py:604
  335.7 9.4 %hidden_back.2 = (bf16[512,1024]{1,0:T(8,128)(2,1)}, f32[1,1024]{1,0:T(1,128)}, bf16[512,2048]{1,0:T(8,128)(2,1)}) custom-call(bf16[512,2048]{1,0:T(8,128)(2,1)} %bitcast.45.grad, f32[512,1024]{1,0:T(8,128)} %get-tuple-element.798.slope, bf16[8,2,64,1024]{3,2,1,0:T(8,128)(2,1)S(1)} %get-tuple-element.799.refs_0_.refs_4_, ...), custom_call_target="tpu_custom_call" | custom-call | flops 4294967 | bytes 20000 | tf_op jit(solution)/shard_map/cond/branch_1_fun/hidden_back/pallas_call | solution.py:1171
  356.0 9.5 %hidden_back.3 = (bf16[512,1024]{1,0:T(8,128)(2,1)}, f32[1,1024]{1,0:T(1,128)}, bf16[512,2048]{1,0:T(8,128)(2,1)}) custom-call(bf16[512,2048]{1,0:T(8,128)(2,1)} %bitcast.46.grad, f32[512,1024]{1,0:T(8,128)} %get-tuple-element.813.slope, bf16[8,2,64,1024]{3,2,1,0:T(8,128)(2,1)S(1)} %get-tuple-element.799.refs_0_.refs_4_, ...), custom_call_target="tpu_custom_call" | custom-call | flops 4294967 | bytes 20000 | tf_op jit(solution)/shard_map/cond/branch_1_fun/hidden_back/pallas_call | solution.py:1171
  366.2 7.9 %conditional.5 = (bf16[128,2048]{1,0:T(8,128)(2,1)}, bf16[128,2048]{1,0:T(8,128)(2,1)}, bf16[128,2048]{1,0:T(8,128)(2,1)}, bf16[128,2048]{1,0:T(8,128)(2,1)}) conditional(s32[]{:T(128)} %convert_element_type.284, () %tuple.180, (bf16[512,2048]{1,0:T(8,128)(2,1)}, bf16[512,2048]{1,0:T(8,128)(2,1)}) %tuple.181), branch_computations={%region_24.24_spmd, %region_25.25_spmd} | conditional | flops 4194304 | bytes 14680136 | solution.py:604
  376.1 53.5 %conditional.25 = (bf16[128,2048]{1,0:T(8,128)(2,1)}, bf16[128,2048]{1,0:T(8,128)(2,1)}, bf16[128,2048]{1,0:T(8,128)(2,1)}, bf16[4,8,64,1024]{3,2,1,0:T(8,128)(2...) conditional(s32[]{:T(128)} %convert_element_type.335, ...), branch_computations={%region_26.27_spmd, %region_27.30_spmd} | conditional | flops 17028872 | bytes 44631444 | solution.py:604
  380.5 49.1 %conditional.6 = (bf16[4,8,64,1024]{3,2,1,0:T(8,128)(2,1)}, f32[1,768]{1,0:T(1,128)}, bf16[3,128,2048]{2,1,0:T(8,128)(2,1)}, bf16[3,128,2048]{2,1,0:T(8,128)(2,1...) conditional(s32[]{:T(128)} %convert_element_type.291, ...), branch_computations={%region_28.28_spmd, %region_29.29_spmd} | conditional | flops 17028872 | bytes 38339488 | solution.py:604
  380.5 9.5 %outer.2 = (bf16[512,1024]{1,0:T(8,128)(2,1)}, bf16[512,1024]{1,0:T(8,128)(2,1)}, bf16[512,1024]{1,0:T(8,128)(2,1)}, bf16[512,1024]{1,0:T(8,128)(2,1)}) custom-call(bf16[512,2048]{1,0:T(8,128)(2,1)} %get-tuple-element.848.left_own, bf16[512,2048]{1,0:T(8,128)(2,1)} %get-tuple-element.849.left_other, bf16[512,1024]{1,0:T(8,128)(2,1)} %get-tuple-element.850.right_own, ...), custom_call_target="tpu_custom_call" | custom-call | flops 4294967 | bytes 20000 | tf_op jit(solution)/shard_map/cond/branch_1_fun/cond/branch_1_fun/outer/pallas_call | solution.py:1190
  407.6 7.4 %attend_back.7 = (bf16[3,256,256]{2,1,0:T(8,128)(2,1)}, f32[1,768]{1,0:T(1,128)}, bf16[3,128,2048]{2,1,0:T(8,128)(2,1)}, bf16[3,128,2048]{2,1,0:T(8,128)(2,1)}) custom-call(bf16[128,2048]{1,0:T(8,128)(2,1)} %get-tuple-element.872.own.refs_12_, bf16[128,2048]{1,0:T(8,128)(2,1)} %get-tuple-element.873.other.refs_13_, ...), custom_call_target="tpu_custom_call" | custom-call | flops 1073741 | bytes 8000 | tf_op jit(solution)/shard_map/cond/branch_1_fun/cond/branch_1_fun/attend_back/pallas_call | solution.py:1116
  415.1 12.7 %heads_grad.1 = bf16[4,8,64,1024]{3,2,1,0:T(8,128)(2,1)} custom-call(bf16[3,128,2048]{2,1,0:T(8,128)(2,1)} %get-tuple-element.831.refs_0_, bf16[3,128,2048]{2,1,0:T(8,128)(2,1)} %get-tuple-element.832.refs_1_, bf16[3,128,2048]{2,1,0:T(8,128)(2,1)} %get-tuple-element.833.refs_2_, bf16[3,128,2048]{2,1,0:T(8,128)(2,1)} %get-tuple-element.834.refs_3_, ...), custom_call_target="tpu_custom_call" | custom-call | flops 4294967 | bytes 30000 | tf_op jit(solution)/shard_map/cond/branch_1_fun/cond/branch_1_fun/heads_grad/pallas_call | solution.py:1257
  436.9 68.5 %conditional.27 = (bf16[512,1024]{1,0:T(8,128)(2,1)}, bf16[512,1024]{1,0:T(8,128)(2,1)}, bf16[512,1024]{1,0:T(8,128)(2,1)}, bf16[3,128,2048]{2,1,0:T(8,128)(2,1)...) conditional(s32[]{:T(128)} %convert_element_type.337, () %tuple.329, ...), branch_computations={%region_32.33_spmd, %region_33.36_spmd} | conditional | flops 10595597 | bytes 71393520 | solution.py:604
  453.8 8.8 %outer.3 = (bf16[512,1024]{1,0:T(8,128)(2,1)}, bf16[512,1024]{1,0:T(8,128)(2,1)}, bf16[512,1024]{1,0:T(8,128)(2,1)}, bf16[512,1024]{1,0:T(8,128)(2,1)}) custom-call(bf16[512,2048]{1,0:T(8,128)(2,1)} %get-tuple-element.984.left_own, bf16[512,2048]{1,0:T(8,128)(2,1)} %get-tuple-element.985.left_other, bf16[512,1024]{1,0:T(8,128)(2,1)S(1)} %copy-done.9, ...), custom_call_target="tpu_custom_call" | custom-call | flops 4294967 | bytes 20000 | tf_op jit(solution)/shard_map/cond/branch_1_fun/outer/pallas_call | solution.py:1190
  471.7 13.0 %conditional.7 = (bf16[32,16,768]{2,1,0:T(8,128)(2,1)}) conditional(s32[]{:T(128)} %convert_element_type.298, () %tuple.212, (f32[1,2048]{1,0:T(1,128)S(1)}, f32[1,768]{1,0:T(1,128)}, f32[1,768]{1,0:T(1,128)}, f32[1,768]{1,0:T(1,128)}, f32[1,768]{1,0:T(1,128)}, /*index=5*/s32[]{:T(128)}, s32[]{:T(128)}, f32[1,2048]{1,0:T(1,128)S(1)}, ...), branch_computations={%region_34.34_spmd, %region_35.35_spmd} | conditional | flops 7173 | bytes 5292674 | solution.py:604
  484.7 16.4 %collective-permute-done.47 = bf16[256,1024]{1,0:T(8,128)(2,1)} collective-permute-done((bf16[256,1024]{1,0:T(8,128)(2,1)}, bf16[256,1024]{1,0:T(8,128)(2,1)}, u32[]{:S(2)}, u32[]{:S(2)}) %collective-permute-start.47) | collective-permute-done | bytes 524320 | tf_op jit(solution)/shard_map/cond/branch_1_fun/ppermute | solution.py:658
  505.4 48.1 %conditional.28 = (f32[9,128,2048]{2,1,0:T(8,128)}, f32[128,36]{1,0:T(8,128)}, bf16[8,64,1024]{2,1,0:T(8,128)(2,1)}, f32[512]{0:T(512)S(1)}, f32[12288]{0:T(1024)S(1)}, /*index=5*/f32[128,36]{0,1:T(8,128)S(1)}) conditional(s32[]{:T(128)} %convert_element_type.338, () %tuple.333, (bf16[9,128,2048]{2,1,0:T(8,128)(2,1)}, ...), branch_computations={%region_36.37_spmd, %region_37.40_spmd} | conditional | flops 4152133 | bytes 16910146 | solution.py:604
  513.6 18.5 %close.1 = (f32[9,128,2048]{2,1,0:T(8,128)}, f32[128,36]{1,0:T(8,128)}, f32[4,2048]{1,0:T(4,128)}) custom-call(s32[1]{0:T(128)} %get-tuple-element.1017.chip, bf16[9,128,2048]{2,1,0:T(8,128)(2,1)} %get-tuple-element.1020.hist, bf16[4,128,2048]{2,1,0:T(8,128)(2,1)S(1)} %get-tuple-element.1021.cot, f32[128,128]{1,0:T(8,128)} %get-tuple-element.1022.coef, ...), custom_call_target="tpu_custom_call" | custom-call | flops 200000 | bytes 20000 | tf_op jit(solution)/shard_map/cond/branch_1_fun/close/pallas_call | solution.py:1352
  564.9 23.5 %conditional.29 = (f32[64,6144]{1,0:T(8,128)S(1)}, f32[64,2048]{1,0:T(8,128)S(1)}) conditional(s32[]{:T(128)} %convert_element_type.342, () %tuple.340, (s32[]{:T(128)}, bf16[8,64,1024]{2,1,0:T(8,128)(2,1)}, s32[]{:T(128)}) %tuple.470), branch_computations={%region_41.42_spmd, %region_42.43_spmd} | conditional | flops 6291482 | bytes 30409264 | solution.py:604
  (452 shorter events, 407.8 us)
Async XLA Ops:
  24.5 55.6 %all-to-all-start.4 = ((bf16[8,2,64,1024]{3,2,1,0:T(8,128)(2,1)}), bf16[8,2,64,1024]{3,2,1,0:T(8,128)(2,1)S(1)}, u32[]{:S(2)}, u32[]{:S(2)}) async-start(bf16[8,2,64,1024]{3,2,1,0:T(8,128)(2,1)} %pack_hidden.1), calls=%async_computation.4 | async-start | bytes 4194304 | tf_op jit(solution)/shard_map/all_to_all | solution.py:749
  28.1 190.5 %all-gather.3.cloned.1.call-start = ((), (), s32[]{:S(2)}) async-start(), calls=%async_computation.9 | async-start | bytes 5242880 | tf_op jit(solution)/shard_map/all_gather | solution.py:887
  43.4 35.8 %collective-permute-start.24 = (bf16[3,128,2048]{2,1,0:T(8,128)(2,1)}, bf16[3,128,2048]{2,1,0:T(8,128)(2,1)}, u32[]{:S(2)}, u32[]{:S(2)}) collective-permute-start(bf16[3,128,2048]{2,1,0:T(8,128)(2,1)} %get-tuple-element.556), channel_id=1, source_target_pairs={{0,16},{8,24},{16,0},{24,8},{1,17},{9,25},{17,1},{25,9},{2,18},{10... | collective-permute-start | bytes 4718600 | tf_op jit(solution)/shard_map/cond/branch_1_fun/ppermute | solution.py:658
  44.9 35.2 %collective-permute-start.23 = (bf16[3,128,2048]{2,1,0:T(8,128)(2,1)}, bf16[3,128,2048]{2,1,0:T(8,128)(2,1)}, u32[]{:S(2)}, u32[]{:S(2)}) collective-permute-start(bf16[3,128,2048]{2,1,0:T(8,128)(2,1)} %get-tuple-element.556), channel_id=1, source_target_pairs={{0,8},{8,0},{16,24},{24,16},{1,9},{9,1},{17,25},{25,17},{2,10},{10... | collective-permute-start | bytes 4718600 | tf_op jit(solution)/shard_map/cond/branch_1_fun/ppermute | solution.py:658
  80.7 56.0 %collective-permute-start.58 = (bf16[128,2048]{1,0:T(8,128)(2,1)S(1)}, bf16[128,2048]{1,0:T(8,128)(2,1)S(1)}, u32[]{:S(2)}, u32[]{:S(2)}) collective-permute-start(bf16[128,2048]{1,0:T(8,128)(2,1)S(1)} %get-tuple-element.1287), channel_id=1, source_target_pairs={{0,3},{1,2},{2,1},{3,0},{4,7},{5,6},{6,5},{7,4},{8,11},{9,10},{10,... | collective-permute-start | bytes 1572872 | tf_op jit(solution)/shard_map/ppermute | solution.py:661
  83.9 52.8 %collective-permute-start.57 = (bf16[128,2048]{1,0:T(8,128)(2,1)S(1)}, bf16[128,2048]{1,0:T(8,128)(2,1)}, u32[]{:S(2)}, u32[]{:S(2)}) collective-permute-start(bf16[128,2048]{1,0:T(8,128)(2,1)S(1)} %get-tuple-element.1287), channel_id=1, source_target_pairs={{0,2},{1,3},{2,0},{3,1},{4,6},{5,7},{6,4},{7,5},{8,10},{9,11},{10,... | collective-permute-start | bytes 1572872 | tf_op jit(solution)/shard_map/ppermute | solution.py:661
  83.9 52.8 %collective-permute-start.56 = (bf16[128,2048]{1,0:T(8,128)(2,1)S(1)}, bf16[128,2048]{1,0:T(8,128)(2,1)}, u32[]{:S(2)}, u32[]{:S(2)}) collective-permute-start(bf16[128,2048]{1,0:T(8,128)(2,1)S(1)} %get-tuple-element.1287), channel_id=1, source_target_pairs={{0,1},{1,0},{2,3},{3,2},{4,5},{5,4},{6,7},{7,6},{8,9},{9,8},{10,11... | collective-permute-start | bytes 1572872 | tf_op jit(solution)/shard_map/ppermute | solution.py:661
  85.1 48.3 %collective-permute-start.6 = (bf16[8,2,64,1024]{3,2,1,0:T(8,128)(2,1)S(1)}, bf16[8,2,64,1024]{3,2,1,0:T(8,128)(2,1)}, u32[]{:S(2)}, u32[]{:S(2)}) collective-permute-start(bf16[8,2,64,1024]{3,2,1,0:T(8,128)(2,1)S(1)} %get-tuple-element.585), channel_id=1, source_target_pairs={{0,16},{8,24},{16,0},{24,8},{1,17},{9,25},{17,1},{25,9},{2,18},{10... | collective-permute-start | bytes 6291464 | tf_op jit(solution)/shard_map/cond/branch_1_fun/ppermute | solution.py:658
  86.0 48.4 %collective-permute-start.5 = (bf16[8,2,64,1024]{3,2,1,0:T(8,128)(2,1)S(1)}, bf16[8,2,64,1024]{3,2,1,0:T(8,128)(2,1)}, u32[]{:S(2)}, u32[]{:S(2)}) collective-permute-start(bf16[8,2,64,1024]{3,2,1,0:T(8,128)(2,1)S(1)} %get-tuple-element.585), channel_id=1, source_target_pairs={{0,8},{8,0},{16,24},{24,16},{1,9},{9,1},{17,25},{25,17},{2,10},{10... | collective-permute-start | bytes 6291464 | tf_op jit(solution)/shard_map/cond/branch_1_fun/ppermute | solution.py:658
  99.9 36.8 %all-to-all-start = ((bf16[32,64,128]{2,1,0:T(8,128)(2,1)}), bf16[32,64,128]{2,1,0:T(8,128)(2,1)}, u32[]{:S(2)}, u32[]{:S(2)}) async-start(bf16[32,64,128]{2,1,0:T(8,128)(2,1)} %get-tuple-element.596), calls=%async_computation | async-start | bytes 1048576 | tf_op jit(solution)/shard_map/cond/branch_1_fun/all_to_all | solution.py:879
  136.8 428.1 %reduce-scatter.2.cloned.1.call-start = ((), (), s32[]{:S(2)}) async-start(), calls=%async_computation.8 | async-start | bytes 5242880 | tf_op jit(solution)/shard_map/reduce_scatter | solution.py:1293
  143.8 25.4 %collective-permute-start.7 = (bf16[8,1,64,1024]{3,2,1,0:T(8,128)(2,1)}, bf16[8,1,64,1024]{3,2,1,0:T(8,128)(2,1)}, u32[]{:S(2)}, u32[]{:S(2)}) collective-permute-start(bf16[8,1,64,1024]{3,2,1,0:T(8,128)(2,1)} %slice.312), channel_id=1, source_target_pairs={{0,16},{8,24},{16,0},{24,8},{1,17},{9,25},{17,1},{25,9},{2,18},{10... | collective-permute-start | bytes 3145736 | tf_op jit(solution)/shard_map/cond/branch_1_fun/ppermute | solution.py:658
  176.9 29.0 %collective-permute-start.11 = (bf16[3,64,2048]{2,1,0:T(8,128)(2,1)}, bf16[3,64,2048]{2,1,0:T(8,128)(2,1)}, u32[]{:S(2)}, u32[]{:S(2)}) collective-permute-start(bf16[3,64,2048]{2,1,0:T(8,128)(2,1)} %slice.221), channel_id=1, source_target_pairs={{0,8},{8,0},{16,24},{24,16},{1,9},{9,1},{17,25},{25,17},{2,10},{10... | collective-permute-start | bytes 2359304 | tf_op jit(solution)/shard_map/cond/branch_1_fun/ppermute | solution.py:658
  177.7 28.3 %collective-permute-start.10 = (bf16[3,64,2048]{2,1,0:T(8,128)(2,1)}, bf16[3,64,2048]{2,1,0:T(8,128)(2,1)}, u32[]{:S(2)}, u32[]{:S(2)}) collective-permute-start(bf16[3,64,2048]{2,1,0:T(8,128)(2,1)} %slice.220), channel_id=1, source_target_pairs={{0,16},{8,24},{16,0},{24,8},{1,17},{9,25},{17,1},{25,9},{2,18},{10... | collective-permute-start | bytes 2359304 | tf_op jit(solution)/shard_map/cond/branch_1_fun/ppermute | solution.py:658
  218.6 55.3 %collective-permute-start.59 = (bf16[128,2048]{1,0:T(8,128)(2,1)}, bf16[128,2048]{1,0:T(8,128)(2,1)}, u32[]{:S(2)}, u32[]{:S(2)}) collective-permute-start(bf16[128,2048]{1,0:T(8,128)(2,1)} %get-tuple-element.1326), channel_id=1, source_target_pairs={{0,1},{1,0},{2,3},{3,2},{4,5},{5,4},{6,7},{7,6},{8,9},{9,8},{10,11... | collective-permute-start | bytes 1572872 | tf_op jit(solution)/shard_map/ppermute | solution.py:661
  218.6 55.3 %collective-permute-start.60 = (bf16[128,2048]{1,0:T(8,128)(2,1)}, bf16[128,2048]{1,0:T(8,128)(2,1)}, u32[]{:S(2)}, u32[]{:S(2)}) collective-permute-start(bf16[128,2048]{1,0:T(8,128)(2,1)} %get-tuple-element.1327), channel_id=1, source_target_pairs={{0,2},{1,3},{2,0},{3,1},{4,6},{5,7},{6,4},{7,5},{8,10},{9,11},{10,... | collective-permute-start | bytes 1572872 | tf_op jit(solution)/shard_map/ppermute | solution.py:661
  219.8 54.2 %collective-permute-start.61 = (bf16[128,2048]{1,0:T(8,128)(2,1)}, bf16[128,2048]{1,0:T(8,128)(2,1)}, u32[]{:S(2)}, u32[]{:S(2)}) collective-permute-start(bf16[128,2048]{1,0:T(8,128)(2,1)} %get-tuple-element.1328), channel_id=1, source_target_pairs={{0,3},{1,2},{2,1},{3,0},{4,7},{5,6},{6,5},{7,4},{8,11},{9,10},{10,... | collective-permute-start | bytes 1572872 | tf_op jit(solution)/shard_map/ppermute | solution.py:661
  282.4 49.5 %collective-permute-start.64 = (bf16[128,2048]{1,0:T(8,128)(2,1)}, bf16[128,2048]{1,0:T(8,128)(2,1)}, u32[]{:S(2)}, u32[]{:S(2)}) collective-permute-start(bf16[128,2048]{1,0:T(8,128)(2,1)} %get-tuple-element.1363), channel_id=1, source_target_pairs={{0,3},{1,2},{2,1},{3,0},{4,7},{5,6},{6,5},{7,4},{8,11},{9,10},{10,... | collective-permute-start | bytes 1572872 | tf_op jit(solution)/shard_map/ppermute | solution.py:661
  283.3 48.6 %collective-permute-start.63 = (bf16[128,2048]{1,0:T(8,128)(2,1)}, bf16[128,2048]{1,0:T(8,128)(2,1)}, u32[]{:S(2)}, u32[]{:S(2)}) collective-permute-start(bf16[128,2048]{1,0:T(8,128)(2,1)} %get-tuple-element.1363), channel_id=1, source_target_pairs={{0,2},{1,3},{2,0},{3,1},{4,6},{5,7},{6,4},{7,5},{8,10},{9,11},{10,... | collective-permute-start | bytes 1572872 | tf_op jit(solution)/shard_map/ppermute | solution.py:661
  283.3 48.6 %collective-permute-start.62 = (bf16[128,2048]{1,0:T(8,128)(2,1)}, bf16[128,2048]{1,0:T(8,128)(2,1)}, u32[]{:S(2)}, u32[]{:S(2)}) collective-permute-start(bf16[128,2048]{1,0:T(8,128)(2,1)} %get-tuple-element.1363), channel_id=1, source_target_pairs={{0,1},{1,0},{2,3},{3,2},{4,5},{5,4},{6,7},{7,6},{8,9},{9,8},{10,11... | collective-permute-start | bytes 1572872 | tf_op jit(solution)/shard_map/ppermute | solution.py:661
  376.1 53.5 %collective-permute-start.41 = (bf16[128,2048]{1,0:T(8,128)(2,1)}, bf16[128,2048]{1,0:T(8,128)(2,1)}, u32[]{:S(2)}, u32[]{:S(2)}) collective-permute-start(bf16[128,2048]{1,0:T(8,128)(2,1)} %get-tuple-element.904), channel_id=1, source_target_pairs={{0,1},{1,0},{2,3},{3,2},{4,5},{5,4},{6,7},{7,6},{8,9},{9,8},{10,11... | collective-permute-start | bytes 1572872 | tf_op jit(solution)/shard_map/cond/branch_1_fun/ppermute | solution.py:661
  376.1 53.5 %collective-permute-start.42 = (bf16[128,2048]{1,0:T(8,128)(2,1)}, bf16[128,2048]{1,0:T(8,128)(2,1)}, u32[]{:S(2)}, u32[]{:S(2)}) collective-permute-start(bf16[128,2048]{1,0:T(8,128)(2,1)} %get-tuple-element.905), channel_id=1, source_target_pairs={{0,2},{1,3},{2,0},{3,1},{4,6},{5,7},{6,4},{7,5},{8,10},{9,11},{10,... | collective-permute-start | bytes 1572872 | tf_op jit(solution)/shard_map/cond/branch_1_fun/ppermute | solution.py:661
  377.4 52.2 %collective-permute-start.43 = (bf16[128,2048]{1,0:T(8,128)(2,1)}, bf16[128,2048]{1,0:T(8,128)(2,1)}, u32[]{:S(2)}, u32[]{:S(2)}) collective-permute-start(bf16[128,2048]{1,0:T(8,128)(2,1)} %get-tuple-element.906), channel_id=1, source_target_pairs={{0,3},{1,2},{2,1},{3,0},{4,7},{5,6},{6,5},{7,4},{8,11},{9,10},{10,... | collective-permute-start | bytes 1572872 | tf_op jit(solution)/shard_map/cond/branch_1_fun/ppermute | solution.py:661
  433.2 72.3 %all-to-all-start.5 = ((bf16[8,64,1024]{2,1,0:T(8,128)(2,1)}), bf16[8,64,1024]{2,1,0:T(8,128)(2,1)S(1)}, u32[]{:S(2)}, u32[]{:S(2)}) async-start(bf16[8,64,1024]{2,1,0:T(8,128)(2,1)} %get-tuple-element.2348), calls=%async_computation.5 | async-start | bytes 2097152 | tf_op jit(solution)/shard_map/all_to_all | solution.py:1298
  452.8 52.6 %collective-permute-start.49 = (bf16[3,128,2048]{2,1,0:T(8,128)(2,1)}, bf16[3,128,2048]{2,1,0:T(8,128)(2,1)}, u32[]{:S(2)}, u32[]{:S(2)}) collective-permute-start(bf16[3,128,2048]{2,1,0:T(8,128)(2,1)} %merge.4), channel_id=1, source_target_pairs={{0,16},{8,24},{16,0},{24,8},{1,17},{9,25},{17,1},{25,9},{2,18},{10... | collective-permute-start | bytes 4718600 | tf_op jit(solution)/shard_map/cond/branch_1_fun/ppermute | solution.py:658
  453.4 52.0 %collective-permute-start.48 = (bf16[3,128,2048]{2,1,0:T(8,128)(2,1)}, bf16[3,128,2048]{2,1,0:T(8,128)(2,1)}, u32[]{:S(2)}, u32[]{:S(2)}) collective-permute-start(bf16[3,128,2048]{2,1,0:T(8,128)(2,1)} %merge.5), channel_id=1, source_target_pairs={{0,8},{8,0},{16,24},{24,16},{1,9},{9,1},{17,25},{25,17},{2,10},{10... | collective-permute-start | bytes 4718600 | tf_op jit(solution)/shard_map/cond/branch_1_fun/ppermute | solution.py:658
  464.8 36.3 %collective-permute-start.47 = (bf16[256,1024]{1,0:T(8,128)(2,1)}, bf16[256,1024]{1,0:T(8,128)(2,1)}, u32[]{:S(2)}, u32[]{:S(2)}) collective-permute-start(bf16[256,1024]{1,0:T(8,128)(2,1)} %get-tuple-element.1984), channel_id=1, source_target_pairs={{0,16},{8,24},{16,0},{24,8},{1,17},{9,25},{17,1},{25,9},{2,18},{10... | collective-permute-start | bytes 1572872 | tf_op jit(solution)/shard_map/cond/branch_1_fun/ppermute | solution.py:658
  466.2 35.1 %collective-permute-start.46 = (bf16[256,1024]{1,0:T(8,128)(2,1)}, bf16[256,1024]{1,0:T(8,128)(2,1)}, u32[]{:S(2)}, u32[]{:S(2)}) collective-permute-start(bf16[256,1024]{1,0:T(8,128)(2,1)} %get-tuple-element.1985), channel_id=1, source_target_pairs={{0,8},{8,0},{16,24},{24,16},{1,9},{9,1},{17,25},{25,17},{2,10},{10... | collective-permute-start | bytes 1572872 | tf_op jit(solution)/shard_map/cond/branch_1_fun/ppermute | solution.py:658
  505.5 35.7 %all-to-all-start.1 = ((bf16[32,16,768]{2,1,0:T(8,128)(2,1)}), bf16[32,16,768]{2,1,0:T(8,128)(2,1)}, u32[]{:S(2)}, u32[]{:S(2)}) async-start(bf16[32,16,768]{2,1,0:T(8,128)(2,1)} %get-tuple-element.1046), calls=%async_computation.1 | async-start | bytes 1572864 | tf_op jit(solution)/shard_map/cond/branch_1_fun/all_to_all | solution.py:1348
  510.3 35.7 %collective-permute-start.14 = (bf16[512,1024]{1,0:T(8,128)(2,1)}, bf16[512,1024]{1,0:T(8,128)(2,1)}, u32[]{:S(2)}, u32[]{:S(2)}) collective-permute-start(bf16[512,1024]{1,0:T(8,128)(2,1)} %get-tuple-element.1040), channel_id=1, source_target_pairs={{0,8},{8,0},{16,24},{24,16},{1,9},{9,1},{17,25},{25,17},{2,10},{10... | collective-permute-start | bytes 3145736 | tf_op jit(solution)/shard_map/cond/branch_1_fun/ppermute | solution.py:658
  512.1 33.9 %collective-permute-start.15 = (bf16[512,1024]{1,0:T(8,128)(2,1)}, bf16[512,1024]{1,0:T(8,128)(2,1)}, u32[]{:S(2)}, u32[]{:S(2)}) collective-permute-start(bf16[512,1024]{1,0:T(8,128)(2,1)} %get-tuple-element.1041), channel_id=1, source_target_pairs={{0,16},{8,24},{16,0},{24,8},{1,17},{9,25},{17,1},{25,9},{2,18},{10... | collective-permute-start | bytes 3145736 | tf_op jit(solution)/shard_map/cond/branch_1_fun/ppermute | solution.py:658
  553.5 34.8 %all-to-all-start.6 = ((bf16[8,64,1024]{2,1,0:T(8,128)(2,1)}), bf16[8,64,1024]{2,1,0:T(8,128)(2,1)}, u32[]{:S(2)}, u32[]{:S(2)}) async-start(bf16[8,64,1024]{2,1,0:T(8,128)(2,1)} %get-tuple-element.1453), calls=%async_computation.7 | async-start | bytes 2097152 | tf_op jit(solution)/shard_map/all_to_all | solution.py:1406
  (99 other events, 1208.9 us)
Sparse Core Ops, SparseCore 0:
  136.9 81.6 all-gather.2
  429.8 95.7 reduce-scatter.1

commit v5 on v4

--- a/solution.py
+++ b/solution.py
@@ -20,7 +20,7 @@
 GROUP = ("core", "rep")
 RING = ("chip", "core")
 ROWS = 16
-MIX_ROWS = 32
+MIX_ROWS = 64
 CHUNK = 512
 VMEM_BYTES = 56 * 1024 * 1024
 EXACT = lax.Precision.HIGHEST
@@ -1214,17 +1214,21 @@
             *hidden_back_side(first_parts, second_parts, inner.hold(grad_other), slopes[1])
         )
 
-        def sums_of_cores(_):
+        lows = (low_own, low_other)
+
+        def sums_of_cores(inner):
             came = swap_core(back)
+            grads = outer(inner, (inner.hold(resid_sides[0]), resid_sides[1]), lows)
+            came = inner.wait(came)
             at = lambda values, k: values[k * length : (k + 1) * length]
-            return [merge(at(back_own, k), at(came, k)) for k in range(rep)]
-
-        merged = inner.scope(sums_of_cores)
+            return grads, [merge(at(back_own, k), at(came, k)) for k in range(rep)]
+
+        first_grads, merged = inner.scope(sums_of_cores)
         halves = inner.wait(*halves) if square else [far_term]
-        lows = (low_own, low_other)
-        return (grad_own, grad_other), lows, sum_own + sum_other, merged, halves, came[0], came[2]
-
-    grad_sides, grad_hidden, grad_first_bias, grad_resid, halves, far_came, own_came = order.scope(
+        sides = (grad_own, grad_other)
+        return sides, first_grads, sum_own + sum_other, merged, halves, came[0], came[2]
+
+    grad_sides, first_grads, grad_first_bias, grad_resid, halves, far_came, own_came = order.scope(
         feed_forward_back
     )
 
@@ -1297,15 +1301,19 @@
     second_total = order.scope(second_sum)
     second_came = lax.all_to_all(order.hold(second_total), GROUP, 0, 0, tiled=True)
 
-    def send_terms(inner):
+    def near_terms_of(inner):
+        first_halves = send_far(inner.hold(first_grads[far]), 0)
         middle = range(1, far)
         swaps = [swap_core(inner.hold(returned[m][3])) for m in middle]
         swaps = list(inner.wait(*swaps)) if len(swaps) > 1 else [inner.wait(*swaps)]
         owns = [results[2] for results in returned]
         near_terms = near_sums(inner, owns, [None, *swaps, far_came], halves)
+        return near_terms, inner.wait(*first_halves) if square else ()
+
+    def send_terms(inner):
+        near_terms, first_halves = inner.scope(near_terms_of)
+        near_terms = inner.hold(*near_terms)
         qkv_back = [hop_chip(near_terms[m - 1], m) for m in around]
-        first_grads = outer(inner, (inner.hold(resid_sides[0]), resid_sides[1]), grad_hidden)
-        first_halves = send_far(inner.hold(first_grads[far]), 0)
 
         def pack_sums(_):
             qkv_bias_all = lax.dynamic_update_index_in_dim(
@@ -1332,20 +1340,17 @@
         sums = inner.scope(pack_sums)
         held = first_grads[1:]
         if square:
-            first_halves = inner.wait(*first_halves)
+            held = inner.wait(*take_along(first_grads[1:far], first_halves, 0))
         qkv_back = inner.wait(*qkv_back)
-        if square:
-            held = inner.wait(*take_along(first_grads[1:far], first_halves, 0))
-        return first_grads[0], held, qkv_back, sums
-
-    first_own_grad, first_terms, qkv_back, sums = order.scope(send_terms)
+        return held, qkv_back, sums
+
+    first_terms, qkv_back, sums = order.scope(send_terms)
     second_came = order.wait(second_came)
     widths = [rows, 3 * cols * fsdp // devices, rows, rows * hid]
 
     qkv_rest = [own_came, *qkv_back]
 
     def close_layer(inner):
-        every = lax.all_to_all(inner.hold(sums), AXES, 0, 0, tiled=True)
         held = inner.hold(*first_terms)
         first_hops = [hop_chip(held[m - 1], m) for m in around]
         close_from = inner.hold(history, cotangent)
@@ -1391,18 +1396,22 @@
             *grad_resid,
         )
         grad_history, grad_mix_in, grad_affine = inner.wait(grad_history, grad_mix_in, grad_affine)
-        every = inner.wait(every)
         first_bias_all = lax.dynamic_update_index_in_dim(
             jnp.zeros((group, hid_cols), SINGLE), grad_first_bias[0], core * rep + line, 0
         )
         late = [by_owner(grad_affine), first_bias_all.reshape(devices, -1)]
-        late = inner.wait(jnp.concatenate(late, 1))
+        late = jnp.concatenate(late, 1).astype(NARROW)
+        lanes = sums.shape[2]
+        late = jnp.pad(late, ((0, 0), (0, -late.shape[1] % lanes))).reshape(devices, -1, lanes)
+        late = inner.wait(jnp.concatenate([sums, late], 1))
         late = lax.all_to_all(late, AXES, 0, 0, tiled=True)
 
-        first_total = total_hidden(inner, first_own_grad, first_hops)
-        return grad_history, grad_mix_in, first_total, inner.wait(late), every
-
-    grad_history, grad_mix_in, first_total, every, sums = order.scope(close_layer)
+        first_total = total_hidden(inner, first_grads[0], first_hops)
+        return grad_history, grad_mix_in, first_total, inner.wait(late)
+
+    grad_history, grad_mix_in, first_total, everything = order.scope(close_layer)
+    everything = everything.astype(SINGLE)
+    sums, every = everything[:, :ROWS], everything[:, ROWS:].reshape(devices, -1)
     first_came = lax.all_to_all(order.hold(first_total), GROUP, 0, 0, tiled=True)
     grad_w_fc2 = order.wait(whole_rows(second_came))
     every = order.wait(jnp.sum(every, 0))
@@ -1445,7 +1454,7 @@
         grad_w_out,
         outs[2],
         grad_w_fc1,
-        every[4 * rows :],
+        every[4 * rows : 4 * rows + hidden // devices],
         grad_w_fc2,
         outs[2],
         outs[3].reshape(rows, hid),

time: 611 us -> 633 us (1.036)
  waiting for transfers between devices: 167 us -> 186 us
  loops' own time: 2.59 us -> 15 us
    ppermute x34, waiting for transfers between devices: 113 us -> 148 us  [hop_chip(): return lax.ppermute(values, 'chip', [(i, i ^ m) for i in range(chips)])]
    another operation x19 -> x20, loops' own time: 2.59 us -> 15 us  [scope(): results = lax.cond(self.hold(self.legal), inside, never)]
    all_to_all x1 -> x0, waiting for transfers between devices: 6.96 us -> none  [close_layer(): every = lax.all_to_all(inner.hold(sums), AXES, 0, 0, tiled=True)]
    ppermute x19, waiting for transfers between devices: 33.8 us -> 26.9 us  [swap_core(): return lax.ppermute(values, 'core', [(0, 1), (1, 0)])]
  transfers between devices with their start and end apart: 74 -> 73, of which waited for: 38 -> 38; matrix products, arithmetic and copies ran while one was open for 17% -> 17% of each run, Pallas kernels for 32% -> 31%
where the time goes in v5:
time: 633 us; the launch traced here: 628 us
  Pallas kernels  205 us (32%)
  waiting for transfers between devices  186 us (29%)
  starting transfers between devices  86.1 us (14%)
  local copies, waits for them, and re-layouts  76.5 us (12%)
  other arithmetic  44.3 us (7%)
  loops' own time  15 us (2%)
  between operations  14.7 us (2%)
    ppermute x34, waiting for transfers between devices, hop_chip(): return lax.ppermute(values, 'chip', [(i, i ^ m) for i in range(chips)])  148 us
    ppermute x34, starting transfers between devices, hop_chip(): return lax.ppermute(values, 'chip', [(i, i ^ m) for i in range(chips)])  35 us
    pallas_call x4, Pallas kernels, attend_back(): pl.pallas_call(attend_back_kernel, out_shape=[shape((3, 2 * length, cols)...  29.6 us
    ppermute x19, waiting for transfers between devices, swap_core(): return lax.ppermute(values, 'core', [(0, 1), (1, 0)])  26.9 us
    pallas_call x4, Pallas kernels, attend(): pl.pallas_call(attend_kernel, out_shape=[shape((3, 2 * length, cols), NAR...  26.5 us
    pallas_call x2, Pallas kernels, outer(): pl.pallas_call(outer_kernel, grid=(chips,), in_specs=[spec((rep * length,...  19.1 us
    pallas_call x2, Pallas kernels, hidden_back_side(): pl.pallas_call(functools.partial(hidden_back_kernel, chips, bool(came)),...  18.9 us
    pallas_call x1, Pallas kernels, close_layer(): pl.pallas_call(functools.partial(close_kernel, chips, len(qkv_rest), rep)...  18.5 us
  transfers between devices with their start and end apart: 73, of which 38 were waited for; matrix products, arithmetic and copies ran while one was open for 17% of the time, Pallas kernels for 31%

profile of v5, /device:TPU:0, one launch (start us, length us, event | category | flops | bytes accessed | tf_op | source)
XLA Modules:
  0.0 628.3 jit_solution(2168753201627746668)
XLA Ops:
  28.3 51.8 %conditional.20 = (bf16[3,128,2048]{2,1,0:T(8,128)(2,1)}, bf16[128,2048]{1,0:T(8,128)(2,1)S(1)}, f32[128,2048]{1,0:T(8,128)}, f32[4,2048]{1,0:T(4,128)}, f32[128...) conditional(s32[]{:T(128)} %convert_element_type.335, ...), branch_computations={%region_0.0_spmd, %region_1.8_spmd} | conditional | flops 1062702 | bytes 25345874 | solution.py:604
  28.3 15.1 %conditional = (bf16[3,128,2048]{2,1,0:T(8,128)(2,1)}, bf16[128,2048]{1,0:T(8,128)(2,1)}, f32[128,2048]{1,0:T(8,128)}, f32[4,2048]{1,0:T(4,128)}, f32[128,128]{1...) conditional(s32[]{:T(128)} %convert_element_type.240, () %tuple.93, ...), branch_computations={%region_2.0_spmd, %region_3.3_spmd} | conditional | flops 165536 | bytes 4030550 | solution.py:604
  33.7 9.0 %streams.1 = (bf16[3,128,2048]{2,1,0:T(8,128)(2,1)}, bf16[128,2048]{1,0:T(8,128)(2,1)}, f32[128,2048]{1,0:T(8,128)}) custom-call(s32[1]{0:T(128)} %get-tuple-element.539.chip, bf16[9,128,2048]{2,1,0:T(8,128)(2,1)} %get-tuple-element.540.hist, f32[128,128]{1,0:T(8,128)} %pad.18.mix, f32[4,2048]{1,0:T(4,128)} %maximum_convert_fusion.affine), custom_call_target="tpu_custom_call" | custom-call | flops 100000 | bytes 10000 | tf_op jit(solution)/shard_map/cond/branch_1_fun/cond/branch_1_fun/streams/pallas_call | solution.py:786
  45.7 7.7 %history_dots.1 = f32[128,128]{1,0:T(8,128)S(1)} custom-call(bf16[9,128,2048]{2,1,0:T(8,128)(2,1)} %get-tuple-element.562.hist, bf16[4,128,2048]{2,1,0:T(8,128)(2,1)} %get-tuple-element.570.cot, f32[128,128]{1,0:T(8,128)S(1)} %broadcast_in_dim.54.weight), custom_call_target="tpu_custom_call" | custom-call | flops 100000 | bytes 10000 | tf_op jit(solution)/shard_map/cond/branch_1_fun/history_dots/pallas_call | solution.py:815
  60.6 18.5 %collective-permute-done.30 = bf16[3,128,2048]{2,1,0:T(8,128)(2,1)} collective-permute-done((bf16[3,128,2048]{2,1,0:T(8,128)(2,1)}, bf16[3,128,2048]{2,1,0:T(8,128)(2,1)}, u32[]{:S(2)}, u32[]{:S(2)}) %collective-permute-start.30) | collective-permute-done | bytes 1572896 | tf_op jit(solution)/shard_map/cond/branch_1_fun/ppermute | solution.py:658
  85.1 51.6 %conditional.21 = (bf16[8,2,64,1024]{3,2,1,0:T(8,128)(2,1)}, bf16[8,2,64,1024]{3,2,1,0:T(8,128)(2,1)}, bf16[2048,128]{1,0:T(8,128)(2,1)}, f32[1,2048]{1,0:T(1,12...) conditional(s32[]{:T(128)} %convert_element_type.336, ...), branch_computations={%region_8.9_spmd, %region_9.12_spmd} | conditional | flops 626144 | bytes 21155228 | solution.py:604
  87.5 12.3 %conditional.2 = (bf16[32,64,128]{2,1,0:T(8,128)(2,1)}, f32[1,2048]{1,0:T(1,128)}, f32[1,768]{1,0:T(1,128)}, f32[1,1024]{1,0:T(1,128)}, f32[1,2048]{1,0:T(1,128)...) conditional(s32[]{:T(128)} %convert_element_type.260, ...), branch_computations={%region_10.10_spmd, %region_11.11_spmd} | conditional | flops 626143 | bytes 2804863 | solution.py:604
  104.1 29.3 %collective-permute-done.6 = bf16[8,2,64,1024]{3,2,1,0:T(8,128)(2,1)} collective-permute-done((bf16[8,2,64,1024]{3,2,1,0:T(8,128)(2,1)S(1)}, bf16[8,2,64,1024]{3,2,1,0:T(8,128)(2,1)}, u32[]{:S(2)}, u32[]{:S(2)}) %collective-permute-start.6) | collective-permute-done | bytes 2097184 | tf_op jit(solution)/shard_map/cond/branch_1_fun/ppermute | solution.py:658
  136.8 76.1 %conditional.22 = (bf16[8,1,64,1024]{3,2,1,0:T(8,128)(2,1)}, bf16[8,1,64,1024]{3,2,1,0:T(8,128)(2,1)S(1)}, bf16[512,2048]{1,0:T(8,128)(2,1)}, bf16[512,2048]{1,0...) conditional(s32[]{:T(128)} %convert_element_type.337, ...), branch_computations={%region_12.13_spmd, %region_13.18_spmd} | conditional | flops 14881390 | bytes 88121168 | solution.py:604
  148.0 8.3 %conditional.3 = (bf16[3,128,2048]{2,1,0:T(8,128)(2,1)}, bf16[3,128,2048]{2,1,0:T(8,128)(2,1)}, bf16[3,128,2048]{2,1,0:T(8,128)(2,1)}) conditional(s32[]{:T(128)} %convert_element_type.261, () %tuple.125, (bf16[3,128,2048]{2,1,0:T(8,128)(2,1)}, bf16[3,128,2048]{2,1,0:T(8,128)(2,1)}, bf16[3,128,2048]{2,1,0:T(8,128)(2,1)}) %tuple.126), branch_computations={%region_14.14_spmd, %region_15.15_spmd} | conditional | bytes 18874512 | solution.py:604
  156.2 12.9 %collective-permute-done.7.refs_3_ = bf16[8,1,64,1024]{3,2,1,0:T(8,128)(2,1)} collective-permute-done((bf16[8,1,64,1024]{3,2,1,0:T(8,128)(2,1)}, bf16[8,1,64,1024]{3,2,1,0:T(8,128)(2,1)}, u32[]{:S(2)}, u32[]{:S(2)}) %collective-permute-start.7) | collective-permute-done | bytes 1048608 | tf_op jit(solution)/shard_map/cond/branch_1_fun/ppermute | solution.py:658
  185.2 20.8 %conditional.4 = (bf16[512,1024]{1,0:T(8,128)(2,1)}, f32[512,1024]{1,0:T(8,128)}, bf16[128,2048]{1,0:T(8,128)(2,1)}, bf16[128,2048]{1,0:T(8,128)(2,1)}, bf16[128...) conditional(s32[]{:T(128)} %convert_element_type.262, () %tuple.131, (bf16[512,1024]{1,0:T(8,128)(2,1)}, ...), branch_computations={%region_16.16_spmd, %region_17.17_spmd} | conditional | flops 6442449 | bytes 16807332 | solution.py:604
  224.2 62.3 %conditional.23 = (bf16[2048,1024]{1,0:T(8,128)(2,1)}, bf16[3,256,256]{2,1,0:T(8,128)(2,1)S(1)}, bf16[3,256,256]{2,1,0:T(8,128)(2,1)}, bf16[3,256,256]{2,1,0:T(8...) conditional(s32[]{:T(128)} %convert_element_type.338, ...), branch_computations={%region_18.19_spmd, %region_19.20_spmd} | conditional | flops 10324276 | bytes 51937008 | solution.py:604
  298.1 44.7 %conditional.24 = (bf16[3,256,256]{2,1,0:T(8,128)(2,1)}, f32[1,768]{1,0:T(1,128)}, bf16[3,128,2048]{2,1,0:T(8,128)(2,1)}, bf16[3,128,2048]{2,1,0:T(8,128)(2,1)},...) conditional(s32[]{:T(128)} %convert_element_type.339, ...), branch_computations={%region_20.21_spmd, %region_21.22_spmd} | conditional | flops 63441720 | bytes 45827804 | solution.py:604
  302.4 7.5 %attend_back.4 = (bf16[3,256,256]{2,1,0:T(8,128)(2,1)}, f32[1,768]{1,0:T(1,128)}, bf16[3,128,2048]{2,1,0:T(8,128)(2,1)}, bf16[3,128,2048]{2,1,0:T(8,128)(2,1)}) custom-call(bf16[128,2048]{1,0:T(8,128)(2,1)} %get-tuple-element.779.own, bf16[128,2048]{1,0:T(8,128)(2,1)} %collective-permute-done.50.other, bf16[2048,1024]{1,0:T(8,128)(2,1)} %get-tuple-element.766.weight, ...), custom_call_target="tpu_custom_call" | custom-call | flops 1073741 | bytes 8000 | tf_op jit(solution)/shard_map/cond/branch_1_fun/attend_back/pallas_call | solution.py:1116
  342.9 46.4 %conditional.25 = (bf16[512,2048]{1,0:T(8,128)(2,1)}, bf16[512,2048]{1,0:T(8,128)(2,1)}, bf16[512,1024]{1,0:T(8,128)(2,1)}, bf16[512,1024]{1,0:T(8,128)(2,1)}, b...) conditional(s32[]{:T(128)} %convert_element_type.340, ...), branch_computations={%region_22.23_spmd, %region_23.26_spmd} | conditional | flops 20226958 | bytes 64043900 | solution.py:604
  346.8 9.4 %hidden_back.2 = (bf16[512,1024]{1,0:T(8,128)(2,1)}, f32[1,1024]{1,0:T(1,128)}, bf16[512,2048]{1,0:T(8,128)(2,1)}) custom-call(bf16[512,2048]{1,0:T(8,128)(2,1)} %bitcast.45.grad, f32[512,1024]{1,0:T(8,128)} %get-tuple-element.830.slope, bf16[8,2,64,1024]{3,2,1,0:T(8,128)(2,1)S(1)} %get-tuple-element.831.refs_0_.refs_4_, ...), custom_call_target="tpu_custom_call" | custom-call | flops 4294967 | bytes 20000 | tf_op jit(solution)/shard_map/cond/branch_1_fun/hidden_back/pallas_call | solution.py:1171
  367.1 9.4 %hidden_back.3 = (bf16[512,1024]{1,0:T(8,128)(2,1)}, f32[1,1024]{1,0:T(1,128)}, bf16[512,2048]{1,0:T(8,128)(2,1)}) custom-call(bf16[512,2048]{1,0:T(8,128)(2,1)} %bitcast.46.grad, f32[512,1024]{1,0:T(8,128)} %get-tuple-element.846.slope, bf16[8,2,64,1024]{3,2,1,0:T(8,128)(2,1)S(1)} %get-tuple-element.831.refs_0_.refs_4_, ...), custom_call_target="tpu_custom_call" | custom-call | flops 4294967 | bytes 20000 | tf_op jit(solution)/shard_map/cond/branch_1_fun/hidden_back/pallas_call | solution.py:1171
  377.3 11.6 %conditional.5 = (bf16[512,1024]{1,0:T(8,128)(2,1)}, bf16[512,1024]{1,0:T(8,128)(2,1)}, bf16[512,1024]{1,0:T(8,128)(2,1)}, bf16[512,1024]{1,0:T(8,128)(2,1)}, bf...) conditional(s32[]{:T(128)} %convert_element_type.289, ...), branch_computations={%region_24.24_spmd, %region_25.25_spmd} | conditional | flops 8489271 | bytes 23088804 | solution.py:604
  377.3 9.6 %outer.2 = (bf16[512,1024]{1,0:T(8,128)(2,1)}, bf16[512,1024]{1,0:T(8,128)(2,1)}, bf16[512,1024]{1,0:T(8,128)(2,1)}, bf16[512,1024]{1,0:T(8,128)(2,1)}) custom-call(bf16[512,2048]{1,0:T(8,128)(2,1)} %get-tuple-element.812.left_own, bf16[512,2048]{1,0:T(8,128)(2,1)} %get-tuple-element.813.left_other, bf16[512,1024]{1,0:T(8,128)(2,1)} %get-tuple-element.814.right_own, ...), custom_call_target="tpu_custom_call" | custom-call | flops 4294967 | bytes 20000 | tf_op jit(solution)/shard_map/cond/branch_1_fun/cond/branch_1_fun/outer/pallas_call | solution.py:1190
  389.9 54.7 %conditional.26 = (bf16[128,2048]{1,0:T(8,128)(2,1)}, bf16[128,2048]{1,0:T(8,128)(2,1)}, bf16[128,2048]{1,0:T(8,128)(2,1)}, bf16[4,8,64,1024]{3,2,1,0:T(8,128)(2...) conditional(s32[]{:T(128)} %convert_element_type.341, ...), branch_computations={%region_26.27_spmd, %region_27.30_spmd} | conditional | flops 17028872 | bytes 44631444 | solution.py:604
  394.3 50.3 %conditional.6 = (bf16[4,8,64,1024]{3,2,1,0:T(8,128)(2,1)}, f32[1,768]{1,0:T(1,128)}, bf16[3,128,2048]{2,1,0:T(8,128)(2,1)}, bf16[3,128,2048]{2,1,0:T(8,128)(2,1...) conditional(s32[]{:T(128)} %convert_element_type.296, ...), branch_computations={%region_28.28_spmd, %region_29.29_spmd} | conditional | flops 17028872 | bytes 38339488 | solution.py:604
  394.3 9.5 %outer.3 = (bf16[512,1024]{1,0:T(8,128)(2,1)}, bf16[512,1024]{1,0:T(8,128)(2,1)}, bf16[512,1024]{1,0:T(8,128)(2,1)}, bf16[512,1024]{1,0:T(8,128)(2,1)}) custom-call(bf16[512,2048]{1,0:T(8,128)(2,1)} %get-tuple-element.886.left_own, bf16[512,2048]{1,0:T(8,128)(2,1)} %get-tuple-element.887.left_other, bf16[512,1024]{1,0:T(8,128)(2,1)} %get-tuple-element.888.right_own, ...), custom_call_target="tpu_custom_call" | custom-call | flops 4294967 | bytes 20000 | tf_op jit(solution)/shard_map/cond/branch_1_fun/cond/branch_1_fun/outer/pallas_call | solution.py:1190
  429.1 12.7 %heads_grad.1 = bf16[4,8,64,1024]{3,2,1,0:T(8,128)(2,1)} custom-call(bf16[3,128,2048]{2,1,0:T(8,128)(2,1)} %get-tuple-element.869.refs_0_, bf16[3,128,2048]{2,1,0:T(8,128)(2,1)} %get-tuple-element.870.refs_1_, bf16[3,128,2048]{2,1,0:T(8,128)(2,1)} %get-tuple-element.871.refs_2_, bf16[3,128,2048]{2,1,0:T(8,128)(2,1)} %get-tuple-element.872.refs_3_, ...), custom_call_target="tpu_custom_call" | custom-call | flops 4294967 | bytes 30000 | tf_op jit(solution)/shard_map/cond/branch_1_fun/cond/branch_1_fun/heads_grad/pallas_call | solution.py:1261
  451.9 56.3 %conditional.28 = (bf16[512,1024]{1,0:T(8,128)(2,1)}, bf16[512,1024]{1,0:T(8,128)(2,1)}, bf16[3,128,2048]{2,1,0:T(8,128)(2,1)}, bf16[3,128,2048]{2,1,0:T(8,128)(2,1)}, bf16[32,16,768]{2,1,0:T(8,128)(2,1)}) conditional(s32[]{:T(128)} %convert_element_type.343, () %tuple.333, (bf16[512,1024]{1,0:T(8,128)(2,1)}, pred[]{:T(512)}, ...), branch_computations={%region_32.33_spmd, %region_33.38_spmd} | conditional | flops 6300631 | bytes 67179248 | solution.py:604
  452.0 19.9 %conditional.7 = (bf16[3,128,2048]{2,1,0:T(8,128)(2,1)}, bf16[3,128,2048]{2,1,0:T(8,128)(2,1)}, bf16[256,1024]{1,0:T(8,128)(2,1)}, f32[256,1024]{1,0:T(8,128)}, f32[256,1024]{1,0:T(8,128)}) conditional(s32[]{:T(128)} %convert_element_type.304, () %tuple.214, (bf16[3,128,2048]{2,1,0:T(8,128)(2,1)}, bf16[3,128,2048]{2,1,0:T(8,128)(2,1)}, ...), branch_computations={%region_34.34_spmd, %region_35.35_spmd} | conditional | flops 526288 | bytes 34623264 | solution.py:604
  477.7 12.9 %conditional.8 = (bf16[32,16,768]{2,1,0:T(8,128)(2,1)}) conditional(s32[]{:T(128)} %convert_element_type.309, () %tuple.217, (f32[1,2048]{1,0:T(1,128)S(1)}, f32[1,768]{1,0:T(1,128)}, f32[1,768]{1,0:T(1,128)}, f32[1,768]{1,0:T(1,128)}, f32[1,768]{1,0:T(1,128)}, /*index=5*/s32[]{:T(128)}, s32[]{:T(128)}, f32[1,2048]{1,0:T(1,128)S(1)}, ...), branch_computations={%region_36.36_spmd, %region_37.37_spmd} | conditional | flops 7173 | bytes 5292674 | solution.py:604
  495.1 12.7 %collective-permute-done.24 = bf16[3,128,2048]{2,1,0:T(8,128)(2,1)} collective-permute-done((bf16[3,128,2048]{2,1,0:T(8,128)(2,1)}, bf16[3,128,2048]{2,1,0:T(8,128)(2,1)}, u32[]{:S(2)}, u32[]{:S(2)}) %collective-permute-start.24) | collective-permute-done | bytes 1572896 | tf_op jit(solution)/shard_map/cond/branch_1_fun/ppermute | solution.py:658
  508.1 68.1 %conditional.29 = (f32[9,128,2048]{2,1,0:T(8,128)}, f32[128,36]{1,0:T(8,128)}, bf16[8,64,1024]{2,1,0:T(8,128)(2,1)}, bf16[32,17,768]{2,1,0:T(8,128)(2,1)}, f32[128,36]{0,1:T(8,128)S(1)}) conditional(s32[]{:T(128)} %convert_element_type.344, () %tuple.337, (bf16[9,128,2048]{2,1,0:T(8,128)(2,1)}, bf16[4,128,2048]{2,1,0:T(8,128)(2,1)S(1)}, ...), branch_computations={%region_38.39_spmd, %region_39.40_spmd} | conditional | flops 5197125 | bytes 17968944 | solution.py:604
  508.1 18.5 %close.1 = (f32[9,128,2048]{2,1,0:T(8,128)}, f32[128,36]{1,0:T(8,128)S(1)}, f32[4,2048]{1,0:T(4,128)}) custom-call(s32[1]{0:T(128)} %get-tuple-element.1057.chip, bf16[9,128,2048]{2,1,0:T(8,128)(2,1)} %get-tuple-element.1060.hist, bf16[4,128,2048]{2,1,0:T(8,128)(2,1)S(1)} %get-tuple-element.1061.cot, f32[128,128]{1,0:T(8,128)} %get-tuple-element.1062.coef, ...), custom_call_target="tpu_custom_call" | custom-call | flops 200000 | bytes 20000 | tf_op jit(solution)/shard_map/cond/branch_1_fun/close/pallas_call | solution.py:1357
  538.9 34.6 %collective-permute-done.14 = bf16[512,1024]{1,0:T(8,128)(2,1)S(1)} collective-permute-done((bf16[512,1024]{1,0:T(8,128)(2,1)}, bf16[512,1024]{1,0:T(8,128)(2,1)S(1)}, u32[]{:S(2)}, u32[]{:S(2)}) %collective-permute-start.14) | collective-permute-done | bytes 1048608 | tf_op jit(solution)/shard_map/cond/branch_1_fun/ppermute | solution.py:658
  592.2 24.2 %conditional.30 = (f32[64,6144]{1,0:T(8,128)S(1)}, f32[64,2048]{1,0:T(8,128)S(1)}) conditional(s32[]{:T(128)} %convert_element_type.349, () %tuple.344, (s32[]{:T(128)}, bf16[8,64,1024]{2,1,0:T(8,128)(2,1)}, s32[]{:T(128)}) %tuple.476), branch_computations={%region_43.44_spmd, %region_44.45_spmd} | conditional | flops 6291482 | bytes 30409264 | solution.py:604
  (449 shorter events, 407.8 us)
Async XLA Ops:
  24.5 55.6 %all-to-all-start.3 = ((bf16[8,2,64,1024]{3,2,1,0:T(8,128)(2,1)}), bf16[8,2,64,1024]{3,2,1,0:T(8,128)(2,1)S(1)}, u32[]{:S(2)}, u32[]{:S(2)}) async-start(bf16[8,2,64,1024]{3,2,1,0:T(8,128)(2,1)} %pack_hidden.1), calls=%async_computation.3 | async-start | bytes 4194304 | tf_op jit(solution)/shard_map/all_to_all | solution.py:749
  28.1 190.4 %all-gather.3.cloned.1.call-start = ((), (), s32[]{:S(2)}) async-start(), calls=%async_computation.8 | async-start | bytes 5242880 | tf_op jit(solution)/shard_map/all_gather | solution.py:887
  43.4 35.7 %collective-permute-start.30 = (bf16[3,128,2048]{2,1,0:T(8,128)(2,1)}, bf16[3,128,2048]{2,1,0:T(8,128)(2,1)}, u32[]{:S(2)}, u32[]{:S(2)}) collective-permute-start(bf16[3,128,2048]{2,1,0:T(8,128)(2,1)} %get-tuple-element.579), channel_id=1, source_target_pairs={{0,16},{8,24},{16,0},{24,8},{1,17},{9,25},{17,1},{25,9},{2,18},{10... | collective-permute-start | bytes 4718600 | tf_op jit(solution)/shard_map/cond/branch_1_fun/ppermute | solution.py:658
  44.9 35.2 %collective-permute-start.29 = (bf16[3,128,2048]{2,1,0:T(8,128)(2,1)}, bf16[3,128,2048]{2,1,0:T(8,128)(2,1)}, u32[]{:S(2)}, u32[]{:S(2)}) collective-permute-start(bf16[3,128,2048]{2,1,0:T(8,128)(2,1)} %get-tuple-element.579), channel_id=1, source_target_pairs={{0,8},{8,0},{16,24},{24,16},{1,9},{9,1},{17,25},{25,17},{2,10},{10... | collective-permute-start | bytes 4718600 | tf_op jit(solution)/shard_map/cond/branch_1_fun/ppermute | solution.py:658
  80.7 56.0 %collective-permute-start.58 = (bf16[128,2048]{1,0:T(8,128)(2,1)S(1)}, bf16[128,2048]{1,0:T(8,128)(2,1)S(1)}, u32[]{:S(2)}, u32[]{:S(2)}) collective-permute-start(bf16[128,2048]{1,0:T(8,128)(2,1)S(1)} %get-tuple-element.1326), channel_id=1, source_target_pairs={{0,3},{1,2},{2,1},{3,0},{4,7},{5,6},{6,5},{7,4},{8,11},{9,10},{10,... | collective-permute-start | bytes 1572872 | tf_op jit(solution)/shard_map/ppermute | solution.py:661
  83.9 52.8 %collective-permute-start.57 = (bf16[128,2048]{1,0:T(8,128)(2,1)S(1)}, bf16[128,2048]{1,0:T(8,128)(2,1)}, u32[]{:S(2)}, u32[]{:S(2)}) collective-permute-start(bf16[128,2048]{1,0:T(8,128)(2,1)S(1)} %get-tuple-element.1326), channel_id=1, source_target_pairs={{0,2},{1,3},{2,0},{3,1},{4,6},{5,7},{6,4},{7,5},{8,10},{9,11},{10,... | collective-permute-start | bytes 1572872 | tf_op jit(solution)/shard_map/ppermute | solution.py:661
  83.9 52.8 %collective-permute-start.56 = (bf16[128,2048]{1,0:T(8,128)(2,1)S(1)}, bf16[128,2048]{1,0:T(8,128)(2,1)}, u32[]{:S(2)}, u32[]{:S(2)}) collective-permute-start(bf16[128,2048]{1,0:T(8,128)(2,1)S(1)} %get-tuple-element.1326), channel_id=1, source_target_pairs={{0,1},{1,0},{2,3},{3,2},{4,5},{5,4},{6,7},{7,6},{8,9},{9,8},{10,11... | collective-permute-start | bytes 1572872 | tf_op jit(solution)/shard_map/ppermute | solution.py:661
  85.1 48.3 %collective-permute-start.6 = (bf16[8,2,64,1024]{3,2,1,0:T(8,128)(2,1)S(1)}, bf16[8,2,64,1024]{3,2,1,0:T(8,128)(2,1)}, u32[]{:S(2)}, u32[]{:S(2)}) collective-permute-start(bf16[8,2,64,1024]{3,2,1,0:T(8,128)(2,1)S(1)} %get-tuple-element.608), channel_id=1, source_target_pairs={{0,16},{8,24},{16,0},{24,8},{1,17},{9,25},{17,1},{25,9},{2,18},{10... | collective-permute-start | bytes 6291464 | tf_op jit(solution)/shard_map/cond/branch_1_fun/ppermute | solution.py:658
  85.9 48.5 %collective-permute-start.5 = (bf16[8,2,64,1024]{3,2,1,0:T(8,128)(2,1)S(1)}, bf16[8,2,64,1024]{3,2,1,0:T(8,128)(2,1)}, u32[]{:S(2)}, u32[]{:S(2)}) collective-permute-start(bf16[8,2,64,1024]{3,2,1,0:T(8,128)(2,1)S(1)} %get-tuple-element.608), channel_id=1, source_target_pairs={{0,8},{8,0},{16,24},{24,16},{1,9},{9,1},{17,25},{25,17},{2,10},{10... | collective-permute-start | bytes 6291464 | tf_op jit(solution)/shard_map/cond/branch_1_fun/ppermute | solution.py:658
  99.8 36.9 %all-to-all-start = ((bf16[32,64,128]{2,1,0:T(8,128)(2,1)}), bf16[32,64,128]{2,1,0:T(8,128)(2,1)}, u32[]{:S(2)}, u32[]{:S(2)}) async-start(bf16[32,64,128]{2,1,0:T(8,128)(2,1)} %get-tuple-element.619), calls=%async_computation | async-start | bytes 1048576 | tf_op jit(solution)/shard_map/cond/branch_1_fun/all_to_all | solution.py:879
  136.7 455.5 %reduce-scatter.2.cloned.1.call-start = ((), (), s32[]{:S(2)}) async-start(), calls=%async_computation.7 | async-start | bytes 5242880 | tf_op jit(solution)/shard_map/reduce_scatter | solution.py:1297
  143.8 25.4 %collective-permute-start.7 = (bf16[8,1,64,1024]{3,2,1,0:T(8,128)(2,1)}, bf16[8,1,64,1024]{3,2,1,0:T(8,128)(2,1)}, u32[]{:S(2)}, u32[]{:S(2)}) collective-permute-start(bf16[8,1,64,1024]{3,2,1,0:T(8,128)(2,1)} %slice.320), channel_id=1, source_target_pairs={{0,16},{8,24},{16,0},{24,8},{1,17},{9,25},{17,1},{25,9},{2,18},{10... | collective-permute-start | bytes 3145736 | tf_op jit(solution)/shard_map/cond/branch_1_fun/ppermute | solution.py:658
  147.3 25.0 %collective-permute-start.8 = (bf16[8,1,64,1024]{3,2,1,0:T(8,128)(2,1)}, bf16[8,1,64,1024]{3,2,1,0:T(8,128)(2,1)S(1)}, u32[]{:S(2)}, u32[]{:S(2)}) collective-permute-start(bf16[8,1,64,1024]{3,2,1,0:T(8,128)(2,1)} %slice.321), channel_id=1, source_target_pairs={{0,8},{8,0},{16,24},{24,16},{1,9},{9,1},{17,25},{25,17},{2,10},{10... | collective-permute-start | bytes 3145736 | tf_op jit(solution)/shard_map/cond/branch_1_fun/ppermute | solution.py:658
  176.9 29.1 %collective-permute-start.11 = (bf16[3,64,2048]{2,1,0:T(8,128)(2,1)}, bf16[3,64,2048]{2,1,0:T(8,128)(2,1)}, u32[]{:S(2)}, u32[]{:S(2)}) collective-permute-start(bf16[3,64,2048]{2,1,0:T(8,128)(2,1)} %slice.225), channel_id=1, source_target_pairs={{0,8},{8,0},{16,24},{24,16},{1,9},{9,1},{17,25},{25,17},{2,10},{10... | collective-permute-start | bytes 2359304 | tf_op jit(solution)/shard_map/cond/branch_1_fun/ppermute | solution.py:658
  177.6 28.4 %collective-permute-start.10 = (bf16[3,64,2048]{2,1,0:T(8,128)(2,1)}, bf16[3,64,2048]{2,1,0:T(8,128)(2,1)}, u32[]{:S(2)}, u32[]{:S(2)}) collective-permute-start(bf16[3,64,2048]{2,1,0:T(8,128)(2,1)} %slice.224), channel_id=1, source_target_pairs={{0,16},{8,24},{16,0},{24,8},{1,17},{9,25},{17,1},{25,9},{2,18},{10... | collective-permute-start | bytes 2359304 | tf_op jit(solution)/shard_map/cond/branch_1_fun/ppermute | solution.py:658
  218.6 67.9 %collective-permute-start.59 = (bf16[128,2048]{1,0:T(8,128)(2,1)}, bf16[128,2048]{1,0:T(8,128)(2,1)}, u32[]{:S(2)}, u32[]{:S(2)}) collective-permute-start(bf16[128,2048]{1,0:T(8,128)(2,1)} %get-tuple-element.1365), channel_id=1, source_target_pairs={{0,1},{1,0},{2,3},{3,2},{4,5},{5,4},{6,7},{7,6},{8,9},{9,8},{10,11... | collective-permute-start | bytes 1572872 | tf_op jit(solution)/shard_map/ppermute | solution.py:661
  218.6 67.9 %collective-permute-start.60 = (bf16[128,2048]{1,0:T(8,128)(2,1)}, bf16[128,2048]{1,0:T(8,128)(2,1)}, u32[]{:S(2)}, u32[]{:S(2)}) collective-permute-start(bf16[128,2048]{1,0:T(8,128)(2,1)} %get-tuple-element.1366), channel_id=1, source_target_pairs={{0,2},{1,3},{2,0},{3,1},{4,6},{5,7},{6,4},{7,5},{8,10},{9,11},{10,... | collective-permute-start | bytes 1572872 | tf_op jit(solution)/shard_map/ppermute | solution.py:661
  219.7 66.8 %collective-permute-start.61 = (bf16[128,2048]{1,0:T(8,128)(2,1)}, bf16[128,2048]{1,0:T(8,128)(2,1)}, u32[]{:S(2)}, u32[]{:S(2)}) collective-permute-start(bf16[128,2048]{1,0:T(8,128)(2,1)} %get-tuple-element.1367), channel_id=1, source_target_pairs={{0,3},{1,2},{2,1},{3,0},{4,7},{5,6},{6,5},{7,4},{8,11},{9,10},{10,... | collective-permute-start | bytes 1572872 | tf_op jit(solution)/shard_map/ppermute | solution.py:661
  293.7 49.2 %collective-permute-start.64 = (bf16[128,2048]{1,0:T(8,128)(2,1)}, bf16[128,2048]{1,0:T(8,128)(2,1)}, u32[]{:S(2)}, u32[]{:S(2)}) collective-permute-start(bf16[128,2048]{1,0:T(8,128)(2,1)} %get-tuple-element.1402), channel_id=1, source_target_pairs={{0,3},{1,2},{2,1},{3,0},{4,7},{5,6},{6,5},{7,4},{8,11},{9,10},{10,... | collective-permute-start | bytes 1572872 | tf_op jit(solution)/shard_map/ppermute | solution.py:661
  294.5 48.4 %collective-permute-start.63 = (bf16[128,2048]{1,0:T(8,128)(2,1)}, bf16[128,2048]{1,0:T(8,128)(2,1)}, u32[]{:S(2)}, u32[]{:S(2)}) collective-permute-start(bf16[128,2048]{1,0:T(8,128)(2,1)} %get-tuple-element.1402), channel_id=1, source_target_pairs={{0,2},{1,3},{2,0},{3,1},{4,6},{5,7},{6,4},{7,5},{8,10},{9,11},{10,... | collective-permute-start | bytes 1572872 | tf_op jit(solution)/shard_map/ppermute | solution.py:661
  294.5 48.4 %collective-permute-start.62 = (bf16[128,2048]{1,0:T(8,128)(2,1)}, bf16[128,2048]{1,0:T(8,128)(2,1)}, u32[]{:S(2)}, u32[]{:S(2)}) collective-permute-start(bf16[128,2048]{1,0:T(8,128)(2,1)} %get-tuple-element.1402), channel_id=1, source_target_pairs={{0,1},{1,0},{2,3},{3,2},{4,5},{5,4},{6,7},{7,6},{8,9},{9,8},{10,11... | collective-permute-start | bytes 1572872 | tf_op jit(solution)/shard_map/ppermute | solution.py:661
  364.1 24.8 %collective-permute-start.42 = (bf16[3,64,2048]{2,1,0:T(8,128)(2,1)}, bf16[3,64,2048]{2,1,0:T(8,128)(2,1)}, u32[]{:S(2)}, u32[]{:S(2)}) collective-permute-start(bf16[3,64,2048]{2,1,0:T(8,128)(2,1)} %get-tuple-element.2000), channel_id=1, source_target_pairs={{0,16},{8,24},{16,0},{24,8},{1,17},{9,25},{17,1},{25,9},{2,18},{10... | collective-permute-start | bytes 2359304 | tf_op jit(solution)/shard_map/cond/branch_1_fun/ppermute | solution.py:658
  389.9 54.7 %collective-permute-start.47 = (bf16[128,2048]{1,0:T(8,128)(2,1)}, bf16[128,2048]{1,0:T(8,128)(2,1)}, u32[]{:S(2)}, u32[]{:S(2)}) collective-permute-start(bf16[128,2048]{1,0:T(8,128)(2,1)} %get-tuple-element.942), channel_id=1, source_target_pairs={{0,1},{1,0},{2,3},{3,2},{4,5},{5,4},{6,7},{7,6},{8,9},{9,8},{10,11... | collective-permute-start | bytes 1572872 | tf_op jit(solution)/shard_map/cond/branch_1_fun/ppermute | solution.py:661
  389.9 54.7 %collective-permute-start.48 = (bf16[128,2048]{1,0:T(8,128)(2,1)}, bf16[128,2048]{1,0:T(8,128)(2,1)}, u32[]{:S(2)}, u32[]{:S(2)}) collective-permute-start(bf16[128,2048]{1,0:T(8,128)(2,1)} %get-tuple-element.943), channel_id=1, source_target_pairs={{0,2},{1,3},{2,0},{3,1},{4,6},{5,7},{6,4},{7,5},{8,10},{9,11},{10,... | collective-permute-start | bytes 1572872 | tf_op jit(solution)/shard_map/cond/branch_1_fun/ppermute | solution.py:661
  391.2 53.3 %collective-permute-start.49 = (bf16[128,2048]{1,0:T(8,128)(2,1)}, bf16[128,2048]{1,0:T(8,128)(2,1)}, u32[]{:S(2)}, u32[]{:S(2)}) collective-permute-start(bf16[128,2048]{1,0:T(8,128)(2,1)} %get-tuple-element.944), channel_id=1, source_target_pairs={{0,3},{1,2},{2,1},{3,0},{4,7},{5,6},{6,5},{7,4},{8,11},{9,10},{10,... | collective-permute-start | bytes 1572872 | tf_op jit(solution)/shard_map/cond/branch_1_fun/ppermute | solution.py:661
  448.1 60.0 %all-to-all-start.4 = ((bf16[8,64,1024]{2,1,0:T(8,128)(2,1)}), bf16[8,64,1024]{2,1,0:T(8,128)(2,1)S(1)}, u32[]{:S(2)}, u32[]{:S(2)}) async-start(bf16[8,64,1024]{2,1,0:T(8,128)(2,1)} %get-tuple-element.2400), calls=%async_computation.4 | async-start | bytes 2097152 | tf_op jit(solution)/shard_map/all_to_all | solution.py:1302
  471.9 36.0 %collective-permute-start.24 = (bf16[3,128,2048]{2,1,0:T(8,128)(2,1)}, bf16[3,128,2048]{2,1,0:T(8,128)(2,1)}, u32[]{:S(2)}, u32[]{:S(2)}) collective-permute-start(bf16[3,128,2048]{2,1,0:T(8,128)(2,1)} %get-tuple-element.1053), channel_id=1, source_target_pairs={{0,8},{8,0},{16,24},{24,16},{1,9},{9,1},{17,25},{25,17},{2,10},{10... | collective-permute-start | bytes 4718600 | tf_op jit(solution)/shard_map/cond/branch_1_fun/ppermute | solution.py:658
  472.5 35.7 %collective-permute-start.25 = (bf16[3,128,2048]{2,1,0:T(8,128)(2,1)}, bf16[3,128,2048]{2,1,0:T(8,128)(2,1)}, u32[]{:S(2)}, u32[]{:S(2)}) collective-permute-start(bf16[3,128,2048]{2,1,0:T(8,128)(2,1)} %get-tuple-element.1054), channel_id=1, source_target_pairs={{0,16},{8,24},{16,0},{24,8},{1,17},{9,25},{17,1},{25,9},{2,18},{10... | collective-permute-start | bytes 4718600 | tf_op jit(solution)/shard_map/cond/branch_1_fun/ppermute | solution.py:658
  530.1 46.2 %all-to-all-start.1 = ((bf16[32,17,768]{2,1,0:T(8,128)(2,1)}), bf16[32,17,768]{2,1,0:T(8,128)(2,1)}, u32[]{:S(2)}, u32[]{:S(2)}) async-start(bf16[32,17,768]{2,1,0:T(8,128)(2,1)} %pad_maximum_fusion.11), calls=%async_computation.1 | async-start | bytes 2359296 | tf_op jit(solution)/shard_map/cond/branch_1_fun/all_to_all | solution.py:1407
  535.6 37.9 %collective-permute-start.14 = (bf16[512,1024]{1,0:T(8,128)(2,1)}, bf16[512,1024]{1,0:T(8,128)(2,1)S(1)}, u32[]{:S(2)}, u32[]{:S(2)}) collective-permute-start(bf16[512,1024]{1,0:T(8,128)(2,1)} %get-tuple-element.1080), channel_id=1, source_target_pairs={{0,8},{8,0},{16,24},{24,16},{1,9},{9,1},{17,25},{25,17},{2,10},{10... | collective-permute-start | bytes 3145736 | tf_op jit(solution)/shard_map/cond/branch_1_fun/ppermute | solution.py:658
  537.4 36.1 %collective-permute-start.15 = (bf16[512,1024]{1,0:T(8,128)(2,1)}, bf16[512,1024]{1,0:T(8,128)(2,1)S(1)}, u32[]{:S(2)}, u32[]{:S(2)}) collective-permute-start(bf16[512,1024]{1,0:T(8,128)(2,1)} %get-tuple-element.1081), channel_id=1, source_target_pairs={{0,16},{8,24},{16,0},{24,8},{1,17},{9,25},{17,1},{25,9},{2,18},{10... | collective-permute-start | bytes 3145736 | tf_op jit(solution)/shard_map/cond/branch_1_fun/ppermute | solution.py:658
  576.3 40.1 %all-to-all-start.5 = ((bf16[8,64,1024]{2,1,0:T(8,128)(2,1)}), bf16[8,64,1024]{2,1,0:T(8,128)(2,1)}, u32[]{:S(2)}, u32[]{:S(2)}) async-start(bf16[8,64,1024]{2,1,0:T(8,128)(2,1)} %get-tuple-element.1492), calls=%async_computation.6 | async-start | bytes 2097152 | tf_op jit(solution)/shard_map/all_to_all | solution.py:1415
  (95 other events, 1125.2 us)
Sparse Core Ops, SparseCore 0:
  136.8 81.6 all-gather.2
  444.7 90.1 reduce-scatter.1
